TPU v7x, 128 devices: a whole 4x4x4 slice. The times are simulated.
128 devices in a mesh: region: 16 (over z, x), dom: 8 (over y, core).
Axes of the slice: x: 4, y: 4, z: 4, core: 2. Of those that a mesh axis runs over, the one named last changes fastest.
Arguments:
- slave_disp: float32 [12, 2097152], P(None, ('region', 'dom')), may hold values from -4 to 4
- slave_normal: float32 [3, 2097152], P(None, ('region', 'dom')), may hold values from -6 to 6
- gap_zero: float32 [4, 2097152], P(None, ('region', 'dom')), may hold values from -6 to 6
- quad_weight: float32 [4, 2097152], P(None, ('region', 'dom')), may hold values from 0.1 to 1
- proj_coord: float32 [8, 2097152], P(None, ('region', 'dom')), may hold values from -1 to 1
- multiplier: float32 [4, 2097152], P(None, ('region', 'dom')), may hold values from 0 to 2
- active: int32 [4, 2097152], P(None, ('region', 'dom')), may hold values 0 or 1
- pair_owner: int32 [2097152, 1], P(('region', 'dom')), may hold values from 0 to 127; in each aligned block of 16384 rows (0 to 16383, 16384 to 32767, ...) at most 256 rows name the same one
- pair_slot: int32 [2097152], P(('region', 'dom')), may hold values from 0 to 4095
- master_vol: float32 [12, 524288], P(None, ('region', 'dom')), may hold values from -4 to 4
- surf_pick: int32 [128, 4096], P(('region', 'dom')), may hold values from 0 to 4095, each once within a row
Outputs:
- weighted_gap: float32 [4, 2097152], P(None, ('region', 'dom'))
- multiplier_new: float32 [4, 2097152], P(None, ('region', 'dom'))
- master_force: float32 [12, 524288], P(None, ('region', 'dom'))
Inputs may be any that keep to these rules, and one draw needn't show every extreme that they name: `pair_owner`: among the 16384 rows of one device no owner is named more than 256 times, a bound that some block reaches. `surf_pick`: each row is a permutation of 0 to 4095.
All inputs are finite; a program needn't handle non-finite values. No bound on the sum of `active` on one device may be relied on, other than what follows from the above.
Results may differ from a plain program's by a relative error of at most 0.0003.
Values sent between devices are 32-bit elements; how exact they have to be, the bound alone decides.
No kernel may reach another device: no remote copies, remote signals or barrier semaphores. Data moves between devices by JAX's collectives and lax.ppermute only.
A program may use at most 128 MiB of HBM per device.

v0:
```python
import math

import jax
import jax.numpy as jnp
from jax import lax
from jax.sharding import PartitionSpec as P

gauss_point = 1.0 / math.sqrt(3.0)
node_xs = [-1.0, 1.0, 1.0, -1.0]
node_ys = [-1.0, -1.0, 1.0, 1.0]
point_xs = [-gauss_point, gauss_point, gauss_point, -gauss_point]
point_ys = [-gauss_point, -gauss_point, gauss_point, gauss_point]
slave_table = [
    [(1.0 + node_xs[c] * point_xs[q]) * (1.0 + node_ys[c] * point_ys[q]) * 0.25 for q in range(4)]
    for c in range(4)
]


def master_shapes(proj_coord):
    result = []
    for q in range(4):
        first = proj_coord[2 * q]
        second = proj_coord[2 * q + 1]
        result.append(
            [(1.0 + node_xs[c] * first) * (1.0 + node_ys[c] * second) * 0.25 for c in range(4)]
        )
    return result


def normal_part(normal, displace):
    return [
        normal[0] * displace[3 * c]
        + normal[1] * displace[3 * c + 1]
        + normal[2] * displace[3 * c + 2]
        for c in range(4)
    ]


def mortar_from_along(proj_coord, weight, along):
    shapes = master_shapes(proj_coord)
    points = []
    for q in range(4):
        total = shapes[q][0] * along[0]
        for c in range(1, 4):
            total = total + shapes[q][c] * along[c]
        points.append(weight[q] * total)
    result = []
    for a in range(4):
        total = slave_table[a][0] * points[0]
        for q in range(1, 4):
            total = total + slave_table[a][q] * points[q]
        result.append(total)
    return jnp.stack(result)


def mortar_term(proj_coord, normal, weight, master_disp):
    return mortar_from_along(proj_coord, weight, normal_part(normal, master_disp))


def slave_term(slave_disp, normal, gap_zero, weight):
    along = normal_part(normal, slave_disp)
    points = []
    for q in range(4):
        total = gap_zero[q]
        for b in range(4):
            total = total + slave_table[b][q] * along[b]
        points.append(weight[q] * total)
    result = []
    for a in range(4):
        total = slave_table[a][0] * points[0]
        for q in range(1, 4):
            total = total + slave_table[a][q] * points[q]
        result.append(total)
    return jnp.stack(result)


def nodal_factor(proj_coord, weight, lagrange):
    shapes = master_shapes(proj_coord)
    coeff = []
    for q in range(4):
        total = slave_table[0][q] * lagrange[0]
        for a in range(1, 4):
            total = total + slave_table[a][q] * lagrange[a]
        coeff.append(weight[q] * total)
    result = []
    for c in range(4):
        total = shapes[0][c] * coeff[0]
        for q in range(1, 4):
            total = total + shapes[q][c] * coeff[q]
        result.append(total)
    return jnp.stack(result)


def spread_normal(factor, normal):
    result = []
    for c in range(4):
        for j in range(3):
            result.append(factor[c] * normal[j])
    return jnp.stack(result)


def send_out(block, region_count, dom_count, capacity):
    rows = block.shape[0]
    owners = region_count * dom_count
    moved = lax.all_to_all(block, ("region", "dom"), split_axis=1, concat_axis=1, tiled=True)
    return moved.reshape(rows, owners * capacity)


def send_back(block, region_count, dom_count, capacity):
    rows = block.shape[0]
    owners = region_count * dom_count
    moved = lax.all_to_all(block, ("region", "dom"), split_axis=1, concat_axis=1, tiled=True)
    return moved.reshape(rows, owners * capacity)


def send_terms(block, region_count, dom_count, capacity):
    rows = block.shape[0]
    owners = region_count * dom_count
    moved = lax.all_to_all(block, ("region", "dom"), split_axis=1, concat_axis=1, tiled=True)
    return moved.reshape(rows, owners * capacity)


def owner_ranks(target, owners):
    count = target.shape[0]
    stride = math.gcd(count, 512)
    blocks = count // stride
    onehot = (target[:, None] == jnp.arange(owners, dtype=jnp.int32)[None, :]).astype(jnp.bfloat16)
    grouped = onehot.reshape(blocks, stride, owners)
    lower = (jnp.arange(stride)[:, None] >= jnp.arange(stride)[None, :]).astype(jnp.bfloat16)
    within = jnp.einsum("ij,njo->nio", lower, grouped, preferred_element_type=jnp.float32)
    totals = within[:, stride - 1, :]
    offsets = jnp.cumsum(totals, axis=0) - totals
    running = within + offsets[:, None, :] - 1.0
    ranks = jnp.sum(running * grouped.astype(jnp.float32), axis=2).reshape(count)
    return ranks.astype(jnp.int32)


def on_device(
    slave_disp,
    slave_normal,
    gap_zero,
    quad_weight,
    proj_coord,
    multiplier,
    active,
    pair_owner,
    pair_slot,
    master_vol,
    surf_pick,
):
    region_count = lax.axis_size("region")
    dom_count = lax.axis_size("dom")
    owners = region_count * dom_count
    count = slave_disp.shape[1]
    width = master_vol.shape[1]
    capacity = max(2, 2 * count // owners)
    picked = jnp.take(master_vol, surf_pick[0], axis=1)
    moved = lax.all_to_all(
        picked.reshape(12, dom_count, width // dom_count),
        "dom",
        split_axis=1,
        concat_axis=1,
        tiled=True,
    )
    master_surf = moved.reshape(12, width)
    target = pair_owner[:, 0]
    ranks = owner_ranks(target, owners)
    places = target * capacity + ranks
    source = (
        jnp.full((owners * capacity,), count, jnp.int32)
        .at[places]
        .set(jnp.arange(count, dtype=jnp.int32))
    )
    filled = source < count
    source_row = jnp.minimum(source, count - 1)
    slave_part = slave_term(slave_disp, slave_normal, gap_zero, quad_weight)

    def to_slots(values):
        rows = values.shape[0]
        taken = jnp.take(values, source_row, axis=1)
        return jnp.where(filled[None, :], taken, 0.0).reshape(rows, owners, capacity)

    payload = jnp.concatenate(
        [proj_coord, slave_normal, quad_weight, pair_slot[None, :].astype(jnp.float32)], axis=0
    )
    received = send_out(to_slots(payload), region_count, dom_count, capacity)
    recv_proj = received[0:8]
    recv_normal = received[8:11]
    recv_weight = received[11:15]
    recv_slot = received[15].astype(jnp.int32)
    master_disp = jnp.take(master_surf, recv_slot, axis=1)
    mortar_slots = mortar_term(recv_proj, recv_normal, recv_weight, master_disp).reshape(
        4, owners, capacity
    )
    returned = send_back(mortar_slots, region_count, dom_count, capacity)
    mortar = jnp.take(returned, places, axis=1)
    weighted_gap = slave_part - mortar
    multiplier_new = jnp.where(active == 1, jnp.maximum(multiplier - weighted_gap, 0.0), 0.0)
    lagrange_in = send_terms(to_slots(multiplier_new), region_count, dom_count, capacity)
    factor = nodal_factor(recv_proj, recv_weight, lagrange_in)
    force = spread_normal(factor, recv_normal)
    surf_force = jnp.zeros((12, width), jnp.float32).at[:, recv_slot].add(force)
    back_moved = lax.all_to_all(
        surf_force.reshape(12, dom_count, width // dom_count),
        "dom",
        split_axis=1,
        concat_axis=1,
        tiled=True,
    )
    back_local = back_moved.reshape(12, width)
    inverse = (
        jnp.zeros((width,), jnp.int32).at[surf_pick[0]].set(jnp.arange(width, dtype=jnp.int32))
    )
    master_force = jnp.take(back_local, inverse, axis=1)
    return (weighted_gap, multiplier_new, master_force)


def solution(mesh):
    return jax.shard_map(
        on_device,
        mesh=mesh,
        in_specs=(
            P(None, ("region", "dom")),
            P(None, ("region", "dom")),
            P(None, ("region", "dom")),
            P(None, ("region", "dom")),
            P(None, ("region", "dom")),
            P(None, ("region", "dom")),
            P(None, ("region", "dom")),
            P(("region", "dom"), None),
            P(("region", "dom")),
            P(None, ("region", "dom")),
            P(("region", "dom"), None),
        ),
        out_specs=(
            P(None, ("region", "dom")),
            P(None, ("region", "dom")),
            P(None, ("region", "dom")),
        ),
        check_vma=False,
    )
```

profile of v0, /device:TPU:1, one launch (start us, length us, event | category | flops | bytes accessed | tf_op | source)
XLA Modules:
  0.0 948.6 jit_solution(587744632752684037)
XLA Ops:
  2.1 1.6 copy.329
  3.7 14.2 %gather_fusion.4 = f32[4096,12]{1,0:T(8,128)} fusion(f32[12,4096]{0,1:T(8,128)S(1)} %copy.329, s32[4096]{0:T(1024)S(1)} %fusion.19), kind=kCustom, calls=%fused_computation.clone | custom fusion | bytes 409600 | tf_op jit(solution)/shard_map/jit(_take)/gather | solution.py:157
  17.8 3.6 broadcast_select_fusion
  21.5 1.3 copy.330
  22.8 6.0 all-to-all-start.1
  30.1 2.4 fusion.3
  32.5 3.3 copy-done
  37.7 2.8 subtract_reduce_fusion
  40.5 4.7 multiply_reduce_fusion
  46.2 60.4 %scatter_custom_fusion = s32[32768]{0:T(1024)S(1)} fusion(s32[16384]{0:T(1024)S(1)} %bitcast.173, s32[16384]{0:T(1024)S(1)} %iota.25, s32[]{:T(128)} %constant.53.clone.1), kind=kCustom, calls=%fused_computation.109 | custom fusion | bytes 131076 | tf_op jit(solution)/shard_map/scatter | solution.py:172
  106.9 4.7 copy.325
  111.6 112.4 %gather_fusion = f32[32768,16]{1,0:T(8,128)} fusion(f32[16,16384]{0,1:T(8,128)} %copy.325, s32[32768]{0:T(1024)S(1)} %fusion.16), kind=kCustom, calls=%fused_computation.2 | custom fusion | bytes 4325376 | tf_op jit(solution)/shard_map/jit(_take)/gather | solution.py:180
  224.0 9.8 %copy.326 = f32[16,128,256]{2,0,1:T(8,128)S(1)} copy(f32[16,128,256]{0,2,1:T(8,128)} %bitcast.110) | data formatting | bytes 4194304 | tf_op jit(solution)/shard_map/jit(_take)/gather | solution.py:180
  233.9 3.7 multiply_add_fusion.17
  237.5 1.8 select_select_fusion
  239.4 10.8 %all-to-all-start = ((f32[16,128,256]{2,0,1:T(8,128)}), f32[16,128,256]{2,0,1:T(8,128)}, u32[]{:S(2)}, u32[]{:S(2)}) async-start(f32[16,128,256]{2,0,1:T(8,128)} %select_select_fusion), calls=%async_computation | async-start | bytes 4194304 | tf_op jit(solution)/shard_map/all_to_all | solution.py:105
  250.2 3.4 add_add_fusion.1
  254.3 26.1 %all-to-all-done = f32[16,128,256]{2,0,1:T(8,128)} async-done(((f32[16,128,256]{2,0,1:T(8,128)}), f32[16,128,256]{2,0,1:T(8,128)}, u32[]{:S(2)}, u32[]{:S(2)}) %all-to-all-start) | async-done | bytes 2097184 | tf_op jit(solution)/shard_map/all_to_all | solution.py:105
  280.4 8.8 fusion.31
  294.6 119.5 %gather_fusion.1 = f32[32768,12]{1,0:T(8,128)} fusion(f32[12,4096]{0,1:T(8,128)S(1)} %bitcast.109, s32[32768]{0:T(1024)} %broadcast_clamp_fusion), kind=kCustom, calls=%fused_computation.3 | custom fusion | bytes 3276800 | tf_op jit(solution)/shard_map/jit(_take)/gather | solution.py:191
  414.1 9.9 %copy.332 = f32[32768,12]{0,1:T(8,128)S(1)} copy(f32[32768,12]{1,0:T(8,128)} %gather_fusion.1) | data formatting | bytes 3145728 | tf_op jit(solution)/shard_map/jit(_take)/gather | solution.py:191
  426.1 1.1 copy.378
  427.2 1.1 copy.377
  434.4 1.9 add_multiply_fusion.2
  437.4 2.0 add_reduce_fusion.3
  439.8 1.1 copy.339
  440.9 4.3 all-to-all-start.2
  445.7 13.2 %all-to-all-done.2 = f32[4,128,256]{2,0,1:T(4,128)S(1)} async-done(((f32[4,128,256]{2,0,1:T(4,128)}), f32[4,128,256]{2,0,1:T(4,128)S(1)}, u32[]{:S(2)}, u32[]{:S(2)}) %all-to-all-start.2) | async-done | bytes 524320 | tf_op jit(solution)/shard_map/all_to_all | solution.py:112
  458.9 8.5 copy.340
  467.4 60.6 %gather_fusion.2 = f32[16384,4]{1,0:T(8,128)} fusion(f32[4,32768]{0,1:T(8,128)} %bitcast.111, s32[16384]{0:T(1024)S(1)} %broadcast_clamp_fusion.1), kind=kCustom, calls=%fused_computation.4 | custom fusion | bytes 589824 | tf_op jit(solution)/shard_map/jit(_take)/gather | solution.py:196
  528.0 5.5 copy.341
  533.5 1.1 maximum_select_fusion
  534.6 5.0 copy.342
  539.7 112.4 %gather_fusion.3 = f32[32768,4]{1,0:T(8,128)} fusion(f32[4,16384]{0,1:T(8,128)} %copy.342, s32[32768]{0:T(1024)S(1)} %fusion.16), kind=kCustom, calls=%fused_computation.5 | custom fusion | bytes 1179648 | tf_op jit(solution)/shard_map/jit(_take)/gather | solution.py:180
  652.1 9.5 copy.343
  662.7 4.6 all-to-all-start.3
  667.3 15.8 %scatter_custom_fusion.2 = s32[4096]{0:T(1024)S(1)} fusion(s32[4096]{0:T(1024)S(1)} %bitcast.178, s32[4096]{0:T(1024)S(1)} %iota.26, s32[]{:T(128)} %constant.50.clone.1), kind=kCustom, calls=%fused_computation.131 | custom fusion | bytes 16388 | tf_op jit(solution)/shard_map/scatter | solution.py:212
  684.9 1.5 fusion.23
  686.5 2.0 fusion.24
  689.2 4.9 stack.20
  694.0 8.8 copy.348
  702.8 187.8 %scatter_custom_fusion.1 = f32[12,4096]{0,1:T(8,128)S(1)} fusion(s32[32768]{0:T(1024)} %bitcast.171, f32[32768,12]{1,0:T(8,128)} %copy.348, f32[]{:T(128)} %constant.42.clone.1), kind=kCustom, calls=%fused_computation.21 | custom fusion | flops 393216 | bytes 197120 | tf_op jit(solution)/shard_map/scatter-add | solution.py:202
  890.6 1.3 copy.349
  891.9 30.0 %all-to-all-start.4 = ((f32[12,8,512]{2,0,1:T(8,128)}), f32[12,8,512]{2,0,1:T(8,128)S(1)}, u32[]{:S(2)}, u32[]{:S(2)}) async-start(f32[12,8,512]{2,0,1:T(8,128)} %copy.349), calls=%async_computation.4 | async-start | bytes 524288 | tf_op jit(solution)/shard_map/all_to_all | solution.py:203
  922.0 6.5 all-to-all-done.4
  929.1 14.2 %gather_fusion.5 = f32[4096,12]{1,0:T(8,128)} fusion(f32[12,4096]{0,1:T(8,128)S(1)} %bitcast.116, s32[4096]{0:T(1024)S(1)} %copy-done.53), kind=kCustom, calls=%fused_computation.1.clone | custom fusion | bytes 409600 | tf_op jit(solution)/shard_map/jit(_take)/gather | solution.py:214
  943.3 3.6 select_bitcast_fusion
  946.9 1.3 copy.351
  (172 shorter events, 25.9 us)
Async XLA Ops:
  21.4 7.8 copy-start.48
  22.8 216.6 %all-to-all-start.1 = ((f32[12,8,512]{2,0,1:T(8,128)}), f32[12,8,512]{2,0,1:T(8,128)S(1)}, u32[]{:S(2)}, u32[]{:S(2)}) async-start(f32[12,8,512]{2,0,1:T(8,128)} %copy.330), calls=%async_computation.1 | async-start | bytes 524288 | tf_op jit(solution)/shard_map/all_to_all | solution.py:158
  32.5 3.3 copy-start
  40.5 66.2 %copy-start.54 = (s32[16384]{0:T(1024)S(1)}, s32[16384]{0:T(1024)}, u32[]{:S(2)}) copy-start(s32[16384]{0:T(1024)} %param.21) | copy-start | bytes 196612
  40.5 66.2 %copy-start.1 = (f32[3,16384]{1,0:T(4,128)S(1)}, f32[3,16384]{1,0:T(4,128)}, u32[]{:S(2)}) copy-start(f32[3,16384]{1,0:T(4,128)} %param.14) | copy-start | bytes 589828
  40.5 66.2 %copy-start.30 = (f32[4,16384]{1,0:T(4,128)S(1)}, f32[4,16384]{1,0:T(4,128)}, u32[]{:S(2)}) copy-start(f32[4,16384]{1,0:T(4,128)} %param.16) | copy-start | bytes 786436
  40.5 66.2 %copy-start.36 = (f32[8,16384]{1,0:T(8,128)S(1)}, f32[8,16384]{1,0:T(8,128)}, u32[]{:S(2)}) copy-start(f32[8,16384]{1,0:T(8,128)} %param.17) | copy-start | bytes 1572868
  233.8 5.6 copy-start.37
  233.8 5.5 copy-start.39
  239.4 10.8 %copy-start.51 = (f32[4,16384]{1,0:T(4,128)S(1)}, f32[4,16384]{1,0:T(4,128)}, u32[]{:S(2)}) copy-start(f32[4,16384]{1,0:T(4,128)} %param.15) | copy-start | bytes 786436
  239.4 41.0 %all-to-all-start = ((f32[16,128,256]{2,0,1:T(8,128)}), f32[16,128,256]{2,0,1:T(8,128)}, u32[]{:S(2)}, u32[]{:S(2)}) async-start(f32[16,128,256]{2,0,1:T(8,128)} %select_select_fusion), calls=%async_computation | async-start | bytes 4194304 | tf_op jit(solution)/shard_map/all_to_all | solution.py:105
  289.1 4.0 copy-start.28
  424.0 8.7 copy-start.34
  424.1 8.9 copy-start.33
  424.1 9.0 copy-start.32
  424.1 9.2 copy-start.31
  426.1 10.2 %copy-start.4 = (f32[1,1,128,256]{3,1,2,0:T(1,128)}, f32[1,1,128,256]{3,1,2,0:T(1,128)S(1)}, u32[]{:S(2)}) copy-start(f32[1,1,128,256]{3,1,2,0:T(1,128)S(1)} %copy.379) | copy-start | bytes 393220
  427.2 9.1 copy-start.8
  428.3 8.0 copy-start.10
  429.4 6.9 copy-start.24
  430.5 5.8 copy-start.12
  431.6 4.7 copy-start.14
  432.7 3.6 copy-start.16
  432.9 3.5 copy-start.26
  433.1 3.3 copy-start.18
  433.2 3.2 copy-start.20
  433.4 3.0 copy-start.22
  439.5 5.7 copy-start.44
  439.5 5.7 copy-start.45
  439.5 5.7 copy-start.46
  439.5 5.7 copy-start.47
  439.6 6.0 copy-start.50
  440.9 18.0 %all-to-all-start.2 = ((f32[4,128,256]{2,0,1:T(4,128)}), f32[4,128,256]{2,0,1:T(4,128)S(1)}, u32[]{:S(2)}, u32[]{:S(2)}) async-start(f32[4,128,256]{2,0,1:T(4,128)} %copy.339), calls=%async_computation.2 | async-start | bytes 1048576 | tf_op jit(solution)/shard_map/all_to_all | solution.py:112
  528.0 5.5 copy-start.41
  528.0 5.5 copy-start.42
  528.0 5.5 copy-start.43
  534.6 5.1 copy-start.29
  652.1 9.5 copy-start.38
  652.1 9.5 %copy-start.40 = (pred[128,256]{1,0:T(8,128)(4,1)S(1)}, pred[128,256]{1,0:T(8,128)(4,1)}, u32[]{:S(2)}) copy-start(pred[128,256]{1,0:T(8,128)(4,1)} %copy-done.39) | copy-start | bytes 98308
  661.6 5.7 copy-start.52
  662.7 22.2 %copy-start.7 = (f32[1,1,128,256]{3,1,2,0:T(1,128)S(1)}, f32[1,1,128,256]{3,1,2,0:T(1,128)}, u32[]{:S(2)}) copy-start(f32[1,1,128,256]{3,1,2,0:T(1,128)} %copy.372) | copy-start | bytes 393220
  662.7 22.3 %copy-start.25 = (f32[1,1,128,256]{3,1,2,0:T(1,128)S(1)}, f32[1,1,128,256]{3,1,2,0:T(1,128)}, u32[]{:S(2)}) copy-start(f32[1,1,128,256]{3,1,2,0:T(1,128)} %copy-done.24) | copy-start | bytes 393220
  662.7 22.3 %copy-start.27 = (f32[1,1,128,256]{3,1,2,0:T(1,128)S(1)}, f32[1,1,128,256]{3,1,2,0:T(1,128)}, u32[]{:S(2)}) copy-start(f32[1,1,128,256]{3,1,2,0:T(1,128)} %copy-done.26) | copy-start | bytes 393220
  662.7 21.1 %all-to-all-start.3 = ((f32[4,128,256]{2,0,1:T(4,128)}), f32[4,128,256]{2,0,1:T(4,128)S(1)}, u32[]{:S(2)}, u32[]{:S(2)}) async-start(f32[4,128,256]{2,0,1:T(4,128)} %select_select_fusion.1), calls=%async_computation.3 | async-start | bytes 1048576 | tf_op jit(solution)/shard_map/all_to_all | solution.py:119
  684.1 2.4 copy-start.3
  684.1 2.3 copy-start.5
  890.6 38.5 %copy-start.53 = (s32[4096]{0:T(1024)S(1)}, s32[4096]{0:T(1024)}, u32[]{:S(2)}) copy-start(s32[4096]{0:T(1024)} %fusion.20) | copy-start | bytes 49156
  891.9 36.5 %all-to-all-start.4 = ((f32[12,8,512]{2,0,1:T(8,128)}), f32[12,8,512]{2,0,1:T(8,128)S(1)}, u32[]{:S(2)}, u32[]{:S(2)}) async-start(f32[12,8,512]{2,0,1:T(8,128)} %copy.349), calls=%async_computation.4 | async-start | bytes 524288 | tf_op jit(solution)/shard_map/all_to_all | solution.py:203
  (12 other events, 21.9 us)
where the time goes:
time: 960 us; the launch traced here: 949 us
  local copies, waits for them, and re-layouts  603 us (63%)
  other arithmetic  239 us (25%)
  starting transfers between devices  55.7 us (6%)
  waiting for transfers between devices  45.7 us (5%)
    gather x4, local copies, waits for them, and re-layouts, to_slots(): taken = jnp.take(values, source_row, axis=1)  244 us
    scatter-add x1, other arithmetic, on_device(): surf_force = jnp.zeros((12, width), jnp.float32).at[:, recv_slot].add(force)  188 us
    gather x2, local copies, waits for them, and re-layouts, on_device(): master_disp = jnp.take(master_surf, recv_slot, axis=1)  129 us
    gather x2, local copies, waits for them, and re-layouts, on_device(): mortar = jnp.take(returned, places, axis=1)  66.1 us
    scatter x1, local copies, waits for them, and re-layouts, on_device(): source = jnp.full((owners * capacity,), count, jnp.int32).at[places].set(...  60.4 us
    all_to_all x1, starting transfers between devices, on_device(): lax.all_to_all(surf_force.reshape(12, dom_count, width // dom_count), 'do...  30 us
    all_to_all x1, waiting for transfers between devices, send_out(): lax.all_to_all(block, ('region', 'dom'), split_axis=1, concat_axis=1, til...  26.1 us
    unnamed x134, local copies, waits for them, and re-layouts  19.7 us
  transfers between devices with their start and end apart: 5, of which 3 were waited for; matrix products, arithmetic and copies ran while one was open for 24% of the time, Pallas kernels for 0%

commit v1 on v0

v1 whole, which is shorter than its diff:
```python
import functools
import math

import jax
import jax.numpy as jnp
from jax import lax
from jax.experimental import pallas as pl
from jax.experimental.pallas import tpu as pltpu
from jax.sharding import PartitionSpec as P

gauss_point = 1.0 / math.sqrt(3.0)
node_xs = [-1.0, 1.0, 1.0, -1.0]
node_ys = [-1.0, -1.0, 1.0, 1.0]
point_xs = [-gauss_point, gauss_point, gauss_point, -gauss_point]
point_ys = [-gauss_point, -gauss_point, gauss_point, gauss_point]
slave_table = [
    [(1.0 + node_xs[c] * point_xs[q]) * (1.0 + node_ys[c] * point_ys[q]) * 0.25 for q in range(4)]
    for c in range(4)
]

BF = jnp.bfloat16
F32 = jnp.float32
LANE = 256

NN = (((1,), (0,)), ((), ()))
NT = (((1,), (1,)), ((), ()))


def sub_iota(rows, cols):
    return lax.broadcasted_iota(jnp.int32, (rows, cols), 0)


def split(values):
    high = values.astype(BF)
    return high, (values - high.astype(F32)).astype(BF)


def onehot(index, size):
    n = index.shape[1]
    base = (jnp.broadcast_to(index, (16, n)) - sub_iota(16, n)).astype(F32).astype(BF)
    one, zero = jnp.ones((16, n), BF), jnp.zeros((16, n), BF)
    return jnp.concatenate(
        [jnp.where(base == jnp.asarray(16 * g, BF), one, zero) for g in range(size // 16)], axis=0
    )


def spread(index, values, group, count):
    n = index.shape[1]
    base = (jnp.broadcast_to(index, (16, n)) - sub_iota(16, n) // (16 // group)).astype(F32).astype(BF)
    zero = jnp.zeros((16, n), BF)
    return [
        [jnp.where(base == jnp.asarray(group * g, BF), v, zero) for g in range(count // group)]
        for v in values
    ]


def fill_table(rows, table):
    lows = rows.shape[1] // LANE
    parts = [rows[0:8, l * LANE : (l + 1) * LANE] for l in range(lows)]
    parts += [rows[8:12, l * LANE : (l + 1) * LANE] for l in range(lows)]
    high, low = split(jnp.concatenate(parts, axis=0))
    table[0 : 12 * lows, :] = high
    table[12 * lows :, :] = low


def pick_table(table, index, lows):
    n = index.shape[1]
    grabbed = lax.dot_general(table, onehot(index % LANE, LANE), NN, preferred_element_type=F32)
    total = 12 * lows
    low = jnp.broadcast_to(index // LANE, (8, n))
    pair = low - sub_iota(8, n) // 4
    first = jnp.zeros((8, n), F32)
    for l in range(lows):
        at = 8 * l
        value = grabbed[at : at + 8] + grabbed[total + at : total + at + 8]
        first = jnp.where(low == l, value, first)
    second = jnp.zeros((8, n), F32)
    for l in range(lows // 2):
        at = 8 * lows + 8 * l
        value = grabbed[at : at + 8] + grabbed[total + at : total + at + 8]
        second = jnp.where(pair == 2 * l, value, second)
    return first, second[0:4] + second[4:8]


def add_table(first, second, index, lows):
    high, low = split(first)
    group = jnp.concatenate([high.astype(F32), low.astype(F32)], axis=0).astype(BF)
    wide = spread(index // LANE, [group], 1, lows)[0]
    high, low = split(second)
    high, low = high.astype(F32), low.astype(F32)
    group = jnp.concatenate([high, low, high, low], axis=0).astype(BF)
    narrow = spread(index // LANE, [group], 2, lows)[0]
    stacked = jnp.concatenate(wide + narrow, axis=0)
    return lax.dot_general(
        stacked, onehot(index % LANE, LANE), NT, preferred_element_type=F32
    )


def table_part(total, lows, l):
    first = total[16 * l : 16 * l + 8] + total[16 * l + 8 : 16 * l + 16]
    at = 16 * lows + 8 * l
    return first, total[at : at + 4] + total[at + 4 : at + 8]


def pick_kernel(vol, pick, out, table):
    width = vol.shape[1]
    lows = width // LANE
    rows = vol[...]
    fill_table(
        jnp.concatenate([rows[3 * c + j : 3 * c + j + 1] for j in range(3) for c in range(4)], axis=0),
        table,
    )
    count, _, part = out.shape
    for k in range(count):
        first, second = pick_table(table[...], pick[:, k * part : (k + 1) * part], lows)
        out[k, 0:8, :] = first
        out[k, 8:12, :] = second


def owner_pairs(values):
    left = values[:, 0:128].reshape(-1, 8, 128)
    right = values[:, 128:256].reshape(-1, 8, 128)
    sub = lax.broadcasted_iota(jnp.int32, left.shape, 1)
    even = jnp.where(sub < 4, left, pltpu.roll(right, 4, 1))
    odd = jnp.where(sub < 4, pltpu.roll(left, 4, 1), right)
    return even, odd


def owner_rows(even, odd):
    sub = lax.broadcasted_iota(jnp.int32, even.shape, 1)
    left = jnp.where(sub < 4, even, pltpu.roll(odd, 4, 1)).reshape(-1, 128)
    right = jnp.where(sub < 4, pltpu.roll(even, 4, 1), odd).reshape(-1, 128)
    return jnp.concatenate([left, right], axis=1)


def slot_terms(values, owner, rank, owners):
    high, low = split(jnp.concatenate([values] * 4, axis=0))
    first, second = spread(owner, [high, low], 4, owners)
    stacked = jnp.concatenate(first + second, axis=0)
    return lax.dot_general(stacked, onehot(rank, LANE), NT, preferred_element_type=F32)


def store_slots(total, out):
    half = total.shape[0] // 2
    even, odd = owner_pairs(total[0:half, :] + total[half:, :])
    out[:, 0] = even
    out[:, 1] = odd


def request_kernel(step, owner, slot, normal, out, rank, total):
    count = owner.shape[1]
    owners = 2 * out.shape[0]
    row = sub_iota(256, 512)
    col = lax.broadcasted_iota(jnp.int32, (256, 512), 1)
    upper = ((row <= col) | (col >= 256)).astype(F32).astype(BF)

    def ranks(i, base):
        for u in range(4):
            lanes = pl.ds(pl.multiple_of(i * 1024 + u * 256, 256), 256)
            named = onehot(owner[:, lanes], owners)
            sums = lax.dot_general(named, upper, NN, preferred_element_type=F32)
            seen = named.astype(F32) * (sums[:, 0:256] + base)
            rank[:, lanes] = (jnp.sum(seen, axis=0, keepdims=True) - 1.0).astype(jnp.int32)
            base = base + sums[:, 256:512]
        return base

    lax.fori_loop(0, count // 1024, ranks, jnp.zeros((owners, 256), F32))
    total[...] = jnp.zeros_like(total)

    def slots(i, _):
        lanes = pl.ds(pl.multiple_of(i * step, step), step)
        values = jnp.concatenate([slot[:, lanes].astype(F32), normal[:, lanes]], axis=0)
        total[...] += slot_terms(values, owner[:, lanes], rank[:, lanes], owners)
        return 0

    lax.fori_loop(0, count // step, slots, 0)
    store_slots(total[...], out)


def along_kernel(group, surf, recv, out, table):
    lows = surf.shape[0] * surf.shape[2] // LANE
    fill_table(jnp.concatenate([surf[s] for s in range(surf.shape[0])], axis=1), table)

    def step(i, _):
        parts = [recv[i * group + u] for u in range(group)]
        block = jnp.concatenate([p[4 * h : 4 * h + 4] for p in parts for h in range(2)], axis=1)
        index = block[0:1].astype(jnp.int32)
        first, second = pick_table(table[...], index, lows)
        along = first[0:4] * block[1:2] + first[4:8] * block[2:3] + second * block[3:4]
        for u in range(group):
            for h in range(2):
                at = (2 * u + h) * 128
                out[i * group + u, 4 * h : 4 * h + 4, :] = along[:, at : at + 128]
        return 0

    lax.fori_loop(0, recv.shape[0] // group, step, 0)


def signs(xs, inner):
    sub = sub_iota(8, 1)

    def column(number):
        value = jnp.full((8, 1), xs[3], F32)
        for c in range(3):
            value = jnp.where(number == c, xs[c], value)
        return value

    return [column(sub % 4)] * 2 if inner else [column(sub // 4), column(sub // 4 + 2)]


def local_kernel(step, disp, normal, gap, weight, proj, toward, back, part):
    count = disp.shape[1]
    sub4 = sub_iota(4, 1)

    def column(xs):
        value = jnp.full((4, 1), xs[3], F32)
        for a in range(3):
            value = jnp.where(sub4 == a, xs[a], value)
        return value

    def body(i, _):
        lanes = pl.ds(pl.multiple_of(i * step, step), step)
        p, w, d, n, g = proj[:, lanes], weight[:, lanes], disp[:, lanes], normal[:, lanes], gap[:, lanes]
        for inner, out in ((False, toward), (True, back)):
            node_x, node_y = signs(node_xs, inner), signs(node_ys, inner)
            sums = [None, None]
            for q in range(4):
                table = signs([slave_table[a][q] * 0.25 for a in range(4)], not inner)
                first = jnp.broadcast_to(p[2 * q : 2 * q + 1], (8, step))
                second = jnp.broadcast_to(p[2 * q + 1 : 2 * q + 2], (8, step))
                along = jnp.broadcast_to(w[q : q + 1], (8, step))
                for h in range(2):
                    term = (1.0 + node_x[h] * first) * (1.0 + node_y[h] * second) * (along * table[h])
                    sums[h] = term if q == 0 else sums[h] + term
            out[0:8, lanes] = sums[0]
            out[8:16, lanes] = sums[1]
        total = g
        for b in range(4):
            along = n[0:1] * d[3 * b : 3 * b + 1] + n[1:2] * d[3 * b + 1 : 3 * b + 2] + n[2:3] * d[3 * b + 2 : 3 * b + 3]
            total = total + column(slave_table[b]) * along
        points = w * total
        result = column([slave_table[a][0] for a in range(4)]) * points[0:1]
        for q in range(1, 4):
            result = result + column([slave_table[a][q] for a in range(4)]) * points[q : q + 1]
        part[:, lanes] = result
        return 0

    lax.fori_loop(0, count // step, body, 0)


def doubled(values):
    n = values.shape[1]
    rows = [jnp.broadcast_to(values[c : c + 1], (4, n)) for c in range(4)]
    return jnp.concatenate(rows[0:2], axis=0), jnp.concatenate(rows[2:4], axis=0)


def combine(factors, values):
    one, two = doubled(values)
    both = factors[0:8] * one + factors[8:16] * two
    return both[0:4] + both[4:8]


def update_kernel(step, owner, rank, recv, toward, back, part, multiplier, active, gap_out, new_out, out, table, total):
    count = owner.shape[1]
    owners = 2 * out.shape[0]
    half = owners * 4
    high, low = split(owner_rows(recv[:, 0], recv[:, 1]))
    table[0:half, :] = high
    table[half:, :] = low
    total[...] = jnp.zeros_like(total)

    def body(i, _):
        lanes = pl.ds(pl.multiple_of(i * step, step), step)
        names, places = owner[:, lanes], rank[:, lanes]
        grabbed = lax.dot_general(table[...], onehot(places, LANE), NN, preferred_element_type=F32)
        base = jnp.broadcast_to(names, (8, step)) - sub_iota(8, step) // 4
        along = jnp.zeros((8, step), F32)
        for g in range(owners // 2):
            value = grabbed[8 * g : 8 * g + 8] + grabbed[half + 8 * g : half + 8 * g + 8]
            along = jnp.where(base == 2 * g, value, along)
        mortar = combine(toward[:, lanes], along[0:4] + along[4:8])
        weighted = part[:, lanes] - mortar
        lagrange = jnp.where(active[:, lanes] == 1, jnp.maximum(multiplier[:, lanes] - weighted, 0.0), 0.0)
        gap_out[:, lanes] = weighted
        new_out[:, lanes] = lagrange
        total[...] += slot_terms(combine(back[:, lanes], lagrange), names, places, owners)
        return 0

    lax.fori_loop(0, count // step, body, 0)
    store_slots(total[...], out)


def force_kernel(group, recv, factor, out, total):
    lows = out.shape[0] * out.shape[2] // LANE
    total[...] = jnp.zeros_like(total)

    def step(i, _):
        parts = [recv[i * group + u] for u in range(group)]
        block = jnp.concatenate([p[4 * h : 4 * h + 4] for p in parts for h in range(2)], axis=1)
        parts = [factor[i * group + u] for u in range(group)]
        node = jnp.concatenate([p[4 * h : 4 * h + 4] for p in parts for h in range(2)], axis=1)
        index = block[0:1].astype(jnp.int32)
        first = jnp.concatenate([node * block[1:2], node * block[2:3]], axis=0)
        total[...] += add_table(first, node * block[3:4], index, lows)
        return 0

    lax.fori_loop(0, recv.shape[0] // group, step, 0)
    sums = total[...]
    per = out.shape[2] // LANE
    for l in range(lows):
        first, second = table_part(sums, lows, l)
        lanes = slice(l % per * LANE, (l % per + 1) * LANE)
        out[l // per, 0:8, lanes] = first
        out[l // per, 8:12, lanes] = second


def place_kernel(moved, pick, out):
    lows = out.shape[1] // LANE
    rows = jnp.concatenate([moved[k] for k in range(moved.shape[0])], axis=1)
    sums = add_table(rows[0:8], rows[8:12], pick[...], lows)
    for l in range(lows):
        first, second = table_part(sums, lows, l)
        both = jnp.concatenate([first, second], axis=0)
        ordered = jnp.concatenate(
            [both[4 * j + c : 4 * j + c + 1] for c in range(4) for j in range(3)], axis=0
        )
        out[:, l * LANE : (l + 1) * LANE] = ordered


def call(kernel, outs, scratch, cycles, *args):
    vmem = pl.BlockSpec(memory_space=pltpu.VMEM)
    size = sum(a.size * 4 for a in args) + sum(math.prod(o[0]) * 4 for o in outs)
    result = pl.pallas_call(
        kernel,
        out_shape=[jax.ShapeDtypeStruct(*o) for o in outs],
        in_specs=[vmem] * len(args),
        out_specs=[vmem] * len(outs),
        scratch_shapes=[pltpu.VMEM(*s) for s in scratch],
        compiler_params=pltpu.CompilerParams(vmem_limit_bytes=48 * 2**20),
        cost_estimate=pl.CostEstimate(flops=cycles, bytes_accessed=size, transcendentals=0),
    )(*args)
    return result[0] if len(outs) == 1 else result


def on_device(
    slave_disp,
    slave_normal,
    gap_zero,
    quad_weight,
    proj_coord,
    multiplier,
    active,
    pair_owner,
    pair_slot,
    master_vol,
    surf_pick,
):
    region_count = lax.axis_size("region")
    dom_count = lax.axis_size("dom")
    owners = region_count * dom_count
    count = slave_disp.shape[1]
    width = master_vol.shape[1]
    lows = width // LANE
    part = width // dom_count
    step = 1024
    exchange = functools.partial(lax.all_to_all, split_axis=0, concat_axis=0, tiled=True)
    owner = pair_owner.reshape(1, count)
    slots = (owners // 2, 2, 8, 128)
    flat = (owners, 8, 128)
    everyone = ("region", "dom")

    picked = call(
        pick_kernel, [((dom_count, 12, part), F32)], [((24 * lows, LANE), BF)], 4 * 10**9, master_vol, surf_pick
    )
    surf = exchange(picked, "dom")
    request, rank = call(
        functools.partial(request_kernel, step),
        [(slots, F32), ((1, count), jnp.int32)],
        [((8 * owners, LANE), F32)],
        10**10,
        owner,
        pair_slot.reshape(1, count),
        slave_normal,
    )
    recv = exchange(request.reshape(flat), everyone)
    toward, back, slave_part = call(
        functools.partial(local_kernel, 512),
        [((16, count), F32), ((16, count), F32), ((4, count), F32)],
        [],
        10**9,
        slave_disp,
        slave_normal,
        gap_zero,
        quad_weight,
        proj_coord,
    )
    along = call(
        functools.partial(along_kernel, 4), [(flat, F32)], [((24 * lows, LANE), BF)], 10**10, surf, recv
    )
    returned = exchange(along, everyone)
    weighted_gap, multiplier_new, terms = call(
        functools.partial(update_kernel, step),
        [((4, count), F32), ((4, count), F32), (slots, F32)],
        [((8 * owners, LANE), BF), ((8 * owners, LANE), F32)],
        2 * 10**10,
        owner,
        rank,
        returned.reshape(slots),
        toward,
        back,
        slave_part,
        multiplier,
        active,
    )
    factor = exchange(terms.reshape(flat), everyone)
    forces = call(
        functools.partial(force_kernel, 4),
        [((dom_count, 12, part), F32)],
        [((24 * lows, LANE), F32)],
        10**10,
        recv,
        factor,
    )
    moved = exchange(forces, "dom")
    master_force = call(place_kernel, [((12, width), F32)], [], 10**9, moved, surf_pick)
    return (weighted_gap, multiplier_new, master_force)


def solution(mesh):
    both = ("region", "dom")
    return jax.shard_map(
        on_device,
        mesh=mesh,
        in_specs=(P(None, both),) * 7 + (P(both, None), P(both), P(None, both), P(both, None)),
        out_specs=(P(None, both),) * 3,
        check_vma=False,
    )
```

time: 960 us -> 160 us (0.17); the launches traced: 949 us -> 159 us
  local copies, waits for them, and re-layouts: 603 us -> 9.65 us
  other arithmetic: 239 us -> 0 us
  Pallas kernels: 0 us -> 79.1 us
  blocking collectives: 0 us -> 51.5 us
  starting transfers between devices: 55.7 us -> 10.7 us
  waiting for transfers between devices: 45.7 us -> 7.66 us
    gather x10 -> x0, local copies, waits for them, and re-layouts: 468 us -> none  [the longest x4 244 us: to_slots(): taken = jnp.take(values, source_row, axis=1)]
    scatter-add x1 -> x0, other arithmetic: 188 us -> none  [on_device(): surf_force = jnp.zeros((12, width), jnp.float32).at[:, recv_slot].add(force)]
    pallas_call x0 -> x7, Pallas kernels: none -> 79.1 us  [call(): pl.pallas_call(kernel, out_shape=[jax.ShapeDtypeStruct(*o) for o in outs]...]
    scatter x2 -> x0, local copies, waits for them, and re-layouts: 76.1 us -> none  [the longest x1 60.4 us: on_device(): source = jnp.full((owners * capacity,), count, jnp.int32).at[places].set(...]
    all_to_all x0 -> x3, blocking collectives: none -> 51.5 us  [the longest x1 23.6 us: on_device(): recv = exchange(request.reshape(flat), everyone)]
    all_to_all x5 -> x2, starting transfers between devices: 55.7 us -> 10.7 us  [the longest x1 6.1 us: on_device(): surf = exchange(picked, 'dom')]
    all_to_all x5 -> x2, waiting for transfers between devices: 45.7 us -> 7.66 us  [the longest x1 7.66 us: on_device(): returned = exchange(along, everyone)]
    another operation x8 -> x0, local copies, waits for them, and re-layouts: 15.6 us -> none  [the longest x2 13.7 us: spread_normal(): return jnp.stack(result)]
  transfers between devices with their start and end apart: 5 -> 2, of which waited for: 3 -> 1; matrix products, arithmetic and copies ran while one was open for 24% -> 0% of each run, Pallas kernels for 0% -> 13%
where the time goes in v1:
time: 160 us; the launch traced here: 159 us
  Pallas kernels  79.1 us (49%)
  blocking collectives  51.5 us (32%)
  starting transfers between devices  10.7 us (7%)
  local copies, waits for them, and re-layouts  9.65 us (6%)
  waiting for transfers between devices  7.66 us (5%)
    pallas_call x7, Pallas kernels, call(): pl.pallas_call(kernel, out_shape=[jax.ShapeDtypeStruct(*o) for o in outs]...  79.1 us
    all_to_all x1, blocking collectives, on_device(): recv = exchange(request.reshape(flat), everyone)  23.6 us
    all_to_all x1, blocking collectives, on_device(): factor = exchange(terms.reshape(flat), everyone)  17.9 us
    all_to_all x1, blocking collectives, on_device(): moved = exchange(forces, 'dom')  9.98 us
    unnamed x36, local copies, waits for them, and re-layouts  9.65 us
    all_to_all x1, waiting for transfers between devices, on_device(): returned = exchange(along, everyone)  7.66 us
    all_to_all x1, starting transfers between devices, on_device(): surf = exchange(picked, 'dom')  6.1 us
    all_to_all x1, starting transfers between devices, on_device(): returned = exchange(along, everyone)  4.61 us
  transfers between devices with their start and end apart: 2, of which 1 were waited for; matrix products, arithmetic and copies ran while one was open for 0% of the time, Pallas kernels for 13%

profile of v1, /device:TPU:1, one launch (start us, length us, event | category | flops | bytes accessed | tf_op | source)
XLA Modules:
  0.0 159.4 jit_solution(7173378641959558737)
XLA Ops:
  0.6 0.0 copy-start.2
  0.6 0.9 copy-done.2
  1.6 0.0 copy-start.10
  1.6 0.7 copy-done.10
  2.3 1.7 %shard_map.131 = f32[8,12,512]{2,1,0:T(8,128)} custom-call(f32[12,4096]{1,0:T(8,128)S(1)} %copy-done.2, s32[1,4096]{1,0:T(1,128)S(1)} %copy-done.10), custom_call_target="tpu_custom_call" | custom-call | flops 4000000000 | bytes 409600 | tf_op jit(solution)/shard_map/pallas_call | solution.py:333
  4.0 0.0 copy-start.3
  4.0 0.0 copy-start.8
  4.0 0.0 copy-start.9
  4.1 6.1 %all-to-all-start = ((f32[8,12,512]{2,1,0:T(8,128)}), f32[8,12,512]{2,1,0:T(8,128)S(1)}, u32[]{:S(2)}, u32[]{:S(2)}) async-start(f32[8,12,512]{2,1,0:T(8,128)} %shard_map.131), calls=%async_computation | async-start | bytes 524288 | tf_op jit(solution)/shard_map/all_to_all | solution.py:375
  10.2 0.0 copy-done.3
  10.2 0.0 copy-done.8
  10.2 0.0 copy-done.9
  10.2 17.5 %shard_map.130 = (f32[64,2,8,128]{3,2,1,0:T(8,128)S(1)}, s32[1,16384]{1,0:T(1,128)S(1)}) custom-call(s32[1,16384]{1,0:T(1,128)S(1)} %bitcast.9, s32[1,16384]{1,0:T(1,128)S(1)} %bitcast.8, f32[3,16384]{1,0:T(4,128)S(1)} %copy-done.3), custom_call_target="tpu_custom_call" | custom-call | flops 10000000000 | bytes 917504 | tf_op jit(solution)/shard_map/pallas_call | solution.py:333
  27.6 0.0 all-to-all-done.surf
  27.6 23.6 %all_to_all.25.recv = f32[128,8,128]{2,1,0:T(8,128)S(1)} all-to-all(f32[128,8,128]{2,1,0:T(8,128)S(1)} %bitcast.7), channel_id=1, replica_groups=mesh['region'=16,'dom'=8] {'region','dom'}, dimensions={0} | all-to-all | bytes 1048576 | tf_op jit(solution)/shard_map/all_to_all | solution.py:385
  51.3 0.0 copy-start.1
  51.3 0.0 copy-start.5
  51.3 13.6 %shard_map.132 = f32[128,8,128]{2,1,0:T(8,128)} custom-call(f32[8,12,512]{2,1,0:T(8,128)S(1)} %all-to-all-done.surf, f32[128,8,128]{2,1,0:T(8,128)S(1)} %all_to_all.25.recv), custom_call_target="tpu_custom_call" | custom-call | flops 10000000000 | bytes 1245184 | tf_op jit(solution)/shard_map/pallas_call | solution.py:333
  64.9 0.0 copy-start
  64.9 4.6 %all-to-all-start.2 = ((f32[128,8,128]{2,1,0:T(8,128)}), f32[128,8,128]{2,1,0:T(8,128)S(1)}, u32[]{:S(2)}, u32[]{:S(2)}) async-start(f32[128,8,128]{2,1,0:T(8,128)} %shard_map.132), calls=%async_computation.2 | async-start | bytes 1048576 | tf_op jit(solution)/shard_map/all_to_all | solution.py:400
  69.5 0.0 copy-done.1
  69.6 0.0 copy-done.4
  69.6 0.0 copy-done.5
  69.6 0.0 copy-done
  69.6 3.3 %shard_map.133 = (f32[16,16384]{1,0:T(8,128)S(1)}, f32[16,16384]{1,0:T(8,128)S(1)}, f32[4,16384]{1,0:T(4,128)S(1)}) custom-call(f32[12,16384]{1,0:T(8,128)S(1)} %copy-done, f32[3,16384]{1,0:T(4,128)S(1)} %copy-done.3, f32[4,16384]{1,0:T(4,128)S(1)} %copy-done.4, f32[4,16384]{1,0:T(4,128)S(1)} %copy-done.5, f32[8,16384]{1,0:T(8,128)S(1)} %copy-done.1), custom_call_target="tpu_custom_call" | custom-call | flops 1000000000 | bytes 4390912 | tf_op jit(solution)/shard_map/pallas_call | solution.py:333
  72.9 0.0 copy-start.12
  72.9 1.0 copy-done.12
  73.9 0.0 copy-start.14
  73.9 1.0 copy-done.14
  74.8 0.0 copy-start.16
  74.8 0.7 copy-done.16
  75.5 7.7 %all-to-all-done.2 = f32[128,8,128]{2,1,0:T(8,128)S(1)} async-done(((f32[128,8,128]{2,1,0:T(8,128)}), f32[128,8,128]{2,1,0:T(8,128)S(1)}, u32[]{:S(2)}, u32[]{:S(2)}) %all-to-all-start.2) | async-done | bytes 524320 | tf_op jit(solution)/shard_map/all_to_all | solution.py:400
  83.2 0.0 copy-start.6
  83.2 0.9 copy-done.6
  84.1 0.0 copy-start.7
  84.1 0.9 copy-done.7
  85.1 0.0 copy-start.13
  85.1 1.2 copy-done.13
  86.3 1.2 copy-done.15
  87.5 0.0 copy-start.17
  87.5 0.9 copy-done.17
  88.5 27.7 %shard_map.134 = (f32[4,16384]{1,0:T(4,128)}, f32[4,16384]{1,0:T(4,128)}, f32[64,2,8,128]{3,2,1,0:T(8,128)S(1)}) custom-call(s32[1,16384]{1,0:T(1,128)S(1)} %bitcast.10, s32[1,16384]{1,0:T(1,128)S(1)} %get-tuple-element.11.rank, f32[64,2,8,128]{3,2,1,0:T(8,128)S(1)} %bitcast.5, f32[16,16384]{1,0:T(8,128)S(1)} %copy-done.13, f32[16,16384]{1,0:T(8,128)S(1)} %copy-done.15, ...), custom_call_target="tpu_custom_call" | custom-call | flops 20000000000 | bytes 4587520 | tf_op jit(solution)/shard_map/pallas_call | solution.py:333
  116.2 17.9 %all_to_all.26.factor = f32[128,8,128]{2,1,0:T(8,128)S(1)} all-to-all(f32[128,8,128]{2,1,0:T(8,128)S(1)} %bitcast.6), channel_id=1, replica_groups=mesh['region'=16,'dom'=8] {'region','dom'}, dimensions={0} | all-to-all | bytes 1048576 | tf_op jit(solution)/shard_map/all_to_all | solution.py:415
  134.1 13.5 %shard_map.135 = f32[8,12,512]{2,1,0:T(8,128)S(1)} custom-call(f32[128,8,128]{2,1,0:T(8,128)S(1)} %all_to_all.25.recv, f32[128,8,128]{2,1,0:T(8,128)S(1)} %all_to_all.26.factor), custom_call_target="tpu_custom_call" | custom-call | flops 10000000000 | bytes 1245184 | tf_op jit(solution)/shard_map/pallas_call | solution.py:333
  147.6 0.0 copy-start.11
  147.6 10.0 %all_to_all.27.moved = f32[8,12,512]{2,1,0:T(8,128)S(1)} all-to-all(f32[8,12,512]{2,1,0:T(8,128)S(1)} %shard_map.135), channel_id=1, replica_groups=mesh['region'=16,'dom'=8] {'dom'}, dimensions={0} | all-to-all | bytes 393216 | tf_op jit(solution)/shard_map/all_to_all | solution.py:424
  157.6 0.0 copy-done.11
  157.6 1.8 %shard_map.136 = f32[12,4096]{1,0:T(8,128)} custom-call(f32[8,12,512]{2,1,0:T(8,128)S(1)} %all_to_all.27.moved, s32[1,4096]{1,0:T(1,128)S(1)} %copy-done.11), custom_call_target="tpu_custom_call" | custom-call | flops 1000000000 | bytes 409600 | tf_op jit(solution)/shard_map/pallas_call | solution.py:333
  (2 shorter events, 0.0 us)
Async XLA Ops:
  0.6 1.0 copy-start.2
  1.6 0.7 copy-start.10
  4.0 6.1 %copy-start.3 = (f32[3,16384]{1,0:T(4,128)S(1)}, f32[3,16384]{1,0:T(4,128)}, u32[]{:S(2)}) copy-start(f32[3,16384]{1,0:T(4,128)} %normal.3) | copy-start | bytes 589828
  4.0 6.1 %copy-start.8 = (s32[16384]{0:T(1024)S(1)}, s32[16384]{0:T(1024)}, u32[]{:S(2)}) copy-start(s32[16384]{0:T(1024)} %param.19) | copy-start | bytes 196612
  4.0 6.1 %copy-start.9 = (s32[16384,1]{0,1:T(1,128)S(1)}, s32[16384,1]{0,1:T(1,128)}, u32[]{:S(2)}) copy-start(s32[16384,1]{0,1:T(1,128)} %param.18) | copy-start | bytes 196612
  4.1 23.6 %all-to-all-start = ((f32[8,12,512]{2,1,0:T(8,128)}), f32[8,12,512]{2,1,0:T(8,128)S(1)}, u32[]{:S(2)}, u32[]{:S(2)}) async-start(f32[8,12,512]{2,1,0:T(8,128)} %shard_map.131), calls=%async_computation | async-start | bytes 524288 | tf_op jit(solution)/shard_map/all_to_all | solution.py:375
  51.3 18.3 %copy-start.1 = (f32[8,16384]{1,0:T(8,128)S(1)}, f32[8,16384]{1,0:T(8,128)}, u32[]{:S(2)}) copy-start(f32[8,16384]{1,0:T(8,128)} %proj.1) | copy-start | bytes 1572868
  51.3 18.3 %copy-start.4 = (f32[4,16384]{1,0:T(4,128)S(1)}, f32[4,16384]{1,0:T(4,128)}, u32[]{:S(2)}) copy-start(f32[4,16384]{1,0:T(4,128)} %gap.1) | copy-start | bytes 786436
  51.3 18.3 %copy-start.5 = (f32[4,16384]{1,0:T(4,128)S(1)}, f32[4,16384]{1,0:T(4,128)}, u32[]{:S(2)}) copy-start(f32[4,16384]{1,0:T(4,128)} %weight.1) | copy-start | bytes 786436
  64.9 4.7 %copy-start = (f32[12,16384]{1,0:T(8,128)S(1)}, f32[12,16384]{1,0:T(8,128)}, u32[]{:S(2)}) copy-start(f32[12,16384]{1,0:T(8,128)} %disp.1) | copy-start | bytes 2359300
  64.9 18.3 %all-to-all-start.2 = ((f32[128,8,128]{2,1,0:T(8,128)}), f32[128,8,128]{2,1,0:T(8,128)S(1)}, u32[]{:S(2)}, u32[]{:S(2)}) async-start(f32[128,8,128]{2,1,0:T(8,128)} %shard_map.132), calls=%async_computation.2 | async-start | bytes 1048576 | tf_op jit(solution)/shard_map/all_to_all | solution.py:400
  72.9 1.0 copy-start.12
  73.9 1.0 copy-start.14
  74.8 0.7 copy-start.16
  83.2 1.0 copy-start.6
  84.1 0.9 copy-start.7
  85.1 1.2 copy-start.13
  86.3 1.2 copy-start.15
  87.5 0.9 copy-start.17
  147.6 10.0 %copy-start.11 = (s32[1,4096]{1,0:T(1,128)S(1)}, s32[1,4096]{1,0:T(1,128)}, u32[]{:S(2)}) copy-start(s32[1,4096]{1,0:T(1,128)} %pick.3) | copy-start | bytes 49156

commit v2 on v1

--- a/solution.py
+++ b/solution.py
@@ -117,64 +117,143 @@
         out[k, 8:12, :] = second
 
 
-def owner_pairs(values):
-    left = values[:, 0:128].reshape(-1, 8, 128)
-    right = values[:, 128:256].reshape(-1, 8, 128)
-    sub = lax.broadcasted_iota(jnp.int32, left.shape, 1)
-    even = jnp.where(sub < 4, left, pltpu.roll(right, 4, 1))
-    odd = jnp.where(sub < 4, pltpu.roll(left, 4, 1), right)
-    return even, odd
-
-
-def owner_rows(even, odd):
-    sub = lax.broadcasted_iota(jnp.int32, even.shape, 1)
-    left = jnp.where(sub < 4, even, pltpu.roll(odd, 4, 1)).reshape(-1, 128)
-    right = jnp.where(sub < 4, pltpu.roll(even, 4, 1), odd).reshape(-1, 128)
-    return jnp.concatenate([left, right], axis=1)
-
-
-def slot_terms(values, owner, rank, owners):
+def lane_iota(rows, cols):
+    return lax.broadcasted_iota(jnp.int32, (rows, cols), 1)
+
+
+def sort_terms(values, place, lows):
     high, low = split(jnp.concatenate([values] * 4, axis=0))
-    first, second = spread(owner, [high, low], 4, owners)
+    first, second = spread(place // LANE, [high, low], 4, lows)
     stacked = jnp.concatenate(first + second, axis=0)
-    return lax.dot_general(stacked, onehot(rank, LANE), NT, preferred_element_type=F32)
-
-
-def store_slots(total, out):
+    return lax.dot_general(stacked, onehot(place % LANE, LANE), NT, preferred_element_type=F32)
+
+
+def cut_windows(total, offsets, ordered, out, masked):
     half = total.shape[0] // 2
-    even, odd = owner_pairs(total[0:half, :] + total[half:, :])
-    out[:, 0] = even
-    out[:, 1] = odd
-
-
-def request_kernel(step, owner, slot, normal, out, rank, total):
+    sums = total[0:half, :] + total[half:, :]
+    top = sub_iota(8, 128) < 4
+    groups = half // 8
+    left = [sums[8 * g : 8 * g + 8, 0:128] for g in range(groups)]
+    right = [sums[8 * g : 8 * g + 8, 128:256] for g in range(groups)]
+    turned_left = [pltpu.roll(v, 4, 0) for v in left] + [jnp.zeros((8, 128), F32)]
+    turned_right = [pltpu.roll(v, 4, 0) for v in right]
+    for g in range(groups):
+        ordered[4 * g] = jnp.where(top, left[g], turned_right[g])
+        ordered[4 * g + 1] = jnp.where(top, right[g], left[g])
+        ordered[4 * g + 2] = jnp.where(top, turned_left[g], right[g])
+        ordered[4 * g + 3] = jnp.where(top, turned_right[g], turned_left[g + 1])
+    for g in range(4 * groups, ordered.shape[0]):
+        ordered[g] = jnp.zeros((8, 128), F32)
+    lane = lane_iota(8, 128)
+    number = lane + jnp.where(top, 0, 128)
+
+    def window(i, _):
+        for u in range(8):
+            o = i * 8 + u
+            start = offsets[0, o]
+            block, shift = start // 128, start % 128
+            joined = jnp.where(lane >= shift, ordered[block], ordered[block + 1])
+            joined = pltpu.roll(joined, (128 - shift) % 128, 1)
+            if masked:
+                joined = jnp.where(number < offsets[0, o + 1] - start, joined, 0.0)
+            out[o] = joined
+        return 0
+
+    lax.fori_loop(0, out.shape[0] // 8, window, 0)
+
+
+def merge_windows(windows, offsets, merged, table):
+    lane = lane_iota(8, 128)
+    top = sub_iota(8, 128) < 4
+
+    def window(i, carry):
+        for u in range(8):
+            o = i * 8 + u
+            start, later = offsets[0, o], offsets[0, o + 1]
+            block, shift = start // 128, start % 128
+            value = pltpu.roll(windows[o], shift, 1)
+            turned = pltpu.roll(value, 4, 0)
+            one, two = jnp.where(top, value, turned), jnp.where(top, turned, value)
+            first = jnp.where(lane >= shift, one, carry)
+            second = jnp.where(lane >= shift, two, one)
+            merged[block] = first
+            merged[block + 1] = second
+            merged[block + 2] = two
+            ahead = later // 128 - block
+            carry = jnp.where(ahead == 0, first, jnp.where(ahead == 1, second, two))
+        return carry
+
+    lax.fori_loop(0, windows.shape[0] // 8, window, jnp.zeros((8, 128), F32))
+    half = table.shape[0] // 2
+    left, right = [], []
+    for g in range(half // 8):
+        left.append(jnp.where(top, merged[4 * g], merged[4 * g + 2]))
+        right.append(jnp.where(top, merged[4 * g + 1], merged[4 * g + 3]))
+    both = jnp.concatenate([jnp.concatenate(left, axis=0), jnp.concatenate(right, axis=0)], axis=1)
+    high, low = split(both)
+    table[0:half, :] = high
+    table[half:, :] = low
+
+
+def request_kernel(step, owner_hbm, slot_hbm, normal_hbm, out, place, offset, owner, slot, normal, total, named, ordered, scalars, sems):
+    copies = [
+        pltpu.make_async_copy(a, b, sems.at[i])
+        for i, (a, b) in enumerate(((owner_hbm, owner), (slot_hbm, slot), (normal_hbm, normal)))
+    ]
+    for copy in copies:
+        copy.start()
     count = owner.shape[1]
-    owners = 2 * out.shape[0]
-    row = sub_iota(256, 512)
-    col = lax.broadcasted_iota(jnp.int32, (256, 512), 1)
+    owners = out.shape[0]
+    lows = count // LANE
+    total[...] = jnp.zeros_like(total)
+    copies[0].wait()
+
+    def tally(i, sums):
+        for u in range(step // 256):
+            lanes = pl.ds(pl.multiple_of(i * step + u * 256, 256), 256)
+            value = onehot(owner[:, lanes], owners)
+            named[:, lanes] = value
+            sums = sums + value
+        return sums
+
+    sums = lax.fori_loop(0, count // step, tally, jnp.zeros((owners, 256), BF))
+    counts = lax.dot_general(sums, jnp.ones((256, 256), BF), NN, preferred_element_type=F32).astype(BF)
+    before = (sub_iota(owners, owners) > lane_iota(owners, owners)).astype(F32).astype(BF)
+    base = lax.dot_general(before, counts, NN, preferred_element_type=F32) - 1.0
+    counts = lax.dot_general(jnp.ones((16, 256), BF), sums, NT, preferred_element_type=F32).astype(BF)
+    before = (sub_iota(owners, 2 * owners) < lane_iota(owners, 2 * owners)).astype(F32).astype(BF)
+    offset[...] = lax.dot_general(counts, before, NN, preferred_element_type=F32)[0:8].astype(jnp.int32)
+    save = pltpu.make_async_copy(offset, scalars, sems.at[3])
+    save.start()
+    row, col = sub_iota(256, 512), lane_iota(256, 512)
     upper = ((row <= col) | (col >= 256)).astype(F32).astype(BF)
 
     def ranks(i, base):
-        for u in range(4):
-            lanes = pl.ds(pl.multiple_of(i * 1024 + u * 256, 256), 256)
-            named = onehot(owner[:, lanes], owners)
-            sums = lax.dot_general(named, upper, NN, preferred_element_type=F32)
-            seen = named.astype(F32) * (sums[:, 0:256] + base)
-            rank[:, lanes] = (jnp.sum(seen, axis=0, keepdims=True) - 1.0).astype(jnp.int32)
-            base = base + sums[:, 256:512]
+        chunks = []
+        for u in range(step // 256):
+            chunks.append(named[:, pl.ds(pl.multiple_of(i * step + u * 256, 256), 256)])
+        sums = lax.dot_general(jnp.concatenate(chunks, axis=0), upper, NN, preferred_element_type=F32)
+        for u in range(step // 256):
+            part = sums[u * owners : (u + 1) * owners]
+            seen = chunks[u].astype(F32) * (part[:, 0:256] + base)
+            lanes = pl.ds(pl.multiple_of(i * step + u * 256, 256), 256)
+            place[:, lanes] = jnp.sum(seen, axis=0, keepdims=True).astype(jnp.int32)
+            base = base + part[:, 256:512]
         return base
 
-    lax.fori_loop(0, count // 1024, ranks, jnp.zeros((owners, 256), F32))
-    total[...] = jnp.zeros_like(total)
+    lax.fori_loop(0, count // step, ranks, base)
+    copies[1].wait()
+    copies[2].wait()
 
     def slots(i, _):
         lanes = pl.ds(pl.multiple_of(i * step, step), step)
         values = jnp.concatenate([slot[:, lanes].astype(F32), normal[:, lanes]], axis=0)
-        total[...] += slot_terms(values, owner[:, lanes], rank[:, lanes], owners)
+        total[...] += sort_terms(values, place[:, lanes], lows)
         return 0
 
     lax.fori_loop(0, count // step, slots, 0)
-    store_slots(total[...], out)
+    save.wait()
+    cut_windows(total, scalars, ordered, out, True)
 
 
 def along_kernel(group, surf, recv, out, table):
@@ -260,22 +339,31 @@
     return both[0:4] + both[4:8]
 
 
-def update_kernel(step, owner, rank, recv, toward, back, part, multiplier, active, gap_out, new_out, out, table, total):
-    count = owner.shape[1]
-    owners = 2 * out.shape[0]
-    half = owners * 4
-    high, low = split(owner_rows(recv[:, 0], recv[:, 1]))
-    table[0:half, :] = high
-    table[half:, :] = low
+def update_kernel(step, recv, *refs):
+    inputs, outputs, out = refs[0:7], refs[7:9], refs[9]
+    buffers, results = refs[10:17], refs[17:19]
+    table, total, ordered, sems = refs[19:23]
+    copies = [pltpu.make_async_copy(inputs[i], buffers[i], sems.at[i]) for i in range(7)]
+    for copy in copies:
+        copy.start()
+    offsets, place, toward, back, part, multiplier, active = buffers
+    gap_out, new_out = results
+    count = place.shape[1]
+    lows = count // LANE
+    half = lows * 4
     total[...] = jnp.zeros_like(total)
+    copies[0].wait()
+    merge_windows(recv, offsets, ordered, table)
+    for copy in copies[1:]:
+        copy.wait()
 
     def body(i, _):
         lanes = pl.ds(pl.multiple_of(i * step, step), step)
-        names, places = owner[:, lanes], rank[:, lanes]
-        grabbed = lax.dot_general(table[...], onehot(places, LANE), NN, preferred_element_type=F32)
-        base = jnp.broadcast_to(names, (8, step)) - sub_iota(8, step) // 4
+        places = place[:, lanes]
+        grabbed = lax.dot_general(table[...], onehot(places % LANE, LANE), NN, preferred_element_type=F32)
+        base = jnp.broadcast_to(places // LANE, (8, step)) - sub_iota(8, step) // 4
         along = jnp.zeros((8, step), F32)
-        for g in range(owners // 2):
+        for g in range(lows // 2):
             value = grabbed[8 * g : 8 * g + 8] + grabbed[half + 8 * g : half + 8 * g + 8]
             along = jnp.where(base == 2 * g, value, along)
         mortar = combine(toward[:, lanes], along[0:4] + along[4:8])
@@ -283,11 +371,16 @@
         lagrange = jnp.where(active[:, lanes] == 1, jnp.maximum(multiplier[:, lanes] - weighted, 0.0), 0.0)
         gap_out[:, lanes] = weighted
         new_out[:, lanes] = lagrange
-        total[...] += slot_terms(combine(back[:, lanes], lagrange), names, places, owners)
+        total[...] += sort_terms(combine(back[:, lanes], lagrange), places, lows)
         return 0
 
     lax.fori_loop(0, count // step, body, 0)
-    store_slots(total[...], out)
+    saves = [pltpu.make_async_copy(results[i], outputs[i], sems.at[7 + i]) for i in range(2)]
+    for save in saves:
+        save.start()
+    cut_windows(total, offsets, ordered, out, False)
+    for save in saves:
+        save.wait()
 
 
 def force_kernel(group, recv, factor, out, total):
@@ -327,16 +420,17 @@
         out[:, l * LANE : (l + 1) * LANE] = ordered
 
 
-def call(kernel, outs, scratch, cycles, *args):
-    vmem = pl.BlockSpec(memory_space=pltpu.VMEM)
+def call(kernel, ins, outs, scratch, cycles, *args):
     size = sum(a.size * 4 for a in args) + sum(math.prod(o[0]) * 4 for o in outs)
+    spaces = {"v": pltpu.VMEM, "h": pl.ANY}
+    places = [pl.BlockSpec(memory_space=spaces[p]) for p in ins]
     result = pl.pallas_call(
         kernel,
         out_shape=[jax.ShapeDtypeStruct(*o) for o in outs],
-        in_specs=[vmem] * len(args),
-        out_specs=[vmem] * len(outs),
-        scratch_shapes=[pltpu.VMEM(*s) for s in scratch],
-        compiler_params=pltpu.CompilerParams(vmem_limit_bytes=48 * 2**20),
+        in_specs=places[: len(args)],
+        out_specs=places[len(args) :],
+        scratch_shapes=scratch,
+        compiler_params=pltpu.CompilerParams(vmem_limit_bytes=56 * 2**20),
         cost_estimate=pl.CostEstimate(flops=cycles, bytes_accessed=size, transcendentals=0),
     )(*args)
     return result[0] if len(outs) == 1 else result
@@ -362,30 +456,42 @@
     width = master_vol.shape[1]
     lows = width // LANE
     part = width // dom_count
-    step = 1024
+    step = 4096
+    blocks = count // LANE
     exchange = functools.partial(lax.all_to_all, split_axis=0, concat_axis=0, tiled=True)
     owner = pair_owner.reshape(1, count)
-    slots = (owners // 2, 2, 8, 128)
     flat = (owners, 8, 128)
     everyone = ("region", "dom")
-
-    picked = call(
-        pick_kernel, [((dom_count, 12, part), F32)], [((24 * lows, LANE), BF)], 4 * 10**9, master_vol, surf_pick
-    )
-    surf = exchange(picked, "dom")
-    request, rank = call(
+    whole, quad, wide = (1, count), (4, count), (16, count)
+    table = pltpu.VMEM((24 * lows, LANE), BF)
+
+    request, place, offset = call(
         functools.partial(request_kernel, step),
-        [(slots, F32), ((1, count), jnp.int32)],
-        [((8 * owners, LANE), F32)],
+        "hhhvvv",
+        [(flat, F32), (whole, jnp.int32), ((8, 2 * owners), jnp.int32)],
+        [
+            pltpu.VMEM(whole, jnp.int32),
+            pltpu.VMEM(whole, jnp.int32),
+            pltpu.VMEM((3, count), F32),
+            pltpu.VMEM((8 * blocks, LANE), F32),
+            pltpu.VMEM((owners, count), BF),
+            pltpu.VMEM((2 * blocks + 4, 8, 128), F32),
+            pltpu.SMEM((8, 2 * owners), jnp.int32),
+            pltpu.SemaphoreType.DMA((4,)),
+        ],
         10**10,
         owner,
         pair_slot.reshape(1, count),
         slave_normal,
     )
-    recv = exchange(request.reshape(flat), everyone)
+    request, master_vol = lax.optimization_barrier((request, master_vol))
+    recv = exchange(request, everyone)
+    picked = call(pick_kernel, "vvv", [((dom_count, 12, part), F32)], [table], 10**9, master_vol, surf_pick)
+    surf = exchange(picked, "dom")
     toward, back, slave_part = call(
         functools.partial(local_kernel, 512),
-        [((16, count), F32), ((16, count), F32), ((4, count), F32)],
+        "v" * 8,
+        [(wide, F32), (wide, F32), (quad, F32)],
         [],
         10**9,
         slave_disp,
@@ -394,35 +500,49 @@
         quad_weight,
         proj_coord,
     )
-    along = call(
-        functools.partial(along_kernel, 4), [(flat, F32)], [((24 * lows, LANE), BF)], 10**10, surf, recv
-    )
+    along = call(functools.partial(along_kernel, 32), "vvv", [(flat, F32)], [table], 10**10, surf, recv)
     returned = exchange(along, everyone)
     weighted_gap, multiplier_new, terms = call(
         functools.partial(update_kernel, step),
-        [((4, count), F32), ((4, count), F32), (slots, F32)],
-        [((8 * owners, LANE), BF), ((8 * owners, LANE), F32)],
+        "vhhhhhhhhhv",
+        [(quad, F32), (quad, F32), (flat, F32)],
+        [
+            pltpu.SMEM((8, 2 * owners), jnp.int32),
+            pltpu.VMEM(whole, jnp.int32),
+            pltpu.VMEM(wide, F32),
+            pltpu.VMEM(wide, F32),
+            pltpu.VMEM(quad, F32),
+            pltpu.VMEM(quad, F32),
+            pltpu.VMEM(quad, jnp.int32),
+            pltpu.VMEM(quad, F32),
+            pltpu.VMEM(quad, F32),
+            pltpu.VMEM((8 * blocks, LANE), BF),
+            pltpu.VMEM((8 * blocks, LANE), F32),
+            pltpu.VMEM((2 * blocks + 4, 8, 128), F32),
+            pltpu.SemaphoreType.DMA((9,)),
+        ],
         2 * 10**10,
-        owner,
-        rank,
-        returned.reshape(slots),
+        returned,
+        offset,
+        place,
         toward,
         back,
         slave_part,
         multiplier,
         active,
     )
-    factor = exchange(terms.reshape(flat), everyone)
+    factor = exchange(terms, everyone)
     forces = call(
-        functools.partial(force_kernel, 4),
+        functools.partial(force_kernel, 32),
+        "vvv",
         [((dom_count, 12, part), F32)],
-        [((24 * lows, LANE), F32)],
+        [pltpu.VMEM((24 * lows, LANE), F32)],
         10**10,
         recv,
         factor,
     )
     moved = exchange(forces, "dom")
-    master_force = call(place_kernel, [((12, width), F32)], [], 10**9, moved, surf_pick)
+    master_force = call(place_kernel, "vvv", [((12, width), F32)], [], 10**9, moved, surf_pick)
     return (weighted_gap, multiplier_new, master_force)
 
 

time: 160 us -> 141 us (0.88)
  Pallas kernels: 79.1 us -> 61.1 us
  blocking collectives: 51.5 us -> 65.8 us
  local copies, waits for them, and re-layouts: 9.65 us -> 0.79 us
  starting transfers between devices: 10.7 us -> 4.59 us
    pallas_call x7, Pallas kernels: 79.1 us -> 61.1 us  [call(): pl.pallas_call(kernel, out_shape=[jax.ShapeDtypeStruct(*o) for o in outs]...]
    all_to_all x2 -> x3, blocking collectives: 41.5 us -> 54.2 us  [the longest x1 22.4 us: on_device(): recv = exchange(request, everyone)]
    unnamed x36 -> x4, local copies, waits for them, and re-layouts: 9.65 us -> 0.79 us
    all_to_all x1 -> x0, starting transfers between devices: 6.1 us -> none  [on_device(): surf = exchange(picked, 'dom')]
    all_to_all x1, blocking collectives: 9.98 us -> 11.6 us  [on_device(): moved = exchange(forces, 'dom')]
  transfers between devices with their start and end apart: 2 -> 1, of which waited for: 1 -> 1; matrix products, arithmetic and copies ran while one was open for 0% -> 0% of each run, Pallas kernels for 13% -> 4%
where the time goes in v2:
time: 141 us; the launch traced here: 140 us
  blocking collectives  65.8 us (47%)
  Pallas kernels  61.1 us (43%)
  waiting for transfers between devices  7.32 us (5%)
  starting transfers between devices  4.59 us (3%)
    pallas_call x7, Pallas kernels, call(): pl.pallas_call(kernel, out_shape=[jax.ShapeDtypeStruct(*o) for o in outs]...  61.1 us
    all_to_all x1, blocking collectives, on_device(): recv = exchange(request, everyone)  22.4 us
    all_to_all x1, blocking collectives, on_device(): factor = exchange(terms, everyone)  19.1 us
    all_to_all x1, blocking collectives, on_device(): surf = exchange(picked, 'dom')  12.7 us
    all_to_all x1, blocking collectives, on_device(): moved = exchange(forces, 'dom')  11.6 us
    all_to_all x1, waiting for transfers between devices, on_device(): returned = exchange(along, everyone)  7.32 us
    all_to_all x1, starting transfers between devices, on_device(): returned = exchange(along, everyone)  4.59 us
  transfers between devices with their start and end apart: 1, of which 1 were waited for; matrix products, arithmetic and copies ran while one was open for 0% of the time, Pallas kernels for 4%

profile of v2, /device:TPU:1, one launch (start us, length us, event | category | flops | bytes accessed | tf_op | source)
XLA Modules:
  0.0 140.2 jit_solution(9742682359903979965)
XLA Ops:
  0.6 13.3 %shard_map.130 = (f32[128,8,128]{2,1,0:T(8,128)}, s32[1,16384]{1,0:T(1,128)}, s32[8,256]{1,0:T(8,128)}) custom-call(s32[1,16384]{1,0:T(1,128)} %bitcast.2, s32[1,16384]{1,0:T(1,128)} %bitcast.3, f32[3,16384]{1,0:T(4,128)} %normal.1), custom_call_target="tpu_custom_call" | custom-call | flops 10000000000 | bytes 925696 | tf_op jit(solution)/shard_map/pallas_call | solution.py:427
  13.9 2.7 %shard_map.131 = f32[8,12,512]{2,1,0:T(8,128)} custom-call(f32[12,4096]{1,0:T(8,128)} %vol, s32[1,4096]{1,0:T(1,128)} %pick.3), custom_call_target="tpu_custom_call" | custom-call | flops 1000000000 | bytes 409600 | tf_op jit(solution)/shard_map/pallas_call | solution.py:427
  16.6 0.0 copy-start.1
  16.6 12.7 %all_to_all.25.surf = f32[8,12,512]{2,1,0:T(8,128)} all-to-all(f32[8,12,512]{2,1,0:T(8,128)} %shard_map.131), channel_id=1, replica_groups=mesh['region'=16,'dom'=8] {'dom'}, dimensions={0} | all-to-all | bytes 393216 | tf_op jit(solution)/shard_map/all_to_all | solution.py:490
  29.3 0.0 copy-done.1
  29.3 22.4 %all_to_all.26.recv = f32[128,8,128]{2,1,0:T(8,128)} all-to-all(f32[128,8,128]{2,1,0:T(8,128)S(1)} %copy-done.1), channel_id=1, replica_groups=mesh['region'=16,'dom'=8] {'region','dom'}, dimensions={0} | all-to-all | bytes 1048576 | tf_op jit(solution)/shard_map/all_to_all | solution.py:488
  51.8 9.3 %shard_map.132 = f32[128,8,128]{2,1,0:T(8,128)} custom-call(f32[8,12,512]{2,1,0:T(8,128)} %all_to_all.25.surf, f32[128,8,128]{2,1,0:T(8,128)} %all_to_all.26.recv), custom_call_target="tpu_custom_call" | custom-call | flops 10000000000 | bytes 1245184 | tf_op jit(solution)/shard_map/pallas_call | solution.py:427
  61.1 4.6 %all-to-all-start.2 = ((f32[128,8,128]{2,1,0:T(8,128)}), f32[128,8,128]{2,1,0:T(8,128)S(1)}, u32[]{:S(2)}, u32[]{:S(2)}) async-start(f32[128,8,128]{2,1,0:T(8,128)} %shard_map.132), calls=%async_computation.2 | async-start | bytes 1048576 | tf_op jit(solution)/shard_map/all_to_all | solution.py:504
  65.7 6.2 %shard_map.133 = (f32[16,16384]{1,0:T(8,128)}, f32[16,16384]{1,0:T(8,128)}, f32[4,16384]{1,0:T(4,128)}) custom-call(f32[12,16384]{1,0:T(8,128)} %disp.1, f32[3,16384]{1,0:T(4,128)} %normal.1, f32[4,16384]{1,0:T(4,128)} %gap.1, f32[4,16384]{1,0:T(4,128)} %weight.1, f32[8,16384]{1,0:T(8,128)} %proj.1), custom_call_target="tpu_custom_call" | custom-call | flops 1000000000 | bytes 4390912 | tf_op jit(solution)/shard_map/pallas_call | solution.py:427
  71.9 7.3 %all-to-all-done.2.recv = f32[128,8,128]{2,1,0:T(8,128)S(1)} async-done(((f32[128,8,128]{2,1,0:T(8,128)}), f32[128,8,128]{2,1,0:T(8,128)S(1)}, u32[]{:S(2)}, u32[]{:S(2)}) %all-to-all-start.2) | async-done | bytes 524320 | tf_op jit(solution)/shard_map/all_to_all | solution.py:504
  79.2 0.0 copy-start
  79.2 0.8 copy-done
  80.0 17.5 %shard_map.134 = (f32[4,16384]{1,0:T(4,128)}, f32[4,16384]{1,0:T(4,128)}, f32[128,8,128]{2,1,0:T(8,128)}) custom-call(f32[128,8,128]{2,1,0:T(8,128)} %copy-done, s32[8,256]{1,0:T(8,128)} %get-tuple-element.17.refs_0_, s32[1,16384]{1,0:T(1,128)} %get-tuple-element.18.refs_1_, f32[16,16384]{1,0:T(8,128)} %get-tuple-element.19.refs_2_, ...), custom_call_target="tpu_custom_call" | custom-call | flops 20000000000 | bytes 4530176 | tf_op jit(solution)/shard_map/pallas_call | solution.py:427
  97.5 19.1 %all_to_all.27.factor = f32[128,8,128]{2,1,0:T(8,128)} all-to-all(f32[128,8,128]{2,1,0:T(8,128)} %get-tuple-element.24), channel_id=1, replica_groups=mesh['region'=16,'dom'=8] {'region','dom'}, dimensions={0} | all-to-all | bytes 1048576 | tf_op jit(solution)/shard_map/all_to_all | solution.py:534
  116.6 9.3 %shard_map.135 = f32[8,12,512]{2,1,0:T(8,128)} custom-call(f32[128,8,128]{2,1,0:T(8,128)} %all_to_all.26.recv, f32[128,8,128]{2,1,0:T(8,128)} %all_to_all.27.factor), custom_call_target="tpu_custom_call" | custom-call | flops 10000000000 | bytes 1245184 | tf_op jit(solution)/shard_map/pallas_call | solution.py:427
  125.9 11.6 %all_to_all.28.moved = f32[8,12,512]{2,1,0:T(8,128)} all-to-all(f32[8,12,512]{2,1,0:T(8,128)} %shard_map.135), channel_id=1, replica_groups=mesh['region'=16,'dom'=8] {'dom'}, dimensions={0} | all-to-all | bytes 393216 | tf_op jit(solution)/shard_map/all_to_all | solution.py:544
  137.5 2.7 %shard_map.136 = f32[12,4096]{1,0:T(8,128)} custom-call(f32[8,12,512]{2,1,0:T(8,128)} %all_to_all.28.moved, s32[1,4096]{1,0:T(1,128)} %pick.3), custom_call_target="tpu_custom_call" | custom-call | flops 1000000000 | bytes 409600 | tf_op jit(solution)/shard_map/pallas_call | solution.py:427
Async XLA Ops:
  16.6 12.7 %copy-start.1 = (f32[128,8,128]{2,1,0:T(8,128)S(1)}, f32[128,8,128]{2,1,0:T(8,128)}, u32[]{:S(2)}) copy-start(f32[128,8,128]{2,1,0:T(8,128)} %get-tuple-element.16) | copy-start | bytes 1572868
  61.1 18.1 %all-to-all-start.2 = ((f32[128,8,128]{2,1,0:T(8,128)}), f32[128,8,128]{2,1,0:T(8,128)S(1)}, u32[]{:S(2)}, u32[]{:S(2)}) async-start(f32[128,8,128]{2,1,0:T(8,128)} %shard_map.132), calls=%async_computation.2 | async-start | bytes 1048576 | tf_op jit(solution)/shard_map/all_to_all | solution.py:504
  79.2 0.8 copy-start

commit v3 on v2

--- a/solution.py
+++ b/solution.py
@@ -102,19 +102,19 @@
     return first, total[at : at + 4] + total[at + 4 : at + 8]
 
 
-def pick_kernel(vol, pick, out, table):
-    width = vol.shape[1]
+def surface_kernel(vol, pick, out, table):
+    parts, _, width = vol.shape
     lows = width // LANE
-    rows = vol[...]
-    fill_table(
-        jnp.concatenate([rows[3 * c + j : 3 * c + j + 1] for j in range(3) for c in range(4)], axis=0),
-        table,
-    )
-    count, _, part = out.shape
-    for k in range(count):
-        first, second = pick_table(table[...], pick[:, k * part : (k + 1) * part], lows)
-        out[k, 0:8, :] = first
-        out[k, 8:12, :] = second
+    part = width // parts
+    lanes = pl.ds(pl.multiple_of(lax.axis_index("dom") * part, part), part)
+    rows = []
+    for s in range(parts):
+        fill_table(vol[s], table.at[s])
+        first, second = pick_table(table[s], pick[s, :, lanes], lows)
+        rows.append(jnp.concatenate([first, second], axis=0))
+    rows = jnp.concatenate(rows, axis=1)
+    order = [rows[3 * c + j : 3 * c + j + 1] for j in range(3) for c in range(4)]
+    fill_table(jnp.concatenate(order, axis=0), out)
 
 
 def lane_iota(rows, cols):
@@ -256,9 +256,8 @@
     cut_windows(total, scalars, ordered, out, True)
 
 
-def along_kernel(group, surf, recv, out, table):
-    lows = surf.shape[0] * surf.shape[2] // LANE
-    fill_table(jnp.concatenate([surf[s] for s in range(surf.shape[0])], axis=1), table)
+def along_kernel(group, table, recv, out):
+    lows = table.shape[0] // 24
 
     def step(i, _):
         parts = [recv[i * group + u] for u in range(group)]
@@ -339,22 +338,23 @@
     return both[0:4] + both[4:8]
 
 
-def update_kernel(step, recv, *refs):
-    inputs, outputs, out = refs[0:7], refs[7:9], refs[9]
-    buffers, results = refs[10:17], refs[17:19]
-    table, total, ordered, sems = refs[19:23]
-    copies = [pltpu.make_async_copy(inputs[i], buffers[i], sems.at[i]) for i in range(7)]
+def update_kernel(step, *refs):
+    inputs, outputs, out = refs[0:8], refs[8:10], refs[10]
+    buffers, results = refs[11:19], refs[19:21]
+    table, total, ordered, sems = refs[21:25]
+    copies = [pltpu.make_async_copy(inputs[i], buffers[i], sems.at[i]) for i in range(8)]
     for copy in copies:
         copy.start()
-    offsets, place, toward, back, part, multiplier, active = buffers
+    recv, offsets, place, toward, back, part, multiplier, active = buffers
     gap_out, new_out = results
     count = place.shape[1]
     lows = count // LANE
     half = lows * 4
     total[...] = jnp.zeros_like(total)
-    copies[0].wait()
+    for copy in copies[0:2]:
+        copy.wait()
     merge_windows(recv, offsets, ordered, table)
-    for copy in copies[1:]:
+    for copy in copies[2:]:
         copy.wait()
 
     def body(i, _):
@@ -375,7 +375,7 @@
         return 0
 
     lax.fori_loop(0, count // step, body, 0)
-    saves = [pltpu.make_async_copy(results[i], outputs[i], sems.at[7 + i]) for i in range(2)]
+    saves = [pltpu.make_async_copy(results[i], outputs[i], sems.at[8 + i]) for i in range(2)]
     for save in saves:
         save.start()
     cut_windows(total, offsets, ordered, out, False)
@@ -420,7 +420,7 @@
         out[:, l * LANE : (l + 1) * LANE] = ordered
 
 
-def call(kernel, ins, outs, scratch, cycles, *args):
+def call(kernel, ins, outs, scratch, cycles, *args, mebibytes=48):
     size = sum(a.size * 4 for a in args) + sum(math.prod(o[0]) * 4 for o in outs)
     spaces = {"v": pltpu.VMEM, "h": pl.ANY}
     places = [pl.BlockSpec(memory_space=spaces[p]) for p in ins]
@@ -430,7 +430,7 @@
         in_specs=places[: len(args)],
         out_specs=places[len(args) :],
         scratch_shapes=scratch,
-        compiler_params=pltpu.CompilerParams(vmem_limit_bytes=56 * 2**20),
+        compiler_params=pltpu.CompilerParams(vmem_limit_bytes=mebibytes * 2**20),
         cost_estimate=pl.CostEstimate(flops=cycles, bytes_accessed=size, transcendentals=0),
     )(*args)
     return result[0] if len(outs) == 1 else result
@@ -463,8 +463,9 @@
     flat = (owners, 8, 128)
     everyone = ("region", "dom")
     whole, quad, wide = (1, count), (4, count), (16, count)
-    table = pltpu.VMEM((24 * lows, LANE), BF)
-
+
+    volume = lax.all_gather(master_vol, "dom")
+    picks = lax.all_gather(surf_pick, "dom")
     request, place, offset = call(
         functools.partial(request_kernel, step),
         "hhhvvv",
@@ -483,11 +484,18 @@
         owner,
         pair_slot.reshape(1, count),
         slave_normal,
-    )
-    request, master_vol = lax.optimization_barrier((request, master_vol))
+        mebibytes=56,
+    )
     recv = exchange(request, everyone)
-    picked = call(pick_kernel, "vvv", [((dom_count, 12, part), F32)], [table], 10**9, master_vol, surf_pick)
-    surf = exchange(picked, "dom")
+    table = call(
+        surface_kernel,
+        "vvv",
+        [((24 * lows, LANE), BF)],
+        [pltpu.VMEM((dom_count, 24 * lows, LANE), BF)],
+        10**9,
+        volume,
+        picks,
+    )
     toward, back, slave_part = call(
         functools.partial(local_kernel, 512),
         "v" * 8,
@@ -499,14 +507,16 @@
         gap_zero,
         quad_weight,
         proj_coord,
-    )
-    along = call(functools.partial(along_kernel, 32), "vvv", [(flat, F32)], [table], 10**10, surf, recv)
+        mebibytes=56,
+    )
+    along = call(functools.partial(along_kernel, 32), "vvv", [(flat, F32)], [], 10**10, table, recv)
     returned = exchange(along, everyone)
     weighted_gap, multiplier_new, terms = call(
         functools.partial(update_kernel, step),
-        "vhhhhhhhhhv",
+        "hhhhhhhhhhv",
         [(quad, F32), (quad, F32), (flat, F32)],
         [
+            pltpu.VMEM(flat, F32),
             pltpu.SMEM((8, 2 * owners), jnp.int32),
             pltpu.VMEM(whole, jnp.int32),
             pltpu.VMEM(wide, F32),
@@ -519,7 +529,7 @@
             pltpu.VMEM((8 * blocks, LANE), BF),
             pltpu.VMEM((8 * blocks, LANE), F32),
             pltpu.VMEM((2 * blocks + 4, 8, 128), F32),
-            pltpu.SemaphoreType.DMA((9,)),
+            pltpu.SemaphoreType.DMA((10,)),
         ],
         2 * 10**10,
         returned,
@@ -530,6 +540,7 @@
         slave_part,
         multiplier,
         active,
+        mebibytes=56,
     )
     factor = exchange(terms, everyone)
     forces = call(

time: 141 us -> 144 us (1.021)
  blocking collectives: 65.8 us -> 43 us
  starting transfers between devices: 4.59 us -> 21.5 us
  between operations: 0.66 us -> 14.1 us
  Pallas kernels: 61.1 us -> 54.6 us
  local copies, waits for them, and re-layouts: 0.79 us -> 2.41 us
    all_to_all x2 -> x0, blocking collectives: 35.1 us -> none  [the longest x1 22.4 us: on_device(): recv = exchange(request, everyone)]
    all_gather x0 -> x1, blocking collectives: none -> 14.6 us  [on_device(): picks = lax.all_gather(surf_pick, 'dom')]
    all_to_all x0 -> x1, starting transfers between devices: none -> 11.5 us  [on_device(): recv = exchange(request, everyone)]
    pallas_call x7, Pallas kernels: 61.1 us -> 54.6 us  [call(): pl.pallas_call(kernel, out_shape=[jax.ShapeDtypeStruct(*o) for o in outs]...]
    all_to_all x1, starting transfers between devices: 4.59 us -> 9.92 us  [on_device(): returned = exchange(along, everyone)]
    unnamed x4 -> x6, local copies, waits for them, and re-layouts: 0.79 us -> 2.41 us
    all_to_all x1, blocking collectives: 11.6 us -> 9.98 us  [on_device(): moved = exchange(forces, 'dom')]
  transfers between devices with their start and end apart: 1 -> 3, of which waited for: 1 -> 1; matrix products, arithmetic and copies ran while one was open for 0% -> 0% of each run, Pallas kernels for 4% -> 14%
where the time goes in v3:
time: 144 us
  Pallas kernels  54.6 us (38%)
  blocking collectives  43 us (30%)
  starting transfers between devices  21.5 us (15%)
  between operations  14.1 us (10%)
  waiting for transfers between devices  7.98 us (6%)
  local copies, waits for them, and re-layouts  2.41 us (2%)
    pallas_call x7, Pallas kernels, call(): pl.pallas_call(kernel, out_shape=[jax.ShapeDtypeStruct(*o) for o in outs]...  54.6 us
    all_to_all x1, blocking collectives, on_device(): factor = exchange(terms, everyone)  18.4 us
    all_gather x1, blocking collectives, on_device(): picks = lax.all_gather(surf_pick, 'dom')  14.6 us
    all_to_all x1, starting transfers between devices, on_device(): recv = exchange(request, everyone)  11.5 us
    all_to_all x1, blocking collectives, on_device(): moved = exchange(forces, 'dom')  9.98 us
    all_to_all x1, starting transfers between devices, on_device(): returned = exchange(along, everyone)  9.92 us
    all_to_all x1, waiting for transfers between devices, on_device(): returned = exchange(along, everyone)  7.29 us
  transfers between devices with their start and end apart: 3, of which 1 were waited for; matrix products, arithmetic and copies ran while one was open for 0% of the time, Pallas kernels for 14%

profile of v3, /device:TPU:1, one launch (start us, length us, event | category | flops | bytes accessed | tf_op | source)
XLA Modules:
  0.0 143.6 jit_solution(17499013100600264657)
XLA Ops:
  7.2 0.0 all-gather.6.cloned.1.call-start
  7.2 0.7 all-gather.6.cloned.1.call-update
  7.9 0.0 copy-start
  7.9 13.3 %shard_map.131 = (f32[128,8,128]{2,1,0:T(8,128)}, s32[1,16384]{1,0:T(1,128)}, s32[8,256]{1,0:T(8,128)}) custom-call(s32[1,16384]{1,0:T(1,128)} %bitcast.6, s32[1,16384]{1,0:T(1,128)} %bitcast.7, f32[3,16384]{1,0:T(4,128)} %normal.1), custom_call_target="tpu_custom_call" | custom-call | flops 10000000000 | bytes 925696 | tf_op jit(solution)/shard_map/pallas_call | solution.py:427
  21.2 11.5 %all-to-all-start = ((f32[128,8,128]{2,1,0:T(8,128)}), f32[128,8,128]{2,1,0:T(8,128)S(1)}, u32[]{:S(2)}, u32[]{:S(2)}) async-start(f32[128,8,128]{2,1,0:T(8,128)} %get-tuple-element.12), calls=%async_computation | async-start | bytes 1048576 | tf_op jit(solution)/shard_map/all_to_all | solution.py:489
  32.7 0.0 copy-done
  32.8 14.6 %all-gather.3.pick = s32[8,1,4096]{2,1,0:T(1,128)S(1)} all-gather(s32[1,1,4096]{2,1,0:T(1,128)S(1)} %bitcast.4), channel_id=3, replica_groups=mesh['region'=16,'dom'=8] {'dom'}, dimensions={0}, use_global_device_ids=true | all-gather | bytes 147456 | tf_op jit(solution)/shard_map/all_gather | solution.py:468
  47.4 0.0 all-gather.6.cloned.1.call-done.vol
  47.4 0.0 copy-start.1
  47.4 1.6 %copy-done.1 = f32[8,12,4096]{2,1,0:T(8,128)S(1)} copy-done((f32[8,12,4096]{2,1,0:T(8,128)S(1)}, f32[8,12,4096]{2,1,0:T(8,128)}, u32[]{:S(2)}) %copy-start.1) | copy-done | bytes 1572888
  49.0 1.0 shard_map.130.table
  50.0 0.0 all-to-all-done.recv
  50.0 8.2 %shard_map.132 = f32[128,8,128]{2,1,0:T(8,128)} custom-call(bf16[384,256]{1,0:T(8,128)(2,1)S(1)} %shard_map.130.table, f32[128,8,128]{2,1,0:T(8,128)S(1)} %all-to-all-done.recv), custom_call_target="tpu_custom_call" | custom-call | flops 10000000000 | bytes 1441792 | tf_op jit(solution)/shard_map/pallas_call | solution.py:427
  58.2 9.9 %all-to-all-start.1 = ((f32[128,8,128]{2,1,0:T(8,128)}), f32[128,8,128]{2,1,0:T(8,128)S(1)}, u32[]{:S(2)}, u32[]{:S(2)}) async-start(f32[128,8,128]{2,1,0:T(8,128)} %shard_map.132), calls=%async_computation.1 | async-start | bytes 1048576 | tf_op jit(solution)/shard_map/all_to_all | solution.py:513
  68.2 6.2 %shard_map.133 = (f32[16,16384]{1,0:T(8,128)}, f32[16,16384]{1,0:T(8,128)}, f32[4,16384]{1,0:T(4,128)}) custom-call(f32[12,16384]{1,0:T(8,128)} %disp.1, f32[3,16384]{1,0:T(4,128)} %normal.1, f32[4,16384]{1,0:T(4,128)} %gap.1, f32[4,16384]{1,0:T(4,128)} %weight.1, f32[8,16384]{1,0:T(8,128)} %proj.1), custom_call_target="tpu_custom_call" | custom-call | flops 1000000000 | bytes 4390912 | tf_op jit(solution)/shard_map/pallas_call | solution.py:427
  74.4 7.3 %all-to-all-done.1.refs_0_ = f32[128,8,128]{2,1,0:T(8,128)S(1)} async-done(((f32[128,8,128]{2,1,0:T(8,128)}), f32[128,8,128]{2,1,0:T(8,128)S(1)}, u32[]{:S(2)}, u32[]{:S(2)}) %all-to-all-start.1) | async-done | bytes 524320 | tf_op jit(solution)/shard_map/all_to_all | solution.py:513
  81.7 0.0 copy-start.2
  81.7 0.8 copy-done.2
  82.5 16.7 %shard_map.134 = (f32[4,16384]{1,0:T(4,128)}, f32[4,16384]{1,0:T(4,128)}, f32[128,8,128]{2,1,0:T(8,128)}) custom-call(f32[128,8,128]{2,1,0:T(8,128)} %copy-done.2, s32[8,256]{1,0:T(8,128)} %get-tuple-element.13.refs_1_, s32[1,16384]{1,0:T(1,128)} %get-tuple-element.14.refs_2_, f32[16,16384]{1,0:T(8,128)} %get-tuple-element.15.refs_3_, ...), custom_call_target="tpu_custom_call" | custom-call | flops 20000000000 | bytes 4530176 | tf_op jit(solution)/shard_map/pallas_call | solution.py:427
  99.2 18.4 %all_to_all.20.factor = f32[128,8,128]{2,1,0:T(8,128)S(1)} all-to-all(f32[128,8,128]{2,1,0:T(8,128)} %get-tuple-element.20), channel_id=1, replica_groups=mesh['region'=16,'dom'=8] {'region','dom'}, dimensions={0} | all-to-all | bytes 1048576 | tf_op jit(solution)/shard_map/all_to_all | solution.py:545
  117.6 7.4 %shard_map.135 = f32[8,12,512]{2,1,0:T(8,128)S(1)} custom-call(f32[128,8,128]{2,1,0:T(8,128)S(1)} %all-to-all-done.recv, f32[128,8,128]{2,1,0:T(8,128)S(1)} %all_to_all.20.factor), custom_call_target="tpu_custom_call" | custom-call | flops 10000000000 | bytes 1245184 | tf_op jit(solution)/shard_map/pallas_call | solution.py:427
  125.0 10.0 %all_to_all.21.moved = f32[8,12,512]{2,1,0:T(8,128)S(1)} all-to-all(f32[8,12,512]{2,1,0:T(8,128)S(1)} %shard_map.135), channel_id=1, replica_groups=mesh['region'=16,'dom'=8] {'dom'}, dimensions={0} | all-to-all | bytes 393216 | tf_op jit(solution)/shard_map/all_to_all | solution.py:555
  135.0 1.8 %shard_map.136 = f32[12,4096]{1,0:T(8,128)} custom-call(f32[8,12,512]{2,1,0:T(8,128)S(1)} %all_to_all.21.moved, s32[1,4096]{1,0:T(1,128)S(1)} %copy-done), custom_call_target="tpu_custom_call" | custom-call | flops 1000000000 | bytes 409600 | tf_op jit(solution)/shard_map/pallas_call | solution.py:427
Async XLA Ops:
  7.2 40.2 %all-gather.6.cloned.1.call-start = ((), (), s32[]{:S(2)}) async-start(), calls=%async_computation.4 | async-start | bytes 2359296 | tf_op jit(solution)/shard_map/all_gather | solution.py:467
  7.9 24.8 %copy-start = (s32[1,4096]{1,0:T(1,128)S(1)}, s32[1,4096]{1,0:T(1,128)}, u32[]{:S(2)}) copy-start(s32[1,4096]{1,0:T(1,128)} %pick.1) | copy-start | bytes 49156
  21.2 28.8 %all-to-all-start = ((f32[128,8,128]{2,1,0:T(8,128)}), f32[128,8,128]{2,1,0:T(8,128)S(1)}, u32[]{:S(2)}, u32[]{:S(2)}) async-start(f32[128,8,128]{2,1,0:T(8,128)} %get-tuple-element.12), calls=%async_computation | async-start | bytes 1048576 | tf_op jit(solution)/shard_map/all_to_all | solution.py:489
  47.4 1.6 %copy-start.1 = (f32[8,12,4096]{2,1,0:T(8,128)S(1)}, f32[8,12,4096]{2,1,0:T(8,128)}, u32[]{:S(2)}) copy-start(f32[8,12,4096]{2,1,0:T(8,128)} %all-gather.6.cloned.1.call-done.vol) | copy-start | bytes 4718596
  58.2 23.4 %all-to-all-start.1 = ((f32[128,8,128]{2,1,0:T(8,128)}), f32[128,8,128]{2,1,0:T(8,128)S(1)}, u32[]{:S(2)}, u32[]{:S(2)}) async-start(f32[128,8,128]{2,1,0:T(8,128)} %shard_map.132), calls=%async_computation.1 | async-start | bytes 1048576 | tf_op jit(solution)/shard_map/all_to_all | solution.py:513
  81.7 0.8 copy-start.2
Sparse Core Ops, SparseCore 0:
  9.7 32.1 all-gather.5

commit v4 on v2

--- a/solution.py
+++ b/solution.py
@@ -22,6 +22,7 @@
 F32 = jnp.float32
 LANE = 256
 
+UNROLL = 32
 NN = (((1,), (0,)), ((), ()))
 NT = (((1,), (1,)), ((), ()))
 
@@ -42,6 +43,16 @@
     return jnp.concatenate(
         [jnp.where(base == jnp.asarray(16 * g, BF), one, zero) for g in range(size // 16)], axis=0
     )
+
+
+def grab(table, index, apart):
+    half = table.shape[0] // 2
+    hot = onehot(index, LANE)
+    if apart:
+        first = lax.dot_general(table[0:half], hot, NN, preferred_element_type=F32)
+        return first + lax.dot_general(table[half:], hot, NN, preferred_element_type=F32)
+    found = lax.dot_general(table, hot, NN, preferred_element_type=F32)
+    return found[0:half] + found[half:]
 
 
 def spread(index, values, group, count):
@@ -65,19 +76,18 @@
 
 def pick_table(table, index, lows):
     n = index.shape[1]
-    grabbed = lax.dot_general(table, onehot(index % LANE, LANE), NN, preferred_element_type=F32)
-    total = 12 * lows
+    grabbed = grab(table, index % LANE, False)
     low = jnp.broadcast_to(index // LANE, (8, n))
     pair = low - sub_iota(8, n) // 4
     first = jnp.zeros((8, n), F32)
     for l in range(lows):
         at = 8 * l
-        value = grabbed[at : at + 8] + grabbed[total + at : total + at + 8]
+        value = grabbed[at : at + 8]
         first = jnp.where(low == l, value, first)
     second = jnp.zeros((8, n), F32)
     for l in range(lows // 2):
         at = 8 * lows + 8 * l
-        value = grabbed[at : at + 8] + grabbed[total + at : total + at + 8]
+        value = grabbed[at : at + 8]
         second = jnp.where(pair == 2 * l, value, second)
     return first, second[0:4] + second[4:8]
 
@@ -148,8 +158,8 @@
     number = lane + jnp.where(top, 0, 128)
 
     def window(i, _):
-        for u in range(8):
-            o = i * 8 + u
+        for u in range(UNROLL):
+            o = i * UNROLL + u
             start = offsets[0, o]
             block, shift = start // 128, start % 128
             joined = jnp.where(lane >= shift, ordered[block], ordered[block + 1])
@@ -159,7 +169,7 @@
             out[o] = joined
         return 0
 
-    lax.fori_loop(0, out.shape[0] // 8, window, 0)
+    lax.fori_loop(0, out.shape[0] // UNROLL, window, 0)
 
 
 def merge_windows(windows, offsets, merged, table):
@@ -167,8 +177,8 @@
     top = sub_iota(8, 128) < 4
 
     def window(i, carry):
-        for u in range(8):
-            o = i * 8 + u
+        for u in range(UNROLL):
+            o = i * UNROLL + u
             start, later = offsets[0, o], offsets[0, o + 1]
             block, shift = start // 128, start % 128
             value = pltpu.roll(windows[o], shift, 1)
@@ -183,7 +193,7 @@
             carry = jnp.where(ahead == 0, first, jnp.where(ahead == 1, second, two))
         return carry
 
-    lax.fori_loop(0, windows.shape[0] // 8, window, jnp.zeros((8, 128), F32))
+    lax.fori_loop(0, windows.shape[0] // UNROLL, window, jnp.zeros((8, 128), F32))
     half = table.shape[0] // 2
     left, right = [], []
     for g in range(half // 8):
@@ -195,7 +205,7 @@
     table[half:, :] = low
 
 
-def request_kernel(step, owner_hbm, slot_hbm, normal_hbm, out, place, offset, owner, slot, normal, total, named, ordered, scalars, sems):
+def request_kernel(step, owner_hbm, slot_hbm, normal_hbm, out, place, offset, owner, slot, normal, total, named, before, ordered, scalars, sems):
     copies = [
         pltpu.make_async_copy(a, b, sems.at[i])
         for i, (a, b) in enumerate(((owner_hbm, owner), (slot_hbm, slot), (normal_hbm, normal)))
@@ -208,40 +218,44 @@
     total[...] = jnp.zeros_like(total)
     copies[0].wait()
 
+    groups = owners // 16
+
+    def lookup(names, columns):
+        found = names[0:16] * columns[0:16]
+        for g in range(1, groups):
+            found = found + names[16 * g : 16 * g + 16] * columns[16 * g : 16 * g + 16]
+        return jnp.sum(found.astype(F32), axis=0, keepdims=True)
+
     def tally(i, sums):
         for u in range(step // 256):
             lanes = pl.ds(pl.multiple_of(i * step + u * 256, 256), 256)
-            value = onehot(owner[:, lanes], owners)
-            named[:, lanes] = value
-            sums = sums + value
+            names = onehot(owner[:, lanes], owners)
+            named[:, lanes] = names
+            before[:, lanes] = lookup(names, sums)
+            sums = sums + names
         return sums
 
     sums = lax.fori_loop(0, count // step, tally, jnp.zeros((owners, 256), BF))
     counts = lax.dot_general(sums, jnp.ones((256, 256), BF), NN, preferred_element_type=F32).astype(BF)
-    before = (sub_iota(owners, owners) > lane_iota(owners, owners)).astype(F32).astype(BF)
-    base = lax.dot_general(before, counts, NN, preferred_element_type=F32) - 1.0
+    lower = (sub_iota(owners, owners) > lane_iota(owners, owners)).astype(F32).astype(BF)
+    upper = (sub_iota(256, 256) < lane_iota(256, 256)).astype(F32).astype(BF)
+    base = lax.dot_general(lower, counts, NN, preferred_element_type=F32)
+    high, low = split(base + lax.dot_general(sums, upper, NN, preferred_element_type=F32))
     counts = lax.dot_general(jnp.ones((16, 256), BF), sums, NT, preferred_element_type=F32).astype(BF)
-    before = (sub_iota(owners, 2 * owners) < lane_iota(owners, 2 * owners)).astype(F32).astype(BF)
-    offset[...] = lax.dot_general(counts, before, NN, preferred_element_type=F32)[0:8].astype(jnp.int32)
+    upper = (sub_iota(owners, 2 * owners) < lane_iota(owners, 2 * owners)).astype(F32).astype(BF)
+    offset[...] = lax.dot_general(counts, upper, NN, preferred_element_type=F32)[0:8].astype(jnp.int32)
     save = pltpu.make_async_copy(offset, scalars, sems.at[3])
     save.start()
-    row, col = sub_iota(256, 512), lane_iota(256, 512)
-    upper = ((row <= col) | (col >= 256)).astype(F32).astype(BF)
-
-    def ranks(i, base):
-        chunks = []
+
+    def ranks(i, _):
         for u in range(step // 256):
-            chunks.append(named[:, pl.ds(pl.multiple_of(i * step + u * 256, 256), 256)])
-        sums = lax.dot_general(jnp.concatenate(chunks, axis=0), upper, NN, preferred_element_type=F32)
-        for u in range(step // 256):
-            part = sums[u * owners : (u + 1) * owners]
-            seen = chunks[u].astype(F32) * (part[:, 0:256] + base)
             lanes = pl.ds(pl.multiple_of(i * step + u * 256, 256), 256)
-            place[:, lanes] = jnp.sum(seen, axis=0, keepdims=True).astype(jnp.int32)
-            base = base + part[:, 256:512]
-        return base
-
-    lax.fori_loop(0, count // step, ranks, base)
+            names = named[:, lanes]
+            found = before[:, lanes] + lookup(names, high) + lookup(names, low)
+            place[:, lanes] = found.astype(jnp.int32)
+        return 0
+
+    lax.fori_loop(0, count // step, ranks, 0)
     copies[1].wait()
     copies[2].wait()
 
@@ -339,33 +353,32 @@
     return both[0:4] + both[4:8]
 
 
-def update_kernel(step, recv, *refs):
-    inputs, outputs, out = refs[0:7], refs[7:9], refs[9]
-    buffers, results = refs[10:17], refs[17:19]
-    table, total, ordered, sems = refs[19:23]
-    copies = [pltpu.make_async_copy(inputs[i], buffers[i], sems.at[i]) for i in range(7)]
+def update_kernel(step, *refs):
+    inputs, outputs, out = refs[0:8], refs[8:10], refs[10]
+    buffers, results = refs[11:19], refs[19:21]
+    table, total, ordered, sems = refs[21:25]
+    copies = [pltpu.make_async_copy(inputs[i], buffers[i], sems.at[i]) for i in range(8)]
     for copy in copies:
         copy.start()
-    offsets, place, toward, back, part, multiplier, active = buffers
+    recv, offsets, place, toward, back, part, multiplier, active = buffers
     gap_out, new_out = results
     count = place.shape[1]
     lows = count // LANE
-    half = lows * 4
     total[...] = jnp.zeros_like(total)
-    copies[0].wait()
+    for copy in copies[0:2]:
+        copy.wait()
     merge_windows(recv, offsets, ordered, table)
-    for copy in copies[1:]:
+    for copy in copies[2:]:
         copy.wait()
 
     def body(i, _):
         lanes = pl.ds(pl.multiple_of(i * step, step), step)
         places = place[:, lanes]
-        grabbed = lax.dot_general(table[...], onehot(places % LANE, LANE), NN, preferred_element_type=F32)
+        grabbed = grab(table[...], places % LANE, True)
         base = jnp.broadcast_to(places // LANE, (8, step)) - sub_iota(8, step) // 4
         along = jnp.zeros((8, step), F32)
         for g in range(lows // 2):
-            value = grabbed[8 * g : 8 * g + 8] + grabbed[half + 8 * g : half + 8 * g + 8]
-            along = jnp.where(base == 2 * g, value, along)
+            along = jnp.where(base == 2 * g, grabbed[8 * g : 8 * g + 8], along)
         mortar = combine(toward[:, lanes], along[0:4] + along[4:8])
         weighted = part[:, lanes] - mortar
         lagrange = jnp.where(active[:, lanes] == 1, jnp.maximum(multiplier[:, lanes] - weighted, 0.0), 0.0)
@@ -375,7 +388,7 @@
         return 0
 
     lax.fori_loop(0, count // step, body, 0)
-    saves = [pltpu.make_async_copy(results[i], outputs[i], sems.at[7 + i]) for i in range(2)]
+    saves = [pltpu.make_async_copy(results[i], outputs[i], sems.at[8 + i]) for i in range(2)]
     for save in saves:
         save.start()
     cut_windows(total, offsets, ordered, out, False)
@@ -420,7 +433,7 @@
         out[:, l * LANE : (l + 1) * LANE] = ordered
 
 
-def call(kernel, ins, outs, scratch, cycles, *args):
+def call(kernel, ins, outs, scratch, cycles, *args, mebibytes=48):
     size = sum(a.size * 4 for a in args) + sum(math.prod(o[0]) * 4 for o in outs)
     spaces = {"v": pltpu.VMEM, "h": pl.ANY}
     places = [pl.BlockSpec(memory_space=spaces[p]) for p in ins]
@@ -430,7 +443,7 @@
         in_specs=places[: len(args)],
         out_specs=places[len(args) :],
         scratch_shapes=scratch,
-        compiler_params=pltpu.CompilerParams(vmem_limit_bytes=56 * 2**20),
+        compiler_params=pltpu.CompilerParams(vmem_limit_bytes=mebibytes * 2**20),
         cost_estimate=pl.CostEstimate(flops=cycles, bytes_accessed=size, transcendentals=0),
     )(*args)
     return result[0] if len(outs) == 1 else result
@@ -463,10 +476,12 @@
     flat = (owners, 8, 128)
     everyone = ("region", "dom")
     whole, quad, wide = (1, count), (4, count), (16, count)
+
     table = pltpu.VMEM((24 * lows, LANE), BF)
-
+    picked = call(pick_kernel, "vvv", [((dom_count, 12, part), F32)], [table], 10**9, master_vol, surf_pick, mebibytes=60)
+    surf = exchange(picked, "dom")
     request, place, offset = call(
-        functools.partial(request_kernel, step),
+        functools.partial(request_kernel, 2 * step),
         "hhhvvv",
         [(flat, F32), (whole, jnp.int32), ((8, 2 * owners), jnp.int32)],
         [
@@ -475,6 +490,7 @@
             pltpu.VMEM((3, count), F32),
             pltpu.VMEM((8 * blocks, LANE), F32),
             pltpu.VMEM((owners, count), BF),
+            pltpu.VMEM(whole, F32),
             pltpu.VMEM((2 * blocks + 4, 8, 128), F32),
             pltpu.SMEM((8, 2 * owners), jnp.int32),
             pltpu.SemaphoreType.DMA((4,)),
@@ -483,11 +499,9 @@
         owner,
         pair_slot.reshape(1, count),
         slave_normal,
-    )
-    request, master_vol = lax.optimization_barrier((request, master_vol))
+        mebibytes=56,
+    )
     recv = exchange(request, everyone)
-    picked = call(pick_kernel, "vvv", [((dom_count, 12, part), F32)], [table], 10**9, master_vol, surf_pick)
-    surf = exchange(picked, "dom")
     toward, back, slave_part = call(
         functools.partial(local_kernel, 512),
         "v" * 8,
@@ -499,14 +513,16 @@
         gap_zero,
         quad_weight,
         proj_coord,
+        mebibytes=56,
     )
     along = call(functools.partial(along_kernel, 32), "vvv", [(flat, F32)], [table], 10**10, surf, recv)
     returned = exchange(along, everyone)
     weighted_gap, multiplier_new, terms = call(
         functools.partial(update_kernel, step),
-        "vhhhhhhhhhv",
+        "hhhhhhhhhhv",
         [(quad, F32), (quad, F32), (flat, F32)],
         [
+            pltpu.VMEM(flat, F32),
             pltpu.SMEM((8, 2 * owners), jnp.int32),
             pltpu.VMEM(whole, jnp.int32),
             pltpu.VMEM(wide, F32),
@@ -519,7 +535,7 @@
             pltpu.VMEM((8 * blocks, LANE), BF),
             pltpu.VMEM((8 * blocks, LANE), F32),
             pltpu.VMEM((2 * blocks + 4, 8, 128), F32),
-            pltpu.SemaphoreType.DMA((9,)),
+            pltpu.SemaphoreType.DMA((10,)),
         ],
         2 * 10**10,
         returned,
@@ -530,10 +546,11 @@
         slave_part,
         multiplier,
         active,
+        mebibytes=56,
     )
     factor = exchange(terms, everyone)
     forces = call(
-        functools.partial(force_kernel, 32),
+        functools.partial(force_kernel, 64),
         "vvv",
         [((dom_count, 12, part), F32)],
         [pltpu.VMEM((24 * lows, LANE), F32)],

time: 141 us -> 124 us (0.88)
  blocking collectives: 65.8 us -> 52.2 us
  Pallas kernels: 61.1 us -> 52 us
  starting transfers between devices: 4.59 us -> 10.6 us
    all_to_all x1 -> x0, blocking collectives: 12.7 us -> none  [on_device(): surf = exchange(picked, 'dom')]
    pallas_call x7, Pallas kernels: 61.1 us -> 52 us  [call(): pl.pallas_call(kernel, out_shape=[jax.ShapeDtypeStruct(*o) for o in outs]...]
    all_to_all x0 -> x1, starting transfers between devices: none -> 5.97 us  [on_device(): surf = exchange(picked, 'dom')]
    all_to_all x1, blocking collectives: 11.6 us -> 9.97 us  [on_device(): moved = exchange(forces, 'dom')]
    all_to_all x1, blocking collectives: 22.4 us -> 23.9 us  [on_device(): recv = exchange(request, everyone)]
  transfers between devices with their start and end apart: 1 -> 2, of which waited for: 1 -> 1; matrix products, arithmetic and copies ran while one was open for 0% -> 0% of each run, Pallas kernels for 4% -> 14%
where the time goes in v4:
time: 124 us
  blocking collectives  52.2 us (42%)
  Pallas kernels  52 us (42%)
  starting transfers between devices  10.6 us (9%)
  waiting for transfers between devices  7.33 us (6%)
    pallas_call x7, Pallas kernels, call(): pl.pallas_call(kernel, out_shape=[jax.ShapeDtypeStruct(*o) for o in outs]...  52 us
    all_to_all x1, blocking collectives, on_device(): recv = exchange(request, everyone)  23.9 us
    all_to_all x1, blocking collectives, on_device(): factor = exchange(terms, everyone)  18.4 us
    all_to_all x1, blocking collectives, on_device(): moved = exchange(forces, 'dom')  9.97 us
    all_to_all x1, waiting for transfers between devices, on_device(): returned = exchange(along, everyone)  7.32 us
    all_to_all x1, starting transfers between devices, on_device(): surf = exchange(picked, 'dom')  5.97 us
    all_to_all x1, starting transfers between devices, on_device(): returned = exchange(along, everyone)  4.59 us
  transfers between devices with their start and end apart: 2, of which 1 were waited for; matrix products, arithmetic and copies ran while one was open for 0% of the time, Pallas kernels for 14%

profile of v4, /device:TPU:1, one launch (start us, length us, event | category | flops | bytes accessed | tf_op | source)
XLA Modules:
  0.0 123.6 jit_solution(2336015024570271329)
XLA Ops:
  0.6 2.7 %shard_map.130 = f32[8,12,512]{2,1,0:T(8,128)} custom-call(f32[12,4096]{1,0:T(8,128)} %vol.1, s32[1,4096]{1,0:T(1,128)} %pick.3), custom_call_target="tpu_custom_call" | custom-call | flops 1000000000 | bytes 409600 | tf_op jit(solution)/shard_map/pallas_call | solution.py:440
  3.3 6.0 %all-to-all-start = ((f32[8,12,512]{2,1,0:T(8,128)}), f32[8,12,512]{2,1,0:T(8,128)S(1)}, u32[]{:S(2)}, u32[]{:S(2)}) async-start(f32[8,12,512]{2,1,0:T(8,128)} %shard_map.130), calls=%async_computation | async-start | bytes 524288 | tf_op jit(solution)/shard_map/all_to_all | solution.py:482
  9.3 10.9 %shard_map.131 = (f32[128,8,128]{2,1,0:T(8,128)}, s32[1,16384]{1,0:T(1,128)}, s32[8,256]{1,0:T(8,128)}) custom-call(s32[1,16384]{1,0:T(1,128)} %bitcast.2, s32[1,16384]{1,0:T(1,128)} %bitcast.3, f32[3,16384]{1,0:T(4,128)} %normal.1), custom_call_target="tpu_custom_call" | custom-call | flops 10000000000 | bytes 925696 | tf_op jit(solution)/shard_map/pallas_call | solution.py:440
  20.2 0.0 all-to-all-done.surf
  20.2 23.9 %all_to_all.25.recv = f32[128,8,128]{2,1,0:T(8,128)S(1)} all-to-all(f32[128,8,128]{2,1,0:T(8,128)} %get-tuple-element.12), channel_id=1, replica_groups=mesh['region'=16,'dom'=8] {'region','dom'}, dimensions={0} | all-to-all | bytes 1048576 | tf_op jit(solution)/shard_map/all_to_all | solution.py:504
  44.1 8.2 %shard_map.132 = f32[128,8,128]{2,1,0:T(8,128)} custom-call(f32[8,12,512]{2,1,0:T(8,128)S(1)} %all-to-all-done.surf, f32[128,8,128]{2,1,0:T(8,128)S(1)} %all_to_all.25.recv), custom_call_target="tpu_custom_call" | custom-call | flops 10000000000 | bytes 1245184 | tf_op jit(solution)/shard_map/pallas_call | solution.py:440
  52.3 4.6 %all-to-all-start.2 = ((f32[128,8,128]{2,1,0:T(8,128)}), f32[128,8,128]{2,1,0:T(8,128)S(1)}, u32[]{:S(2)}, u32[]{:S(2)}) async-start(f32[128,8,128]{2,1,0:T(8,128)} %shard_map.132), calls=%async_computation.2 | async-start | bytes 1048576 | tf_op jit(solution)/shard_map/all_to_all | solution.py:519
  56.9 6.2 %shard_map.133 = (f32[16,16384]{1,0:T(8,128)}, f32[16,16384]{1,0:T(8,128)}, f32[4,16384]{1,0:T(4,128)}) custom-call(f32[12,16384]{1,0:T(8,128)} %disp.1, f32[3,16384]{1,0:T(4,128)} %normal.1, f32[4,16384]{1,0:T(4,128)} %gap.1, f32[4,16384]{1,0:T(4,128)} %weight.1, f32[8,16384]{1,0:T(8,128)} %proj.1), custom_call_target="tpu_custom_call" | custom-call | flops 1000000000 | bytes 4390912 | tf_op jit(solution)/shard_map/pallas_call | solution.py:440
  63.1 7.3 %all-to-all-done.2.refs_0_ = f32[128,8,128]{2,1,0:T(8,128)S(1)} async-done(((f32[128,8,128]{2,1,0:T(8,128)}), f32[128,8,128]{2,1,0:T(8,128)S(1)}, u32[]{:S(2)}, u32[]{:S(2)}) %all-to-all-start.2) | async-done | bytes 524320 | tf_op jit(solution)/shard_map/all_to_all | solution.py:519
  70.4 0.0 copy-start.1
  70.4 0.8 copy-done.1
  71.2 15.3 %shard_map.134 = (f32[4,16384]{1,0:T(4,128)}, f32[4,16384]{1,0:T(4,128)}, f32[128,8,128]{2,1,0:T(8,128)}) custom-call(f32[128,8,128]{2,1,0:T(8,128)} %copy-done.1, s32[8,256]{1,0:T(8,128)} %get-tuple-element.13.refs_1_, s32[1,16384]{1,0:T(1,128)} %get-tuple-element.14.refs_2_, f32[16,16384]{1,0:T(8,128)} %get-tuple-element.15.refs_3_, ...), custom_call_target="tpu_custom_call" | custom-call | flops 20000000000 | bytes 4530176 | tf_op jit(solution)/shard_map/pallas_call | solution.py:440
  86.5 18.4 %all_to_all.26.factor = f32[128,8,128]{2,1,0:T(8,128)S(1)} all-to-all(f32[128,8,128]{2,1,0:T(8,128)} %get-tuple-element.20), channel_id=1, replica_groups=mesh['region'=16,'dom'=8] {'region','dom'}, dimensions={0} | all-to-all | bytes 1048576 | tf_op jit(solution)/shard_map/all_to_all | solution.py:551
  104.9 7.0 %shard_map.135 = f32[8,12,512]{2,1,0:T(8,128)S(1)} custom-call(f32[128,8,128]{2,1,0:T(8,128)S(1)} %all_to_all.25.recv, f32[128,8,128]{2,1,0:T(8,128)S(1)} %all_to_all.26.factor), custom_call_target="tpu_custom_call" | custom-call | flops 10000000000 | bytes 1245184 | tf_op jit(solution)/shard_map/pallas_call | solution.py:440
  111.8 0.0 copy-start
  111.9 10.0 %all_to_all.27.moved = f32[8,12,512]{2,1,0:T(8,128)S(1)} all-to-all(f32[8,12,512]{2,1,0:T(8,128)S(1)} %shard_map.135), channel_id=1, replica_groups=mesh['region'=16,'dom'=8] {'dom'}, dimensions={0} | all-to-all | bytes 393216 | tf_op jit(solution)/shard_map/all_to_all | solution.py:561
  121.8 0.0 copy-done
  121.8 1.8 %shard_map.136 = f32[12,4096]{1,0:T(8,128)} custom-call(f32[8,12,512]{2,1,0:T(8,128)S(1)} %all_to_all.27.moved, s32[1,4096]{1,0:T(1,128)S(1)} %copy-done), custom_call_target="tpu_custom_call" | custom-call | flops 1000000000 | bytes 409600 | tf_op jit(solution)/shard_map/pallas_call | solution.py:440
Async XLA Ops:
  3.3 16.9 %all-to-all-start = ((f32[8,12,512]{2,1,0:T(8,128)}), f32[8,12,512]{2,1,0:T(8,128)S(1)}, u32[]{:S(2)}, u32[]{:S(2)}) async-start(f32[8,12,512]{2,1,0:T(8,128)} %shard_map.130), calls=%async_computation | async-start | bytes 524288 | tf_op jit(solution)/shard_map/all_to_all | solution.py:482
  52.3 18.1 %all-to-all-start.2 = ((f32[128,8,128]{2,1,0:T(8,128)}), f32[128,8,128]{2,1,0:T(8,128)S(1)}, u32[]{:S(2)}, u32[]{:S(2)}) async-start(f32[128,8,128]{2,1,0:T(8,128)} %shard_map.132), calls=%async_computation.2 | async-start | bytes 1048576 | tf_op jit(solution)/shard_map/all_to_all | solution.py:519
  70.4 0.8 copy-start.1
  111.8 10.0 %copy-start = (s32[1,4096]{1,0:T(1,128)S(1)}, s32[1,4096]{1,0:T(1,128)}, u32[]{:S(2)}) copy-start(s32[1,4096]{1,0:T(1,128)} %pick.3) | copy-start | bytes 49156

commit v5 on v4

--- a/solution.py
+++ b/solution.py
@@ -132,17 +132,21 @@
 
 
 def sort_terms(values, place, lows):
-    high, low = split(jnp.concatenate([values] * 4, axis=0))
-    first, second = spread(place // LANE, [high, low], 4, lows)
-    stacked = jnp.concatenate(first + second, axis=0)
+    pieces = []
+    for value in values:
+        pieces += split(jnp.concatenate([value] * 4, axis=0))
+    stacked = jnp.concatenate(sum(spread(place // LANE, pieces, 4, lows), []), axis=0)
     return lax.dot_general(stacked, onehot(place % LANE, LANE), NT, preferred_element_type=F32)
 
 
-def cut_windows(total, offsets, ordered, out, masked):
-    half = total.shape[0] // 2
-    sums = total[0:half, :] + total[half:, :]
+def sorted_sums(total, lows):
+    rows = 4 * lows
+    return [total[i : i + rows] + total[i + rows : i + 2 * rows] for i in range(0, total.shape[0], 2 * rows)]
+
+
+def cut_windows(sums, offsets, ordered, out, masked):
     top = sub_iota(8, 128) < 4
-    groups = half // 8
+    groups = sums.shape[0] // 8
     left = [sums[8 * g : 8 * g + 8, 0:128] for g in range(groups)]
     right = [sums[8 * g : 8 * g + 8, 128:256] for g in range(groups)]
     turned_left = [pltpu.roll(v, 4, 0) for v in left] + [jnp.zeros((8, 128), F32)]
@@ -172,7 +176,7 @@
     lax.fori_loop(0, out.shape[0] // UNROLL, window, 0)
 
 
-def merge_windows(windows, offsets, merged, table):
+def merge_windows(windows, offsets, merged, lows):
     lane = lane_iota(8, 128)
     top = sub_iota(8, 128) < 4
 
@@ -194,15 +198,11 @@
         return carry
 
     lax.fori_loop(0, windows.shape[0] // UNROLL, window, jnp.zeros((8, 128), F32))
-    half = table.shape[0] // 2
     left, right = [], []
-    for g in range(half // 8):
+    for g in range(lows // 2):
         left.append(jnp.where(top, merged[4 * g], merged[4 * g + 2]))
         right.append(jnp.where(top, merged[4 * g + 1], merged[4 * g + 3]))
-    both = jnp.concatenate([jnp.concatenate(left, axis=0), jnp.concatenate(right, axis=0)], axis=1)
-    high, low = split(both)
-    table[0:half, :] = high
-    table[half:, :] = low
+    return jnp.concatenate([jnp.concatenate(left, axis=0), jnp.concatenate(right, axis=0)], axis=1)
 
 
 def request_kernel(step, owner_hbm, slot_hbm, normal_hbm, out, place, offset, owner, slot, normal, total, named, before, ordered, scalars, sems):
@@ -262,12 +262,12 @@
     def slots(i, _):
         lanes = pl.ds(pl.multiple_of(i * step, step), step)
         values = jnp.concatenate([slot[:, lanes].astype(F32), normal[:, lanes]], axis=0)
-        total[...] += sort_terms(values, place[:, lanes], lows)
+        total[...] += sort_terms([values], place[:, lanes], lows)
         return 0
 
     lax.fori_loop(0, count // step, slots, 0)
     save.wait()
-    cut_windows(total, scalars, ordered, out, True)
+    cut_windows(sorted_sums(total, lows)[0], scalars, ordered, out, True)
 
 
 def along_kernel(group, surf, recv, out, table):
@@ -289,111 +289,123 @@
     lax.fori_loop(0, recv.shape[0] // group, step, 0)
 
 
-def signs(xs, inner):
-    sub = sub_iota(8, 1)
-
-    def column(number):
-        value = jnp.full((8, 1), xs[3], F32)
-        for c in range(3):
-            value = jnp.where(number == c, xs[c], value)
-        return value
-
-    return [column(sub % 4)] * 2 if inner else [column(sub // 4), column(sub // 4 + 2)]
-
-
-def local_kernel(step, disp, normal, gap, weight, proj, toward, back, part):
-    count = disp.shape[1]
-    sub4 = sub_iota(4, 1)
-
-    def column(xs):
-        value = jnp.full((4, 1), xs[3], F32)
-        for a in range(3):
-            value = jnp.where(sub4 == a, xs[a], value)
-        return value
+def by_node(values, number):
+    result = jnp.full(number.shape, values[3], F32)
+    for c in range(3):
+        result = jnp.where(number == c, values[c], result)
+    return result
+
+
+def turned(values, by):
+    if by % 4 == 0:
+        return values
+    by = by % 4
+    row = lax.broadcasted_iota(jnp.int32, values.shape, 1) % 4
+    return jnp.where(row < 4 - by, pltpu.roll(values, 8 - by, 1), pltpu.roll(values, 4 - by, 1))
+
+
+def sort_kernel(step, place, proj, out, total):
+    lows = place.shape[1] // LANE
+    total[...] = jnp.zeros_like(total)
 
     def body(i, _):
         lanes = pl.ds(pl.multiple_of(i * step, step), step)
-        p, w, d, n, g = proj[:, lanes], weight[:, lanes], disp[:, lanes], normal[:, lanes], gap[:, lanes]
-        for inner, out in ((False, toward), (True, back)):
-            node_x, node_y = signs(node_xs, inner), signs(node_ys, inner)
-            sums = [None, None]
-            for q in range(4):
-                table = signs([slave_table[a][q] * 0.25 for a in range(4)], not inner)
-                first = jnp.broadcast_to(p[2 * q : 2 * q + 1], (8, step))
-                second = jnp.broadcast_to(p[2 * q + 1 : 2 * q + 2], (8, step))
-                along = jnp.broadcast_to(w[q : q + 1], (8, step))
-                for h in range(2):
-                    term = (1.0 + node_x[h] * first) * (1.0 + node_y[h] * second) * (along * table[h])
-                    sums[h] = term if q == 0 else sums[h] + term
-            out[0:8, lanes] = sums[0]
-            out[8:16, lanes] = sums[1]
-        total = g
+        p = proj[:, lanes]
+        values = [jnp.concatenate([p[2 * q + k : 2 * q + k + 1] for q in range(4)], axis=0) for k in range(2)]
+        total[...] += sort_terms(values, place[:, lanes], lows)
+        return 0
+
+    lax.fori_loop(0, place.shape[1] // step, body, 0)
+    for k, value in enumerate(sorted_sums(total, lows)):
+        out[k] = value
+
+
+def local_kernel(step, place, disp, normal, gap, weight, multiplier, active, proj, part, level, factors, total):
+    count = place.shape[1]
+    lows = count // LANE
+    sub4 = sub_iota(4, 1)
+    total[...] = jnp.zeros_like(total)
+
+    def body(i, _):
+        lanes = pl.ds(pl.multiple_of(i * step, step), step)
+        w, d, n, g = weight[:, lanes], disp[:, lanes], normal[:, lanes], gap[:, lanes]
+        points = g
         for b in range(4):
             along = n[0:1] * d[3 * b : 3 * b + 1] + n[1:2] * d[3 * b + 1 : 3 * b + 2] + n[2:3] * d[3 * b + 2 : 3 * b + 3]
-            total = total + column(slave_table[b]) * along
-        points = w * total
-        result = column([slave_table[a][0] for a in range(4)]) * points[0:1]
+            points = points + by_node(slave_table[b], sub4) * along
+        points = w * points
+        result = by_node([slave_table[a][0] for a in range(4)], sub4) * points[0:1]
         for q in range(1, 4):
-            result = result + column([slave_table[a][q] for a in range(4)]) * points[q : q + 1]
+            result = result + by_node([slave_table[a][q] for a in range(4)], sub4) * points[q : q + 1]
         part[:, lanes] = result
+        start = jnp.where(active[:, lanes] == 1, multiplier[:, lanes] - result, -1e30)
+        total[...] += sort_terms([w, start], place[:, lanes], lows)
         return 0
 
     lax.fori_loop(0, count // step, body, 0)
-
-
-def doubled(values):
-    n = values.shape[1]
-    rows = [jnp.broadcast_to(values[c : c + 1], (4, n)) for c in range(4)]
-    return jnp.concatenate(rows[0:2], axis=0), jnp.concatenate(rows[2:4], axis=0)
-
-
-def combine(factors, values):
-    one, two = doubled(values)
-    both = factors[0:8] * one + factors[8:16] * two
-    return both[0:4] + both[4:8]
-
-
-def update_kernel(step, *refs):
-    inputs, outputs, out = refs[0:8], refs[8:10], refs[10]
-    buffers, results = refs[11:19], refs[19:21]
-    table, total, ordered, sems = refs[21:25]
-    copies = [pltpu.make_async_copy(inputs[i], buffers[i], sems.at[i]) for i in range(8)]
+    w, start = sorted_sums(total, lows)
+    level[...] = start
+    first, second, w = [v.reshape(-1, 8, LANE) for v in (proj[0], proj[1], w)]
+    row = lax.broadcasted_iota(jnp.int32, (1, 8, 1), 1) % 4
+    sums = [None] * 4
+    for e in range(4):
+        x, y = turned(first, e), turned(second, e)
+        scaled = turned(w, e) * by_node([slave_table[a][(a + e) % 4] * 0.25 for a in range(4)], row)
+        for d in range(4):
+            node = (row + d) % 4
+            term = (1.0 + by_node(node_xs, node) * x) * (1.0 + by_node(node_ys, node) * y) * scaled
+            sums[d] = term if e == 0 else sums[d] + term
+    for d in range(4):
+        factors[d] = sums[d].reshape(-1, LANE)
+
+
+def update_kernel(*refs):
+    inputs, out, mortar_out = refs[0:4], refs[4], refs[5]
+    recv, offsets, level, factors = refs[6:10]
+    ordered, sems = refs[10:12]
+    copies = [pltpu.make_async_copy(inputs[i], refs[6 + i], sems.at[i]) for i in range(4)]
     for copy in copies:
         copy.start()
-    recv, offsets, place, toward, back, part, multiplier, active = buffers
-    gap_out, new_out = results
+    for copy in copies[0:2]:
+        copy.wait()
+    lows = level.shape[0] // 4
+    along = merge_windows(recv, offsets, ordered, lows).reshape(-1, 8, LANE)
+    for copy in copies[2:]:
+        copy.wait()
+    parts = [factors[d].reshape(-1, 8, LANE) for d in range(4)]
+    mortar = parts[0] * along
+    for d in range(1, 4):
+        mortar = mortar + parts[d] * turned(along, d)
+    mortar_out[...] = mortar.reshape(-1, LANE)
+    lagrange = jnp.maximum(level[...].reshape(-1, 8, LANE) + mortar, 0.0)
+    terms = parts[0] * lagrange
+    for d in range(1, 4):
+        terms = terms + turned(parts[d] * lagrange, 4 - d)
+    cut_windows(terms.reshape(-1, LANE), offsets, ordered, out, False)
+
+
+def restore_kernel(step, mortar, place, part, multiplier, active, gap_out, new_out, table):
     count = place.shape[1]
     lows = count // LANE
-    total[...] = jnp.zeros_like(total)
-    for copy in copies[0:2]:
-        copy.wait()
-    merge_windows(recv, offsets, ordered, table)
-    for copy in copies[2:]:
-        copy.wait()
+    half = table.shape[0] // 2
+    high, low = split(mortar[...])
+    table[0:half, :] = high
+    table[half:, :] = low
 
     def body(i, _):
         lanes = pl.ds(pl.multiple_of(i * step, step), step)
         places = place[:, lanes]
         grabbed = grab(table[...], places % LANE, True)
         base = jnp.broadcast_to(places // LANE, (8, step)) - sub_iota(8, step) // 4
-        along = jnp.zeros((8, step), F32)
+        found = jnp.zeros((8, step), F32)
         for g in range(lows // 2):
-            along = jnp.where(base == 2 * g, grabbed[8 * g : 8 * g + 8], along)
-        mortar = combine(toward[:, lanes], along[0:4] + along[4:8])
-        weighted = part[:, lanes] - mortar
-        lagrange = jnp.where(active[:, lanes] == 1, jnp.maximum(multiplier[:, lanes] - weighted, 0.0), 0.0)
+            found = jnp.where(base == 2 * g, grabbed[8 * g : 8 * g + 8], found)
+        weighted = part[:, lanes] - (found[0:4] + found[4:8])
         gap_out[:, lanes] = weighted
-        new_out[:, lanes] = lagrange
-        total[...] += sort_terms(combine(back[:, lanes], lagrange), places, lows)
+        new_out[:, lanes] = jnp.where(active[:, lanes] == 1, jnp.maximum(multiplier[:, lanes] - weighted, 0.0), 0.0)
         return 0
 
     lax.fori_loop(0, count // step, body, 0)
-    saves = [pltpu.make_async_copy(results[i], outputs[i], sems.at[8 + i]) for i in range(2)]
-    for save in saves:
-        save.start()
-    cut_windows(total, offsets, ordered, out, False)
-    for save in saves:
-        save.wait()
 
 
 def force_kernel(group, recv, factor, out, total):
@@ -475,7 +487,7 @@
     owner = pair_owner.reshape(1, count)
     flat = (owners, 8, 128)
     everyone = ("region", "dom")
-    whole, quad, wide = (1, count), (4, count), (16, count)
+    whole, quad = (1, count), (4, count)
 
     table = pltpu.VMEM((24 * lows, LANE), BF)
     picked = call(pick_kernel, "vvv", [((dom_count, 12, part), F32)], [table], 10**9, master_vol, surf_pick, mebibytes=60)
@@ -502,53 +514,70 @@
         mebibytes=56,
     )
     recv = exchange(request, everyone)
-    toward, back, slave_part = call(
-        functools.partial(local_kernel, 512),
-        "v" * 8,
-        [(wide, F32), (wide, F32), (quad, F32)],
-        [],
-        10**9,
+    sorted_proj = call(
+        functools.partial(sort_kernel, step),
+        "vvv",
+        [((2, 4 * blocks, LANE), F32)],
+        [pltpu.VMEM((16 * blocks, LANE), F32)],
+        10**10,
+        place,
+        proj_coord,
+        mebibytes=56,
+    )
+    surf, sorted_proj = lax.optimization_barrier((surf, sorted_proj))
+    along = call(functools.partial(along_kernel, 32), "vvv", [(flat, F32)], [table], 10**10, surf, recv)
+    returned = exchange(along, everyone)
+    along, sorted_proj = lax.optimization_barrier((along, sorted_proj))
+    slave_part, level, factors = call(
+        functools.partial(local_kernel, step),
+        "v" * 11,
+        [(quad, F32), ((4 * blocks, LANE), F32), ((4, 4 * blocks, LANE), F32)],
+        [pltpu.VMEM((16 * blocks, LANE), F32)],
+        10**10,
+        place,
         slave_disp,
         slave_normal,
         gap_zero,
         quad_weight,
-        proj_coord,
+        multiplier,
+        active,
+        sorted_proj,
         mebibytes=56,
     )
-    along = call(functools.partial(along_kernel, 32), "vvv", [(flat, F32)], [table], 10**10, surf, recv)
-    returned = exchange(along, everyone)
-    weighted_gap, multiplier_new, terms = call(
-        functools.partial(update_kernel, step),
-        "hhhhhhhhhhv",
-        [(quad, F32), (quad, F32), (flat, F32)],
+    terms, mortar = call(
+        update_kernel,
+        "hhhhvv",
+        [(flat, F32), ((4 * blocks, LANE), F32)],
         [
             pltpu.VMEM(flat, F32),
             pltpu.SMEM((8, 2 * owners), jnp.int32),
-            pltpu.VMEM(whole, jnp.int32),
-            pltpu.VMEM(wide, F32),
-            pltpu.VMEM(wide, F32),
-            pltpu.VMEM(quad, F32),
-            pltpu.VMEM(quad, F32),
-            pltpu.VMEM(quad, jnp.int32),
-            pltpu.VMEM(quad, F32),
-            pltpu.VMEM(quad, F32),
-            pltpu.VMEM((8 * blocks, LANE), BF),
-            pltpu.VMEM((8 * blocks, LANE), F32),
+            pltpu.VMEM((4 * blocks, LANE), F32),
+            pltpu.VMEM((4, 4 * blocks, LANE), F32),
             pltpu.VMEM((2 * blocks + 4, 8, 128), F32),
-            pltpu.SemaphoreType.DMA((10,)),
+            pltpu.SemaphoreType.DMA((4,)),
         ],
-        2 * 10**10,
+        10**9,
         returned,
         offset,
+        level,
+        factors,
+        mebibytes=56,
+    )
+    factor = exchange(terms, everyone)
+    weighted_gap, multiplier_new = call(
+        functools.partial(restore_kernel, step),
+        "v" * 7,
+        [(quad, F32), (quad, F32)],
+        [pltpu.VMEM((8 * blocks, LANE), BF)],
+        10**10,
+        mortar,
         place,
-        toward,
-        back,
         slave_part,
         multiplier,
         active,
         mebibytes=56,
     )
-    factor = exchange(terms, everyone)
+    recv, weighted_gap = lax.optimization_barrier((recv, weighted_gap))
     forces = call(
         functools.partial(force_kernel, 64),
         "vvv",

time: 124 us -> 123 us (level)
  blocking collectives: 52.2 us -> 9.99 us
  starting transfers between devices: 10.6 us -> 33.9 us
  Pallas kernels: 52 us -> 68.8 us
    all_to_all x2 -> x0, blocking collectives: 42.2 us -> none  [the longest x1 23.9 us: on_device(): recv = exchange(request, everyone)]
    all_to_all x0 -> x2, starting transfers between devices: none -> 20.1 us  [the longest x1 10.3 us: on_device(): recv = exchange(request, everyone)]
    pallas_call x7 -> x9, Pallas kernels: 52 us -> 68.8 us  [call(): pl.pallas_call(kernel, out_shape=[jax.ShapeDtypeStruct(*o) for o in outs]...]
    all_to_all x0 -> x2, waiting for transfers between devices: none -> 8.25 us  [the longest x1 6.25 us: on_device(): factor = exchange(terms, everyone)]
    all_to_all x1, waiting for transfers between devices: 7.32 us -> 0.01 us  [on_device(): returned = exchange(along, everyone)]
    all_to_all x1, starting transfers between devices: 4.59 us -> 7.77 us  [on_device(): returned = exchange(along, everyone)]
  transfers between devices with their start and end apart: 2 -> 4, of which waited for: 1 -> 2; matrix products, arithmetic and copies ran while one was open for 0% -> 0% of each run, Pallas kernels for 14% -> 35%
where the time goes in v5:
time: 123 us; the launch traced here: 122 us
  Pallas kernels  68.8 us (56%)
  starting transfers between devices  33.9 us (28%)
  blocking collectives  9.99 us (8%)
  waiting for transfers between devices  8.26 us (7%)
    pallas_call x9, Pallas kernels, call(): pl.pallas_call(kernel, out_shape=[jax.ShapeDtypeStruct(*o) for o in outs]...  68.8 us
    all_to_all x1, starting transfers between devices, on_device(): recv = exchange(request, everyone)  10.3 us
    all_to_all x1, blocking collectives, on_device(): moved = exchange(forces, 'dom')  9.99 us
    all_to_all x1, starting transfers between devices, on_device(): factor = exchange(terms, everyone)  9.77 us
    all_to_all x1, starting transfers between devices, on_device(): returned = exchange(along, everyone)  7.77 us
    all_to_all x1, waiting for transfers between devices, on_device(): factor = exchange(terms, everyone)  6.25 us
    all_to_all x1, starting transfers between devices, on_device(): surf = exchange(picked, 'dom')  5.97 us
  transfers between devices with their start and end apart: 4, of which 2 were waited for; matrix products, arithmetic and copies ran while one was open for 0% of the time, Pallas kernels for 35%

profile of v5, /device:TPU:1, one launch (start us, length us, event | category | flops | bytes accessed | tf_op | source)
XLA Modules:
  0.0 122.4 jit_solution(13325490706365497377)
XLA Ops:
  0.6 2.7 %shard_map.131 = f32[8,12,512]{2,1,0:T(8,128)} custom-call(f32[12,4096]{1,0:T(8,128)} %vol.1, s32[1,4096]{1,0:T(1,128)} %pick.3), custom_call_target="tpu_custom_call" | custom-call | flops 1000000000 | bytes 409600 | tf_op jit(solution)/shard_map/pallas_call | solution.py:452
  3.3 6.0 %all-to-all-start.1 = ((f32[8,12,512]{2,1,0:T(8,128)}), f32[8,12,512]{2,1,0:T(8,128)S(1)}, u32[]{:S(2)}, u32[]{:S(2)}) async-start(f32[8,12,512]{2,1,0:T(8,128)} %shard_map.131), calls=%async_computation.1 | async-start | bytes 524288 | tf_op jit(solution)/shard_map/all_to_all | solution.py:494
  9.3 10.9 %shard_map.130 = (f32[128,8,128]{2,1,0:T(8,128)}, s32[1,16384]{1,0:T(1,128)}, s32[8,256]{1,0:T(8,128)}) custom-call(s32[1,16384]{1,0:T(1,128)} %bitcast.2, s32[1,16384]{1,0:T(1,128)} %bitcast.3, f32[3,16384]{1,0:T(4,128)} %normal.1), custom_call_target="tpu_custom_call" | custom-call | flops 10000000000 | bytes 925696 | tf_op jit(solution)/shard_map/pallas_call | solution.py:452
  20.2 0.0 all-to-all-done.1.surf
  20.2 10.3 %all-to-all-start = ((f32[128,8,128]{2,1,0:T(8,128)}), f32[128,8,128]{2,1,0:T(8,128)S(1)}, u32[]{:S(2)}, u32[]{:S(2)}) async-start(f32[128,8,128]{2,1,0:T(8,128)} %get-tuple-element.18), calls=%async_computation | async-start | bytes 1048576 | tf_op jit(solution)/shard_map/all_to_all | solution.py:516
  30.5 11.5 %shard_map.132.proj = f32[2,256,256]{2,1,0:T(8,128)} custom-call(s32[1,16384]{1,0:T(1,128)} %get-tuple-element.19.place, f32[8,16384]{1,0:T(8,128)} %proj.1), custom_call_target="tpu_custom_call" | custom-call | flops 10000000000 | bytes 1114112 | tf_op jit(solution)/shard_map/pallas_call | solution.py:452
  42.0 2.0 %all-to-all-done.recv = f32[128,8,128]{2,1,0:T(8,128)S(1)} async-done(((f32[128,8,128]{2,1,0:T(8,128)}), f32[128,8,128]{2,1,0:T(8,128)S(1)}, u32[]{:S(2)}, u32[]{:S(2)}) %all-to-all-start) | async-done | bytes 524320 | tf_op jit(solution)/shard_map/all_to_all | solution.py:516
  44.0 8.2 %shard_map.133 = f32[128,8,128]{2,1,0:T(8,128)} custom-call(f32[8,12,512]{2,1,0:T(8,128)S(1)} %all-to-all-done.1.surf, f32[128,8,128]{2,1,0:T(8,128)S(1)} %all-to-all-done.recv), custom_call_target="tpu_custom_call" | custom-call | flops 10000000000 | bytes 1245184 | tf_op jit(solution)/shard_map/pallas_call | solution.py:452
  52.3 7.8 %all-to-all-start.2 = ((f32[128,8,128]{2,1,0:T(8,128)}), f32[128,8,128]{2,1,0:T(8,128)S(1)}, u32[]{:S(2)}, u32[]{:S(2)}) async-start(f32[128,8,128]{2,1,0:T(8,128)} %shard_map.133), calls=%async_computation.2 | async-start | bytes 1048576 | tf_op jit(solution)/shard_map/all_to_all | solution.py:529
  60.0 13.6 %shard_map.134 = (f32[4,16384]{1,0:T(4,128)}, f32[256,256]{1,0:T(8,128)}, f32[4,256,256]{2,1,0:T(8,128)}) custom-call(s32[1,16384]{1,0:T(1,128)} %get-tuple-element.19.place, f32[12,16384]{1,0:T(8,128)} %disp.1, f32[3,16384]{1,0:T(4,128)} %normal.1, f32[4,16384]{1,0:T(4,128)} %gap.1, f32[4,16384]{1,0:T(4,128)} %weight.1, f32[4,16384]{1,0:T(4,128)} %multiplier.3, ...), custom_call_target="tpu_custom_call" | custom-call | flops 10000000000 | bytes 4194304 | tf_op jit(solution)/shard_map/pallas_call | solution.py:452
  73.7 0.0 all-to-all-done.2.refs_0_
  73.7 0.0 copy-start.1
  73.7 0.8 copy-done.1
  74.5 5.9 %shard_map.135 = (f32[128,8,128]{2,1,0:T(8,128)}, f32[256,256]{1,0:T(8,128)}) custom-call(f32[128,8,128]{2,1,0:T(8,128)} %copy-done.1, s32[8,256]{1,0:T(8,128)} %get-tuple-element.21.refs_1_, f32[256,256]{1,0:T(8,128)} %get-tuple-element.24.refs_2_, f32[4,256,256]{2,1,0:T(8,128)} %get-tuple-element.25.refs_3_), custom_call_target="tpu_custom_call" | custom-call | flops 1000000000 | bytes 2629632 | tf_op jit(solution)/shard_map/pallas_call | solution.py:452
  80.3 9.8 %all-to-all-start.3 = ((f32[128,8,128]{2,1,0:T(8,128)}), f32[128,8,128]{2,1,0:T(8,128)S(1)}, u32[]{:S(2)}, u32[]{:S(2)}) async-start(f32[128,8,128]{2,1,0:T(8,128)} %get-tuple-element.32), calls=%async_computation.3 | async-start | bytes 1048576 | tf_op jit(solution)/shard_map/all_to_all | solution.py:566
  90.1 7.3 %shard_map.136 = (f32[4,16384]{1,0:T(4,128)}, f32[4,16384]{1,0:T(4,128)}) custom-call(f32[256,256]{1,0:T(8,128)} %get-tuple-element.26.mortar, s32[1,16384]{1,0:T(1,128)} %get-tuple-element.19.place, f32[4,16384]{1,0:T(4,128)} %get-tuple-element.27.part, f32[4,16384]{1,0:T(4,128)} %multiplier.3, s32[4,16384]{1,0:T(4,128)} %active.3), custom_call_target="tpu_custom_call" | custom-call | flops 10000000000 | bytes 1638400 | tf_op jit(solution)/shard_map/pallas_call | solution.py:452
  97.4 6.2 %all-to-all-done.3.factor = f32[128,8,128]{2,1,0:T(8,128)S(1)} async-done(((f32[128,8,128]{2,1,0:T(8,128)}), f32[128,8,128]{2,1,0:T(8,128)S(1)}, u32[]{:S(2)}, u32[]{:S(2)}) %all-to-all-start.3) | async-done | bytes 524320 | tf_op jit(solution)/shard_map/all_to_all | solution.py:566
  103.6 6.9 %shard_map.137 = f32[8,12,512]{2,1,0:T(8,128)S(1)} custom-call(f32[128,8,128]{2,1,0:T(8,128)S(1)} %all-to-all-done.recv, f32[128,8,128]{2,1,0:T(8,128)S(1)} %all-to-all-done.3.factor), custom_call_target="tpu_custom_call" | custom-call | flops 10000000000 | bytes 1245184 | tf_op jit(solution)/shard_map/pallas_call | solution.py:452
  110.6 0.0 copy-start
  110.6 10.0 %all_to_all.25.moved = f32[8,12,512]{2,1,0:T(8,128)S(1)} all-to-all(f32[8,12,512]{2,1,0:T(8,128)S(1)} %shard_map.137), channel_id=1, replica_groups=mesh['region'=16,'dom'=8] {'dom'}, dimensions={0} | all-to-all | bytes 393216 | tf_op jit(solution)/shard_map/all_to_all | solution.py:590
  120.6 0.0 copy-done
  120.6 1.8 %shard_map.138 = f32[12,4096]{1,0:T(8,128)} custom-call(f32[8,12,512]{2,1,0:T(8,128)S(1)} %all_to_all.25.moved, s32[1,4096]{1,0:T(1,128)S(1)} %copy-done), custom_call_target="tpu_custom_call" | custom-call | flops 1000000000 | bytes 409600 | tf_op jit(solution)/shard_map/pallas_call | solution.py:452
Async XLA Ops:
  3.3 16.8 %all-to-all-start.1 = ((f32[8,12,512]{2,1,0:T(8,128)}), f32[8,12,512]{2,1,0:T(8,128)S(1)}, u32[]{:S(2)}, u32[]{:S(2)}) async-start(f32[8,12,512]{2,1,0:T(8,128)} %shard_map.131), calls=%async_computation.1 | async-start | bytes 524288 | tf_op jit(solution)/shard_map/all_to_all | solution.py:494
  20.2 23.9 %all-to-all-start = ((f32[128,8,128]{2,1,0:T(8,128)}), f32[128,8,128]{2,1,0:T(8,128)S(1)}, u32[]{:S(2)}, u32[]{:S(2)}) async-start(f32[128,8,128]{2,1,0:T(8,128)} %get-tuple-element.18), calls=%async_computation | async-start | bytes 1048576 | tf_op jit(solution)/shard_map/all_to_all | solution.py:516
  52.3 21.4 %all-to-all-start.2 = ((f32[128,8,128]{2,1,0:T(8,128)}), f32[128,8,128]{2,1,0:T(8,128)S(1)}, u32[]{:S(2)}, u32[]{:S(2)}) async-start(f32[128,8,128]{2,1,0:T(8,128)} %shard_map.133), calls=%async_computation.2 | async-start | bytes 1048576 | tf_op jit(solution)/shard_map/all_to_all | solution.py:529
  73.7 0.8 copy-start.1
  80.3 23.3 %all-to-all-start.3 = ((f32[128,8,128]{2,1,0:T(8,128)}), f32[128,8,128]{2,1,0:T(8,128)S(1)}, u32[]{:S(2)}, u32[]{:S(2)}) async-start(f32[128,8,128]{2,1,0:T(8,128)} %get-tuple-element.32), calls=%async_computation.3 | async-start | bytes 1048576 | tf_op jit(solution)/shard_map/all_to_all | solution.py:566
  110.6 10.0 %copy-start = (s32[1,4096]{1,0:T(1,128)S(1)}, s32[1,4096]{1,0:T(1,128)}, u32[]{:S(2)}) copy-start(s32[1,4096]{1,0:T(1,128)} %pick.3) | copy-start | bytes 49156

commit v6 on v5

--- a/solution.py
+++ b/solution.py
@@ -23,12 +23,21 @@
 LANE = 256
 
 UNROLL = 32
+PARTS = 2
 NN = (((1,), (0,)), ((), ()))
 NT = (((1,), (1,)), ((), ()))
 
 
 def sub_iota(rows, cols):
     return lax.broadcasted_iota(jnp.int32, (rows, cols), 0)
+
+
+def quotient(value, by):
+    return lax.shift_right_logical(value, jnp.int32(by.bit_length() - 1))
+
+
+def remainder(value, by):
+    return lax.bitwise_and(value, jnp.int32(by - 1))
 
 
 def split(values):
@@ -76,8 +85,8 @@
 
 def pick_table(table, index, lows):
     n = index.shape[1]
-    grabbed = grab(table, index % LANE, False)
-    low = jnp.broadcast_to(index // LANE, (8, n))
+    grabbed = grab(table, remainder(index, LANE), False)
+    low = jnp.broadcast_to(quotient(index, LANE), (8, n))
     pair = low - sub_iota(8, n) // 4
     first = jnp.zeros((8, n), F32)
     for l in range(lows):
@@ -95,14 +104,14 @@
 def add_table(first, second, index, lows):
     high, low = split(first)
     group = jnp.concatenate([high.astype(F32), low.astype(F32)], axis=0).astype(BF)
-    wide = spread(index // LANE, [group], 1, lows)[0]
+    wide = spread(quotient(index, LANE), [group], 1, lows)[0]
     high, low = split(second)
     high, low = high.astype(F32), low.astype(F32)
     group = jnp.concatenate([high, low, high, low], axis=0).astype(BF)
-    narrow = spread(index // LANE, [group], 2, lows)[0]
+    narrow = spread(quotient(index, LANE), [group], 2, lows)[0]
     stacked = jnp.concatenate(wide + narrow, axis=0)
     return lax.dot_general(
-        stacked, onehot(index % LANE, LANE), NT, preferred_element_type=F32
+        stacked, onehot(remainder(index, LANE), LANE), NT, preferred_element_type=F32
     )
 
 
@@ -110,6 +119,22 @@
     first = total[16 * l : 16 * l + 8] + total[16 * l + 8 : 16 * l + 16]
     at = 16 * lows + 8 * l
     return first, total[at : at + 4] + total[at + 4 : at + 8]
+
+
+def store_tile(out, k, t, first, second):
+    tiles = out.shape[1] // 12
+    out[k, 8 * t : 8 * t + 8, :] = first
+    out[k, 8 * tiles + 4 * t : 8 * tiles + 4 * t + 4, :] = second
+
+
+def load_tiles(source):
+    tiles = source.shape[1] // 12
+    rows = []
+    for k in range(source.shape[0]):
+        for t in range(tiles):
+            low = source[k, 8 * tiles + 4 * t : 8 * tiles + 4 * t + 4, :]
+            rows.append(jnp.concatenate([source[k, 8 * t : 8 * t + 8, :], low], axis=0))
+    return jnp.concatenate(rows, axis=1)
 
 
 def pick_kernel(vol, pick, out, table):
@@ -120,11 +145,12 @@
         jnp.concatenate([rows[3 * c + j : 3 * c + j + 1] for j in range(3) for c in range(4)], axis=0),
         table,
     )
-    count, _, part = out.shape
+    count, tiles, _ = out.shape
+    part = width // count
     for k in range(count):
         first, second = pick_table(table[...], pick[:, k * part : (k + 1) * part], lows)
-        out[k, 0:8, :] = first
-        out[k, 8:12, :] = second
+        for t in range(tiles // 12):
+            store_tile(out, k, t, first[:, t * 128 : (t + 1) * 128], second[:, t * 128 : (t + 1) * 128])
 
 
 def lane_iota(rows, cols):
@@ -135,13 +161,32 @@
     pieces = []
     for value in values:
         pieces += split(jnp.concatenate([value] * 4, axis=0))
-    stacked = jnp.concatenate(sum(spread(place // LANE, pieces, 4, lows), []), axis=0)
-    return lax.dot_general(stacked, onehot(place % LANE, LANE), NT, preferred_element_type=F32)
+    stacked = jnp.concatenate(sum(spread(quotient(place, LANE), pieces, 4, lows), []), axis=0)
+    return lax.dot_general(stacked, onehot(remainder(place, LANE), LANE), NT, preferred_element_type=F32)
+
+
+def sort_parts(values, place, total):
+    per = place.shape[1] // PARTS
+    each = total.shape[0] // PARTS
+
+    def body(p, _):
+        lanes = pl.ds(pl.multiple_of(p * per, per), per)
+        rows = pl.ds(pl.multiple_of(p * each, each), each)
+        total[rows, :] = sort_terms(values(lanes), remainder(place[:, lanes], per), per // LANE)
+        return 0
+
+    lax.fori_loop(0, PARTS, body, 0)
 
 
 def sorted_sums(total, lows):
-    rows = 4 * lows
-    return [total[i : i + rows] + total[i + rows : i + 2 * rows] for i in range(0, total.shape[0], 2 * rows)]
+    rows, each = 4 * lows, total.shape[0] // PARTS
+    sums = []
+    for i in range(0, each, 2 * rows):
+        parts = []
+        for at in range(i, total.shape[0], each):
+            parts.append(total[at : at + rows] + total[at + rows : at + 2 * rows])
+        sums.append(jnp.concatenate(parts, axis=0))
+    return sums
 
 
 def cut_windows(sums, offsets, ordered, out, masked):
@@ -161,16 +206,20 @@
     lane = lane_iota(8, 128)
     number = lane + jnp.where(top, 0, 128)
 
+    def cut(start):
+        block, shift = quotient(start, 128), remainder(start, 128)
+        joined = jnp.where(lane >= shift, ordered[block], ordered[block + 1])
+        return pltpu.roll(joined, remainder(128 - shift, 128), 1)
+
     def window(i, _):
         for u in range(UNROLL):
             o = i * UNROLL + u
+            later = offsets[1, o + 1]
+            back = cut(later - 256)
+            if masked:
+                back = jnp.where(number >= 256 + offsets[1, o] - later, back, 0.0)
             start = offsets[0, o]
-            block, shift = start // 128, start % 128
-            joined = jnp.where(lane >= shift, ordered[block], ordered[block + 1])
-            joined = pltpu.roll(joined, (128 - shift) % 128, 1)
-            if masked:
-                joined = jnp.where(number < offsets[0, o + 1] - start, joined, 0.0)
-            out[o] = joined
+            out[o] = jnp.where(number < offsets[0, o + 1] - start, cut(start), back)
         return 0
 
     lax.fori_loop(0, out.shape[0] // UNROLL, window, 0)
@@ -179,29 +228,49 @@
 def merge_windows(windows, offsets, merged, lows):
     lane = lane_iota(8, 128)
     top = sub_iota(8, 128) < 4
+    owners = windows.shape[0]
+    per = 2 * lows // PARTS
+    gap = 8
+
+    def shifted(o, shift):
+        value = pltpu.roll(windows[o], shift, 1)
+        other = pltpu.roll(value, 4, 0)
+        return jnp.where(top, value, other), jnp.where(top, other, value)
 
     def window(i, carry):
+        front, back = carry
         for u in range(UNROLL):
             o = i * UNROLL + u
             start, later = offsets[0, o], offsets[0, o + 1]
-            block, shift = start // 128, start % 128
-            value = pltpu.roll(windows[o], shift, 1)
-            turned = pltpu.roll(value, 4, 0)
-            one, two = jnp.where(top, value, turned), jnp.where(top, turned, value)
-            first = jnp.where(lane >= shift, one, carry)
+            block, shift = quotient(start, 128), remainder(start, 128)
+            one, two = shifted(o, shift)
+            first = jnp.where(lane >= shift, one, front)
             second = jnp.where(lane >= shift, two, one)
             merged[block] = first
             merged[block + 1] = second
             merged[block + 2] = two
-            ahead = later // 128 - block
-            carry = jnp.where(ahead == 0, first, jnp.where(ahead == 1, second, two))
-        return carry
-
-    lax.fori_loop(0, windows.shape[0] // UNROLL, window, jnp.zeros((8, 128), F32))
+            ahead = quotient(later, 128) - block
+            front = jnp.where(ahead == 0, first, jnp.where(ahead == 1, second, two))
+            o = owners - 1 - o
+            start, later = offsets[1, o], offsets[1, o + 1]
+            block, shift = quotient(later, 128) + gap, remainder(later, 128)
+            one, two = shifted(o, shift)
+            second = jnp.where(lane >= shift, two, one)
+            third = jnp.where(lane >= shift, back, two)
+            merged[block - 2] = one
+            merged[block - 1] = second
+            merged[block] = third
+            behind = block - gap - quotient(start, 128)
+            back = jnp.where(behind == 0, third, jnp.where(behind == 1, second, one))
+        return front, back
+
+    zero = jnp.zeros((8, 128), F32)
+    lax.fori_loop(0, owners // UNROLL, window, (zero, zero))
     left, right = [], []
     for g in range(lows // 2):
-        left.append(jnp.where(top, merged[4 * g], merged[4 * g + 2]))
-        right.append(jnp.where(top, merged[4 * g + 1], merged[4 * g + 3]))
+        at = 4 * g if 4 * g < per else 4 * g + gap
+        left.append(jnp.where(top, merged[at], merged[at + 2]))
+        right.append(jnp.where(top, merged[at + 1], merged[at + 3]))
     return jnp.concatenate([jnp.concatenate(left, axis=0), jnp.concatenate(right, axis=0)], axis=1)
 
 
@@ -214,8 +283,7 @@
         copy.start()
     count = owner.shape[1]
     owners = out.shape[0]
-    lows = count // LANE
-    total[...] = jnp.zeros_like(total)
+    lows = count // PARTS // LANE
     copies[0].wait()
 
     groups = owners // 16
@@ -235,44 +303,44 @@
             sums = sums + names
         return sums
 
-    sums = lax.fori_loop(0, count // step, tally, jnp.zeros((owners, 256), BF))
-    counts = lax.dot_general(sums, jnp.ones((256, 256), BF), NN, preferred_element_type=F32).astype(BF)
     lower = (sub_iota(owners, owners) > lane_iota(owners, owners)).astype(F32).astype(BF)
     upper = (sub_iota(256, 256) < lane_iota(256, 256)).astype(F32).astype(BF)
-    base = lax.dot_general(lower, counts, NN, preferred_element_type=F32)
-    high, low = split(base + lax.dot_general(sums, upper, NN, preferred_element_type=F32))
-    counts = lax.dot_general(jnp.ones((16, 256), BF), sums, NT, preferred_element_type=F32).astype(BF)
-    upper = (sub_iota(owners, 2 * owners) < lane_iota(owners, 2 * owners)).astype(F32).astype(BF)
-    offset[...] = lax.dot_general(counts, upper, NN, preferred_element_type=F32)[0:8].astype(jnp.int32)
+    wide = (sub_iota(owners, 2 * owners) < lane_iota(owners, 2 * owners)).astype(F32).astype(BF)
+    per = count // PARTS
+    bases, starts = [], []
+    for p in range(PARTS):
+        sums = lax.fori_loop(p * per // step, (p + 1) * per // step, tally, jnp.zeros((owners, 256), BF))
+        counts = lax.dot_general(sums, jnp.ones((256, 256), BF), NN, preferred_element_type=F32).astype(BF)
+        base = lax.dot_general(lower, counts, NN, preferred_element_type=F32)
+        bases.append(split(base + lax.dot_general(sums, upper, NN, preferred_element_type=F32)))
+        counts = lax.dot_general(jnp.ones((16, 256), BF), sums, NT, preferred_element_type=F32).astype(BF)
+        starts.append(lax.dot_general(counts, wide, NN, preferred_element_type=F32)[0:8] + 1.0 * p * per)
+    offset[...] = jnp.where(sub_iota(8, 2 * owners) == 0, starts[0], starts[1]).astype(jnp.int32)
     save = pltpu.make_async_copy(offset, scalars, sems.at[3])
     save.start()
 
-    def ranks(i, _):
-        for u in range(step // 256):
-            lanes = pl.ds(pl.multiple_of(i * step + u * 256, 256), 256)
-            names = named[:, lanes]
-            found = before[:, lanes] + lookup(names, high) + lookup(names, low)
-            place[:, lanes] = found.astype(jnp.int32)
-        return 0
-
-    lax.fori_loop(0, count // step, ranks, 0)
+    for p in range(PARTS):
+
+        def ranks(i, _):
+            for u in range(step // 256):
+                lanes = pl.ds(pl.multiple_of(i * step + u * 256, 256), 256)
+                names = named[:, lanes]
+                found = before[:, lanes] + lookup(names, bases[p][0]) + lookup(names, bases[p][1])
+                place[:, lanes] = (found + 1.0 * p * per).astype(jnp.int32)
+            return 0
+
+        lax.fori_loop(p * per // step, (p + 1) * per // step, ranks, 0)
     copies[1].wait()
     copies[2].wait()
 
-    def slots(i, _):
-        lanes = pl.ds(pl.multiple_of(i * step, step), step)
-        values = jnp.concatenate([slot[:, lanes].astype(F32), normal[:, lanes]], axis=0)
-        total[...] += sort_terms([values], place[:, lanes], lows)
-        return 0
-
-    lax.fori_loop(0, count // step, slots, 0)
+    sort_parts(lambda lanes: [jnp.concatenate([slot[:, lanes].astype(F32), normal[:, lanes]], axis=0)], place, total)
     save.wait()
     cut_windows(sorted_sums(total, lows)[0], scalars, ordered, out, True)
 
 
 def along_kernel(group, surf, recv, out, table):
-    lows = surf.shape[0] * surf.shape[2] // LANE
-    fill_table(jnp.concatenate([surf[s] for s in range(surf.shape[0])], axis=1), table)
+    lows = table.shape[0] // 24
+    fill_table(load_tiles(surf), table)
 
     def step(i, _):
         parts = [recv[i * group + u] for u in range(group)]
@@ -304,30 +372,20 @@
     return jnp.where(row < 4 - by, pltpu.roll(values, 8 - by, 1), pltpu.roll(values, 4 - by, 1))
 
 
-def sort_kernel(step, place, proj, out, total):
-    lows = place.shape[1] // LANE
-    total[...] = jnp.zeros_like(total)
-
-    def body(i, _):
-        lanes = pl.ds(pl.multiple_of(i * step, step), step)
+def sort_kernel(place, proj, out, total):
+    def values(lanes):
         p = proj[:, lanes]
-        values = [jnp.concatenate([p[2 * q + k : 2 * q + k + 1] for q in range(4)], axis=0) for k in range(2)]
-        total[...] += sort_terms(values, place[:, lanes], lows)
-        return 0
-
-    lax.fori_loop(0, place.shape[1] // step, body, 0)
-    for k, value in enumerate(sorted_sums(total, lows)):
+        return [jnp.concatenate([p[2 * q + k : 2 * q + k + 1] for q in range(4)], axis=0) for k in range(2)]
+
+    sort_parts(values, place, total)
+    for k, value in enumerate(sorted_sums(total, place.shape[1] // PARTS // LANE)):
         out[k] = value
 
 
-def local_kernel(step, place, disp, normal, gap, weight, multiplier, active, proj, part, level, factors, total):
-    count = place.shape[1]
-    lows = count // LANE
+def local_kernel(place, disp, normal, gap, weight, multiplier, active, proj, part, factors, total):
     sub4 = sub_iota(4, 1)
-    total[...] = jnp.zeros_like(total)
-
-    def body(i, _):
-        lanes = pl.ds(pl.multiple_of(i * step, step), step)
+
+    def values(lanes):
         w, d, n, g = weight[:, lanes], disp[:, lanes], normal[:, lanes], gap[:, lanes]
         points = g
         for b in range(4):
@@ -339,12 +397,11 @@
             result = result + by_node([slave_table[a][q] for a in range(4)], sub4) * points[q : q + 1]
         part[:, lanes] = result
         start = jnp.where(active[:, lanes] == 1, multiplier[:, lanes] - result, -1e30)
-        total[...] += sort_terms([w, start], place[:, lanes], lows)
-        return 0
-
-    lax.fori_loop(0, count // step, body, 0)
-    w, start = sorted_sums(total, lows)
-    level[...] = start
+        return [w, start]
+
+    sort_parts(values, place, total)
+    w, start = sorted_sums(total, place.shape[1] // PARTS // LANE)
+    factors[4] = start
     first, second, w = [v.reshape(-1, 8, LANE) for v in (proj[0], proj[1], w)]
     row = lax.broadcasted_iota(jnp.int32, (1, 8, 1), 1) % 4
     sums = [None] * 4
@@ -359,45 +416,44 @@
         factors[d] = sums[d].reshape(-1, LANE)
 
 
-def update_kernel(*refs):
-    inputs, out, mortar_out = refs[0:4], refs[4], refs[5]
-    recv, offsets, level, factors = refs[6:10]
-    ordered, sems = refs[10:12]
-    copies = [pltpu.make_async_copy(inputs[i], refs[6 + i], sems.at[i]) for i in range(4)]
+def update_kernel(recv, offsets_hbm, factors_hbm, out, mortar_out, offsets, factors, ordered, sems):
+    copies = [
+        pltpu.make_async_copy(a, b, sems.at[i])
+        for i, (a, b) in enumerate(((offsets_hbm, offsets), (factors_hbm, factors)))
+    ]
     for copy in copies:
         copy.start()
-    for copy in copies[0:2]:
-        copy.wait()
-    lows = level.shape[0] // 4
+    copies[0].wait()
+    lows = factors.shape[1] // 4
     along = merge_windows(recv, offsets, ordered, lows).reshape(-1, 8, LANE)
-    for copy in copies[2:]:
-        copy.wait()
+    copies[1].wait()
     parts = [factors[d].reshape(-1, 8, LANE) for d in range(4)]
     mortar = parts[0] * along
     for d in range(1, 4):
         mortar = mortar + parts[d] * turned(along, d)
     mortar_out[...] = mortar.reshape(-1, LANE)
-    lagrange = jnp.maximum(level[...].reshape(-1, 8, LANE) + mortar, 0.0)
+    lagrange = jnp.maximum(factors[4].reshape(-1, 8, LANE) + mortar, 0.0)
     terms = parts[0] * lagrange
     for d in range(1, 4):
         terms = terms + turned(parts[d] * lagrange, 4 - d)
     cut_windows(terms.reshape(-1, LANE), offsets, ordered, out, False)
 
 
-def restore_kernel(step, mortar, place, part, multiplier, active, gap_out, new_out, table):
-    count = place.shape[1]
-    lows = count // LANE
-    half = table.shape[0] // 2
-    high, low = split(mortar[...])
-    table[0:half, :] = high
-    table[half:, :] = low
-
-    def body(i, _):
-        lanes = pl.ds(pl.multiple_of(i * step, step), step)
-        places = place[:, lanes]
-        grabbed = grab(table[...], places % LANE, True)
-        base = jnp.broadcast_to(places // LANE, (8, step)) - sub_iota(8, step) // 4
-        found = jnp.zeros((8, step), F32)
+def restore_kernel(mortar, place, part, multiplier, active, gap_out, new_out, table):
+    per = place.shape[1] // PARTS
+    lows = per // LANE
+    rows = 4 * lows
+    for p in range(PARTS):
+        high, low = split(mortar[p * rows : (p + 1) * rows])
+        table[p, 0:rows, :] = high
+        table[p, rows:, :] = low
+
+    def body(p, _):
+        lanes = pl.ds(pl.multiple_of(p * per, per), per)
+        places = remainder(place[:, lanes], per)
+        grabbed = grab(table[p], remainder(places, LANE), True)
+        base = jnp.broadcast_to(quotient(places, LANE), (8, per)) - sub_iota(8, per) // 4
+        found = jnp.zeros((8, per), F32)
         for g in range(lows // 2):
             found = jnp.where(base == 2 * g, grabbed[8 * g : 8 * g + 8], found)
         weighted = part[:, lanes] - (found[0:4] + found[4:8])
@@ -405,11 +461,11 @@
         new_out[:, lanes] = jnp.where(active[:, lanes] == 1, jnp.maximum(multiplier[:, lanes] - weighted, 0.0), 0.0)
         return 0
 
-    lax.fori_loop(0, count // step, body, 0)
+    lax.fori_loop(0, PARTS, body, 0)
 
 
 def force_kernel(group, recv, factor, out, total):
-    lows = out.shape[0] * out.shape[2] // LANE
+    lows = total.shape[0] // 24
     total[...] = jnp.zeros_like(total)
 
     def step(i, _):
@@ -424,17 +480,17 @@
 
     lax.fori_loop(0, recv.shape[0] // group, step, 0)
     sums = total[...]
-    per = out.shape[2] // LANE
+    per = lows // out.shape[0]
     for l in range(lows):
         first, second = table_part(sums, lows, l)
-        lanes = slice(l % per * LANE, (l % per + 1) * LANE)
-        out[l // per, 0:8, lanes] = first
-        out[l // per, 8:12, lanes] = second
+        for t in range(LANE // 128):
+            lanes = slice(t * 128, (t + 1) * 128)
+            store_tile(out, l // per, l % per * (LANE // 128) + t, first[:, lanes], second[:, lanes])
 
 
 def place_kernel(moved, pick, out):
     lows = out.shape[1] // LANE
-    rows = jnp.concatenate([moved[k] for k in range(moved.shape[0])], axis=1)
+    rows = load_tiles(moved)
     sums = add_table(rows[0:8], rows[8:12], pick[...], lows)
     for l in range(lows):
         first, second = table_part(sums, lows, l)
@@ -490,7 +546,7 @@
     whole, quad = (1, count), (4, count)
 
     table = pltpu.VMEM((24 * lows, LANE), BF)
-    picked = call(pick_kernel, "vvv", [((dom_count, 12, part), F32)], [table], 10**9, master_vol, surf_pick, mebibytes=60)
+    picked = call(pick_kernel, "vvv", [((dom_count, 12 * part // 128, 128), F32)], [table], 10**9, master_vol, surf_pick, mebibytes=60)
     surf = exchange(picked, "dom")
     request, place, offset = call(
         functools.partial(request_kernel, 2 * step),
@@ -515,7 +571,7 @@
     )
     recv = exchange(request, everyone)
     sorted_proj = call(
-        functools.partial(sort_kernel, step),
+        sort_kernel,
         "vvv",
         [((2, 4 * blocks, LANE), F32)],
         [pltpu.VMEM((16 * blocks, LANE), F32)],
@@ -525,13 +581,13 @@
         mebibytes=56,
     )
     surf, sorted_proj = lax.optimization_barrier((surf, sorted_proj))
-    along = call(functools.partial(along_kernel, 32), "vvv", [(flat, F32)], [table], 10**10, surf, recv)
+    along = call(functools.partial(along_kernel, 64), "vvv", [(flat, F32)], [table], 10**10, surf, recv)
     returned = exchange(along, everyone)
     along, sorted_proj = lax.optimization_barrier((along, sorted_proj))
-    slave_part, level, factors = call(
-        functools.partial(local_kernel, step),
-        "v" * 11,
-        [(quad, F32), ((4 * blocks, LANE), F32), ((4, 4 * blocks, LANE), F32)],
+    slave_part, factors = call(
+        local_kernel,
+        "v" * 10,
+        [(quad, F32), ((5, 4 * blocks, LANE), F32)],
         [pltpu.VMEM((16 * blocks, LANE), F32)],
         10**10,
         place,
@@ -546,29 +602,26 @@
     )
     terms, mortar = call(
         update_kernel,
-        "hhhhvv",
+        "vhhvv",
         [(flat, F32), ((4 * blocks, LANE), F32)],
         [
-            pltpu.VMEM(flat, F32),
             pltpu.SMEM((8, 2 * owners), jnp.int32),
-            pltpu.VMEM((4 * blocks, LANE), F32),
-            pltpu.VMEM((4, 4 * blocks, LANE), F32),
-            pltpu.VMEM((2 * blocks + 4, 8, 128), F32),
-            pltpu.SemaphoreType.DMA((4,)),
+            pltpu.VMEM((5, 4 * blocks, LANE), F32),
+            pltpu.VMEM((2 * blocks + 12, 8, 128), F32),
+            pltpu.SemaphoreType.DMA((2,)),
         ],
         10**9,
         returned,
         offset,
-        level,
         factors,
-        mebibytes=56,
+        mebibytes=52,
     )
     factor = exchange(terms, everyone)
     weighted_gap, multiplier_new = call(
-        functools.partial(restore_kernel, step),
+        restore_kernel,
         "v" * 7,
         [(quad, F32), (quad, F32)],
-        [pltpu.VMEM((8 * blocks, LANE), BF)],
+        [pltpu.VMEM((PARTS, 8 * blocks // PARTS, LANE), BF)],
         10**10,
         mortar,
         place,
@@ -579,9 +632,9 @@
     )
     recv, weighted_gap = lax.optimization_barrier((recv, weighted_gap))
     forces = call(
-        functools.partial(force_kernel, 64),
+        functools.partial(force_kernel, 128),
         "vvv",
-        [((dom_count, 12, part), F32)],
+        [((dom_count, 12 * part // 128, 128), F32)],
         [pltpu.VMEM((24 * lows, LANE), F32)],
         10**10,
         recv,

time: 123 us -> 110 us (0.89)
  Pallas kernels: 68.8 us -> 52 us
  waiting for transfers between devices: 8.26 us -> 20.2 us
  starting transfers between devices: 33.9 us -> 26.1 us
    pallas_call x9, Pallas kernels: 68.8 us -> 52 us  [call(): pl.pallas_call(kernel, out_shape=[jax.ShapeDtypeStruct(*o) for o in outs]...]
    all_to_all x1, waiting for transfers between devices: 2 us -> 6.81 us  [on_device(): recv = exchange(request, everyone)]
    all_to_all x1, waiting for transfers between devices: 0.01 us -> 4.6 us  [on_device(): returned = exchange(along, everyone)]
    all_to_all x1, starting transfers between devices: 9.77 us -> 5.19 us  [on_device(): factor = exchange(terms, everyone)]
    all_to_all x1, starting transfers between devices: 7.77 us -> 4.59 us  [on_device(): returned = exchange(along, everyone)]
    all_to_all x1, waiting for transfers between devices: 6.25 us -> 8.79 us  [on_device(): factor = exchange(terms, everyone)]
  transfers between devices with their start and end apart: 4 -> 4, of which waited for: 2 -> 3; matrix products, arithmetic and copies ran while one was open for 0% -> 0% of each run, Pallas kernels for 35% -> 26%
where the time goes in v6:
time: 110 us; the launch traced here: 109 us
  Pallas kernels  52 us (47%)
  starting transfers between devices  26.1 us (24%)
  waiting for transfers between devices  20.2 us (18%)
  blocking collectives  9.35 us (8%)
    pallas_call x9, Pallas kernels, call(): pl.pallas_call(kernel, out_shape=[jax.ShapeDtypeStruct(*o) for o in outs]...  52 us
    all_to_all x1, starting transfers between devices, on_device(): recv = exchange(request, everyone)  10.3 us
    all_to_all x1, blocking collectives, on_device(): moved = exchange(forces, 'dom')  9.35 us
    all_to_all x1, waiting for transfers between devices, on_device(): factor = exchange(terms, everyone)  8.79 us
    all_to_all x1, waiting for transfers between devices, on_device(): recv = exchange(request, everyone)  6.81 us
    all_to_all x1, starting transfers between devices, on_device(): surf = exchange(picked, 'dom')  5.97 us
    all_to_all x1, starting transfers between devices, on_device(): factor = exchange(terms, everyone)  5.19 us
    all_to_all x1, waiting for transfers between devices, on_device(): returned = exchange(along, everyone)  4.6 us
  transfers between devices with their start and end apart: 4, of which 3 were waited for; matrix products, arithmetic and copies ran while one was open for 0% of the time, Pallas kernels for 26%

profile of v6, /device:TPU:1, one launch (start us, length us, event | category | flops | bytes accessed | tf_op | source)
XLA Modules:
  0.0 109.1 jit_solution(10089517684812973321)
XLA Ops:
  0.6 2.7 %shard_map.131 = f32[8,48,128]{2,1,0:T(8,128)} custom-call(f32[12,4096]{1,0:T(8,128)} %vol.1, s32[1,4096]{1,0:T(1,128)} %pick.3), custom_call_target="tpu_custom_call" | custom-call | flops 1000000000 | bytes 409600 | tf_op jit(solution)/shard_map/pallas_call | solution.py:508
  3.3 6.0 %all-to-all-start.1 = ((f32[8,48,128]{2,1,0:T(8,128)}), f32[8,48,128]{2,1,0:T(8,128)S(1)}, u32[]{:S(2)}, u32[]{:S(2)}) async-start(f32[8,48,128]{2,1,0:T(8,128)} %shard_map.131), calls=%async_computation.1 | async-start | bytes 393216 | tf_op jit(solution)/shard_map/all_to_all | solution.py:550
  9.3 8.1 %shard_map.130 = (f32[128,8,128]{2,1,0:T(8,128)}, s32[1,16384]{1,0:T(1,128)}, s32[8,256]{1,0:T(8,128)}) custom-call(s32[1,16384]{1,0:T(1,128)} %bitcast.2, s32[1,16384]{1,0:T(1,128)} %bitcast.3, f32[3,16384]{1,0:T(4,128)} %normal.1), custom_call_target="tpu_custom_call" | custom-call | flops 10000000000 | bytes 925696 | tf_op jit(solution)/shard_map/pallas_call | solution.py:508
  17.3 0.0 all-to-all-done.1.surf
  17.4 10.3 %all-to-all-start = ((f32[128,8,128]{2,1,0:T(8,128)}), f32[128,8,128]{2,1,0:T(8,128)S(1)}, u32[]{:S(2)}, u32[]{:S(2)}) async-start(f32[128,8,128]{2,1,0:T(8,128)} %get-tuple-element.17), calls=%async_computation | async-start | bytes 1048576 | tf_op jit(solution)/shard_map/all_to_all | solution.py:572
  27.7 6.7 %shard_map.132.proj = f32[2,256,256]{2,1,0:T(8,128)} custom-call(s32[1,16384]{1,0:T(1,128)} %get-tuple-element.18.place, f32[8,16384]{1,0:T(8,128)} %proj.1), custom_call_target="tpu_custom_call" | custom-call | flops 10000000000 | bytes 1114112 | tf_op jit(solution)/shard_map/pallas_call | solution.py:508
  34.4 6.8 %all-to-all-done.recv = f32[128,8,128]{2,1,0:T(8,128)S(1)} async-done(((f32[128,8,128]{2,1,0:T(8,128)}), f32[128,8,128]{2,1,0:T(8,128)S(1)}, u32[]{:S(2)}, u32[]{:S(2)}) %all-to-all-start) | async-done | bytes 524320 | tf_op jit(solution)/shard_map/all_to_all | solution.py:572
  41.2 7.8 %shard_map.133 = f32[128,8,128]{2,1,0:T(8,128)} custom-call(f32[8,48,128]{2,1,0:T(8,128)S(1)} %all-to-all-done.1.surf, f32[128,8,128]{2,1,0:T(8,128)S(1)} %all-to-all-done.recv), custom_call_target="tpu_custom_call" | custom-call | flops 10000000000 | bytes 1245184 | tf_op jit(solution)/shard_map/pallas_call | solution.py:508
  49.0 4.6 %all-to-all-start.2 = ((f32[128,8,128]{2,1,0:T(8,128)}), f32[128,8,128]{2,1,0:T(8,128)S(1)}, u32[]{:S(2)}, u32[]{:S(2)}) async-start(f32[128,8,128]{2,1,0:T(8,128)} %shard_map.133), calls=%async_computation.2 | async-start | bytes 1048576 | tf_op jit(solution)/shard_map/all_to_all | solution.py:585
  53.6 0.0 copy-start.2
  53.6 8.9 %shard_map.134 = (f32[4,16384]{1,0:T(4,128)}, f32[5,256,256]{2,1,0:T(8,128)}) custom-call(s32[1,16384]{1,0:T(1,128)} %get-tuple-element.18.place, f32[12,16384]{1,0:T(8,128)} %disp.1, f32[3,16384]{1,0:T(4,128)} %normal.1, f32[4,16384]{1,0:T(4,128)} %gap.1, f32[4,16384]{1,0:T(4,128)} %weight.1, f32[4,16384]{1,0:T(4,128)} %multiplier.3, s32[4,16384]{1,0:T(4,128)} %active.3, ...), custom_call_target="tpu_custom_call" | custom-call | flops 10000000000 | bytes 4194304 | tf_op jit(solution)/shard_map/pallas_call | solution.py:508
  62.5 4.6 %all-to-all-done.2.recv = f32[128,8,128]{2,1,0:T(8,128)S(1)} async-done(((f32[128,8,128]{2,1,0:T(8,128)}), f32[128,8,128]{2,1,0:T(8,128)S(1)}, u32[]{:S(2)}, u32[]{:S(2)}) %all-to-all-start.2) | async-done | bytes 524320 | tf_op jit(solution)/shard_map/all_to_all | solution.py:585
  67.1 0.0 copy-done.2
  67.1 4.8 %shard_map.135 = (f32[128,8,128]{2,1,0:T(8,128)}, f32[256,256]{1,0:T(8,128)S(1)}) custom-call(f32[128,8,128]{2,1,0:T(8,128)S(1)} %all-to-all-done.2.recv, s32[8,256]{1,0:T(8,128)S(1)} %copy-done.2, f32[5,256,256]{2,1,0:T(8,128)} %get-tuple-element.23.factors_hbm), custom_call_target="tpu_custom_call" | custom-call | flops 1000000000 | bytes 2629632 | tf_op jit(solution)/shard_map/pallas_call | solution.py:508
  71.9 0.0 copy-start.1
  71.9 0.7 copy-done.1
  72.6 5.2 %all-to-all-start.3 = ((f32[128,8,128]{2,1,0:T(8,128)}), f32[128,8,128]{2,1,0:T(8,128)S(1)}, u32[]{:S(2)}, u32[]{:S(2)}) async-start(f32[128,8,128]{2,1,0:T(8,128)} %get-tuple-element.30), calls=%async_computation.3 | async-start | bytes 1048576 | tf_op jit(solution)/shard_map/all_to_all | solution.py:619
  77.8 4.7 %shard_map.136 = (f32[4,16384]{1,0:T(4,128)}, f32[4,16384]{1,0:T(4,128)}) custom-call(f32[256,256]{1,0:T(8,128)} %copy-done.1, s32[1,16384]{1,0:T(1,128)} %get-tuple-element.18.place, f32[4,16384]{1,0:T(4,128)} %get-tuple-element.25.part, f32[4,16384]{1,0:T(4,128)} %multiplier.3, s32[4,16384]{1,0:T(4,128)} %active.3), custom_call_target="tpu_custom_call" | custom-call | flops 10000000000 | bytes 1638400 | tf_op jit(solution)/shard_map/pallas_call | solution.py:508
  82.5 0.0 copy-start
  82.5 8.8 %all-to-all-done.3.factor = f32[128,8,128]{2,1,0:T(8,128)S(1)} async-done(((f32[128,8,128]{2,1,0:T(8,128)}), f32[128,8,128]{2,1,0:T(8,128)S(1)}, u32[]{:S(2)}, u32[]{:S(2)}) %all-to-all-start.3) | async-done | bytes 524320 | tf_op jit(solution)/shard_map/all_to_all | solution.py:619
  91.3 6.7 %shard_map.137 = f32[8,48,128]{2,1,0:T(8,128)S(1)} custom-call(f32[128,8,128]{2,1,0:T(8,128)S(1)} %all-to-all-done.recv, f32[128,8,128]{2,1,0:T(8,128)S(1)} %all-to-all-done.3.factor), custom_call_target="tpu_custom_call" | custom-call | flops 10000000000 | bytes 1245184 | tf_op jit(solution)/shard_map/pallas_call | solution.py:508
  98.0 9.3 %all_to_all.25.moved = f32[8,48,128]{2,1,0:T(8,128)S(1)} all-to-all(f32[8,48,128]{2,1,0:T(8,128)S(1)} %shard_map.137), channel_id=1, replica_groups=mesh['region'=16,'dom'=8] {'dom'}, dimensions={0} | all-to-all | bytes 393216 | tf_op jit(solution)/shard_map/all_to_all | solution.py:643
  107.3 0.0 copy-done
  107.3 1.8 %shard_map.138 = f32[12,4096]{1,0:T(8,128)} custom-call(f32[8,48,128]{2,1,0:T(8,128)S(1)} %all_to_all.25.moved, s32[1,4096]{1,0:T(1,128)S(1)} %copy-done), custom_call_target="tpu_custom_call" | custom-call | flops 1000000000 | bytes 409600 | tf_op jit(solution)/shard_map/pallas_call | solution.py:508
Async XLA Ops:
  3.3 14.0 %all-to-all-start.1 = ((f32[8,48,128]{2,1,0:T(8,128)}), f32[8,48,128]{2,1,0:T(8,128)S(1)}, u32[]{:S(2)}, u32[]{:S(2)}) async-start(f32[8,48,128]{2,1,0:T(8,128)} %shard_map.131), calls=%async_computation.1 | async-start | bytes 393216 | tf_op jit(solution)/shard_map/all_to_all | solution.py:550
  17.4 23.9 %all-to-all-start = ((f32[128,8,128]{2,1,0:T(8,128)}), f32[128,8,128]{2,1,0:T(8,128)S(1)}, u32[]{:S(2)}, u32[]{:S(2)}) async-start(f32[128,8,128]{2,1,0:T(8,128)} %get-tuple-element.17), calls=%async_computation | async-start | bytes 1048576 | tf_op jit(solution)/shard_map/all_to_all | solution.py:572
  49.0 18.1 %all-to-all-start.2 = ((f32[128,8,128]{2,1,0:T(8,128)}), f32[128,8,128]{2,1,0:T(8,128)S(1)}, u32[]{:S(2)}, u32[]{:S(2)}) async-start(f32[128,8,128]{2,1,0:T(8,128)} %shard_map.133), calls=%async_computation.2 | async-start | bytes 1048576 | tf_op jit(solution)/shard_map/all_to_all | solution.py:585
  53.6 13.5 %copy-start.2 = (s32[8,256]{1,0:T(8,128)S(1)}, s32[8,256]{1,0:T(8,128)}, u32[]{:S(2)}) copy-start(s32[8,256]{1,0:T(8,128)} %get-tuple-element.20.offsets_hbm) | copy-start | bytes 24580
  71.9 0.7 copy-start.1
  72.6 18.7 %all-to-all-start.3 = ((f32[128,8,128]{2,1,0:T(8,128)}), f32[128,8,128]{2,1,0:T(8,128)S(1)}, u32[]{:S(2)}, u32[]{:S(2)}) async-start(f32[128,8,128]{2,1,0:T(8,128)} %get-tuple-element.30), calls=%async_computation.3 | async-start | bytes 1048576 | tf_op jit(solution)/shard_map/all_to_all | solution.py:619
  82.5 24.8 %copy-start = (s32[1,4096]{1,0:T(1,128)S(1)}, s32[1,4096]{1,0:T(1,128)}, u32[]{:S(2)}) copy-start(s32[1,4096]{1,0:T(1,128)} %pick.3) | copy-start | bytes 49156

commit v7 on v6

--- a/solution.py
+++ b/solution.py
@@ -274,18 +274,10 @@
     return jnp.concatenate([jnp.concatenate(left, axis=0), jnp.concatenate(right, axis=0)], axis=1)
 
 
-def request_kernel(step, owner_hbm, slot_hbm, normal_hbm, out, place, offset, owner, slot, normal, total, named, before, ordered, scalars, sems):
-    copies = [
-        pltpu.make_async_copy(a, b, sems.at[i])
-        for i, (a, b) in enumerate(((owner_hbm, owner), (slot_hbm, slot), (normal_hbm, normal)))
-    ]
-    for copy in copies:
-        copy.start()
+def request_kernel(step, owner, slot, normal, out, place, offset, total, named, before, ordered, scalars, sem):
     count = owner.shape[1]
     owners = out.shape[0]
     lows = count // PARTS // LANE
-    copies[0].wait()
-
     groups = owners // 16
 
     def lookup(names, columns):
@@ -316,7 +308,7 @@
         counts = lax.dot_general(jnp.ones((16, 256), BF), sums, NT, preferred_element_type=F32).astype(BF)
         starts.append(lax.dot_general(counts, wide, NN, preferred_element_type=F32)[0:8] + 1.0 * p * per)
     offset[...] = jnp.where(sub_iota(8, 2 * owners) == 0, starts[0], starts[1]).astype(jnp.int32)
-    save = pltpu.make_async_copy(offset, scalars, sems.at[3])
+    save = pltpu.make_async_copy(offset, scalars, sem)
     save.start()
 
     for p in range(PARTS):
@@ -330,8 +322,6 @@
             return 0
 
         lax.fori_loop(p * per // step, (p + 1) * per // step, ranks, 0)
-    copies[1].wait()
-    copies[2].wait()
 
     sort_parts(lambda lanes: [jnp.concatenate([slot[:, lanes].astype(F32), normal[:, lanes]], axis=0)], place, total)
     save.wait()
@@ -550,24 +540,20 @@
     surf = exchange(picked, "dom")
     request, place, offset = call(
         functools.partial(request_kernel, 2 * step),
-        "hhhvvv",
+        "vvvvvv",
         [(flat, F32), (whole, jnp.int32), ((8, 2 * owners), jnp.int32)],
         [
-            pltpu.VMEM(whole, jnp.int32),
-            pltpu.VMEM(whole, jnp.int32),
-            pltpu.VMEM((3, count), F32),
             pltpu.VMEM((8 * blocks, LANE), F32),
             pltpu.VMEM((owners, count), BF),
             pltpu.VMEM(whole, F32),
             pltpu.VMEM((2 * blocks + 4, 8, 128), F32),
             pltpu.SMEM((8, 2 * owners), jnp.int32),
-            pltpu.SemaphoreType.DMA((4,)),
+            pltpu.SemaphoreType.DMA,
         ],
         10**10,
         owner,
         pair_slot.reshape(1, count),
         slave_normal,
-        mebibytes=56,
     )
     recv = exchange(request, everyone)
     sorted_proj = call(
@@ -628,7 +614,7 @@
         slave_part,
         multiplier,
         active,
-        mebibytes=56,
+        mebibytes=48,
     )
     recv, weighted_gap = lax.optimization_barrier((recv, weighted_gap))
     forces = call(

time: 110 us -> 108 us (0.982)
  Pallas kernels: 52 us -> 49.9 us
  waiting for transfers between devices: 20.2 us -> 21.4 us
    pallas_call x9, Pallas kernels: 52 us -> 49.9 us  [call(): pl.pallas_call(kernel, out_shape=[jax.ShapeDtypeStruct(*o) for o in outs]...]
    all_to_all x1, waiting for transfers between devices: 8.79 us -> 9.96 us  [on_device(): factor = exchange(terms, everyone)]
  transfers between devices with their start and end apart: 4 -> 4, of which waited for: 3 -> 3; matrix products, arithmetic and copies ran while one was open for 0% -> 0% of each run, Pallas kernels for 26% -> 24%
where the time goes in v7:
time: 108 us
  Pallas kernels  49.9 us (46%)
  starting transfers between devices  26.1 us (24%)
  waiting for transfers between devices  21.4 us (20%)
  blocking collectives  9.36 us (9%)
    pallas_call x9, Pallas kernels, call(): pl.pallas_call(kernel, out_shape=[jax.ShapeDtypeStruct(*o) for o in outs]...  49.9 us
    all_to_all x1, starting transfers between devices, on_device(): recv = exchange(request, everyone)  10.3 us
    all_to_all x1, waiting for transfers between devices, on_device(): factor = exchange(terms, everyone)  9.96 us
    all_to_all x1, blocking collectives, on_device(): moved = exchange(forces, 'dom')  9.36 us
    all_to_all x1, waiting for transfers between devices, on_device(): recv = exchange(request, everyone)  6.84 us
    all_to_all x1, starting transfers between devices, on_device(): surf = exchange(picked, 'dom')  5.97 us
    all_to_all x1, starting transfers between devices, on_device(): factor = exchange(terms, everyone)  5.21 us
    all_to_all x1, waiting for transfers between devices, on_device(): returned = exchange(along, everyone)  4.6 us
  transfers between devices with their start and end apart: 4, of which 3 were waited for; matrix products, arithmetic and copies ran while one was open for 0% of the time, Pallas kernels for 24%

profile of v7, /device:TPU:1, one launch (start us, length us, event | category | flops | bytes accessed | tf_op | source)
XLA Modules:
  0.0 107.6 jit_solution(9037748581302756964)
XLA Ops:
  0.6 0.0 copy-start
  0.6 0.0 copy-start.4
  0.7 0.0 copy-start.3
  0.7 2.7 %shard_map.131 = f32[8,48,128]{2,1,0:T(8,128)} custom-call(f32[12,4096]{1,0:T(8,128)} %vol.1, s32[1,4096]{1,0:T(1,128)} %pick.3), custom_call_target="tpu_custom_call" | custom-call | flops 1000000000 | bytes 409600 | tf_op jit(solution)/shard_map/pallas_call | solution.py:498
  3.4 6.0 %all-to-all-start.1 = ((f32[8,48,128]{2,1,0:T(8,128)}), f32[8,48,128]{2,1,0:T(8,128)S(1)}, u32[]{:S(2)}, u32[]{:S(2)}) async-start(f32[8,48,128]{2,1,0:T(8,128)} %shard_map.131), calls=%async_computation.1 | async-start | bytes 393216 | tf_op jit(solution)/shard_map/all_to_all | solution.py:540
  9.3 0.0 copy-done
  9.4 0.0 copy-done.4
  9.4 0.0 copy-done.3
  9.4 7.2 %shard_map.130 = (f32[128,8,128]{2,1,0:T(8,128)}, s32[1,16384]{1,0:T(1,128)S(1)}, s32[8,256]{1,0:T(8,128)S(1)}) custom-call(s32[1,16384]{1,0:T(1,128)S(1)} %bitcast.2, s32[1,16384]{1,0:T(1,128)S(1)} %bitcast.3, f32[3,16384]{1,0:T(4,128)S(1)} %copy-done), custom_call_target="tpu_custom_call" | custom-call | flops 10000000000 | bytes 925696 | tf_op jit(solution)/shard_map/pallas_call | solution.py:498
  16.6 0.0 copy-start.7
  16.6 0.0 all-to-all-done.1.surf
  16.6 10.3 %all-to-all-start = ((f32[128,8,128]{2,1,0:T(8,128)}), f32[128,8,128]{2,1,0:T(8,128)S(1)}, u32[]{:S(2)}, u32[]{:S(2)}) async-start(f32[128,8,128]{2,1,0:T(8,128)} %get-tuple-element.17), calls=%async_computation | async-start | bytes 1048576 | tf_op jit(solution)/shard_map/all_to_all | solution.py:558
  26.9 0.0 copy-done.7
  26.9 6.7 %shard_map.132.proj = f32[2,256,256]{2,1,0:T(8,128)} custom-call(s32[1,16384]{1,0:T(1,128)} %copy-done.7, f32[8,16384]{1,0:T(8,128)} %proj.1), custom_call_target="tpu_custom_call" | custom-call | flops 10000000000 | bytes 1114112 | tf_op jit(solution)/shard_map/pallas_call | solution.py:498
  33.6 6.8 %all-to-all-done.recv = f32[128,8,128]{2,1,0:T(8,128)S(1)} async-done(((f32[128,8,128]{2,1,0:T(8,128)}), f32[128,8,128]{2,1,0:T(8,128)S(1)}, u32[]{:S(2)}, u32[]{:S(2)}) %all-to-all-start) | async-done | bytes 524320 | tf_op jit(solution)/shard_map/all_to_all | solution.py:558
  40.4 7.8 %shard_map.133 = f32[128,8,128]{2,1,0:T(8,128)} custom-call(f32[8,48,128]{2,1,0:T(8,128)S(1)} %all-to-all-done.1.surf, f32[128,8,128]{2,1,0:T(8,128)S(1)} %all-to-all-done.recv), custom_call_target="tpu_custom_call" | custom-call | flops 10000000000 | bytes 1245184 | tf_op jit(solution)/shard_map/pallas_call | solution.py:498
  48.2 4.6 %all-to-all-start.2 = ((f32[128,8,128]{2,1,0:T(8,128)}), f32[128,8,128]{2,1,0:T(8,128)S(1)}, u32[]{:S(2)}, u32[]{:S(2)}) async-start(f32[128,8,128]{2,1,0:T(8,128)} %shard_map.133), calls=%async_computation.2 | async-start | bytes 1048576 | tf_op jit(solution)/shard_map/all_to_all | solution.py:571
  52.8 8.9 %shard_map.134 = (f32[4,16384]{1,0:T(4,128)}, f32[5,256,256]{2,1,0:T(8,128)}) custom-call(s32[1,16384]{1,0:T(1,128)} %copy-done.7, f32[12,16384]{1,0:T(8,128)} %disp.1, f32[3,16384]{1,0:T(4,128)} %normal.3, f32[4,16384]{1,0:T(4,128)} %gap.1, f32[4,16384]{1,0:T(4,128)} %weight.1, f32[4,16384]{1,0:T(4,128)} %multiplier.3, s32[4,16384]{1,0:T(4,128)} %active.3, ...), custom_call_target="tpu_custom_call" | custom-call | flops 10000000000 | bytes 4194304 | tf_op jit(solution)/shard_map/pallas_call | solution.py:498
  61.7 4.6 %all-to-all-done.2.recv = f32[128,8,128]{2,1,0:T(8,128)S(1)} async-done(((f32[128,8,128]{2,1,0:T(8,128)}), f32[128,8,128]{2,1,0:T(8,128)S(1)}, u32[]{:S(2)}, u32[]{:S(2)}) %all-to-all-start.2) | async-done | bytes 524320 | tf_op jit(solution)/shard_map/all_to_all | solution.py:571
  66.3 0.0 copy-start.1
  66.3 0.0 copy-start.2
  66.3 0.0 copy-start.6
  66.3 0.0 copy-start.8
  66.3 4.7 %shard_map.135 = (f32[128,8,128]{2,1,0:T(8,128)}, f32[256,256]{1,0:T(8,128)S(1)}) custom-call(f32[128,8,128]{2,1,0:T(8,128)S(1)} %all-to-all-done.2.recv, s32[8,256]{1,0:T(8,128)S(1)} %get-tuple-element.20.offsets_hbm, f32[5,256,256]{2,1,0:T(8,128)} %get-tuple-element.23.factors_hbm), custom_call_target="tpu_custom_call" | custom-call | flops 1000000000 | bytes 2629632 | tf_op jit(solution)/shard_map/pallas_call | solution.py:498
  71.1 5.2 %all-to-all-start.3 = ((f32[128,8,128]{2,1,0:T(8,128)}), f32[128,8,128]{2,1,0:T(8,128)S(1)}, u32[]{:S(2)}, u32[]{:S(2)}) async-start(f32[128,8,128]{2,1,0:T(8,128)} %get-tuple-element.30), calls=%async_computation.3 | async-start | bytes 1048576 | tf_op jit(solution)/shard_map/all_to_all | solution.py:605
  76.3 0.0 copy-done.1
  76.3 0.0 copy-done.2
  76.3 0.0 copy-done.6
  76.3 0.0 copy-done.8
  76.3 3.5 %shard_map.136 = (f32[4,16384]{1,0:T(4,128)}, f32[4,16384]{1,0:T(4,128)}) custom-call(f32[256,256]{1,0:T(8,128)S(1)} %get-tuple-element.24.mortar, s32[1,16384]{1,0:T(1,128)S(1)} %copy-done.8, f32[4,16384]{1,0:T(4,128)S(1)} %copy-done.6, f32[4,16384]{1,0:T(4,128)S(1)} %copy-done.1, s32[4,16384]{1,0:T(4,128)S(1)} %copy-done.2), custom_call_target="tpu_custom_call" | custom-call | flops 10000000000 | bytes 1638400 | tf_op jit(solution)/shard_map/pallas_call | solution.py:498
  79.8 0.0 copy-start.5
  79.8 10.0 %all-to-all-done.3.factor = f32[128,8,128]{2,1,0:T(8,128)S(1)} async-done(((f32[128,8,128]{2,1,0:T(8,128)}), f32[128,8,128]{2,1,0:T(8,128)S(1)}, u32[]{:S(2)}, u32[]{:S(2)}) %all-to-all-start.3) | async-done | bytes 524320 | tf_op jit(solution)/shard_map/all_to_all | solution.py:605
  89.8 6.7 %shard_map.137 = f32[8,48,128]{2,1,0:T(8,128)S(1)} custom-call(f32[128,8,128]{2,1,0:T(8,128)S(1)} %all-to-all-done.recv, f32[128,8,128]{2,1,0:T(8,128)S(1)} %all-to-all-done.3.factor), custom_call_target="tpu_custom_call" | custom-call | flops 10000000000 | bytes 1245184 | tf_op jit(solution)/shard_map/pallas_call | solution.py:498
  96.5 9.4 %all_to_all.25.moved = f32[8,48,128]{2,1,0:T(8,128)S(1)} all-to-all(f32[8,48,128]{2,1,0:T(8,128)S(1)} %shard_map.137), channel_id=1, replica_groups=mesh['region'=16,'dom'=8] {'dom'}, dimensions={0} | all-to-all | bytes 393216 | tf_op jit(solution)/shard_map/all_to_all | solution.py:629
  105.8 0.0 copy-done.5
  105.8 1.8 %shard_map.138 = f32[12,4096]{1,0:T(8,128)} custom-call(f32[8,48,128]{2,1,0:T(8,128)S(1)} %all_to_all.25.moved, s32[1,4096]{1,0:T(1,128)S(1)} %copy-done.5), custom_call_target="tpu_custom_call" | custom-call | flops 1000000000 | bytes 409600 | tf_op jit(solution)/shard_map/pallas_call | solution.py:498
Async XLA Ops:
  0.6 8.7 %copy-start = (f32[3,16384]{1,0:T(4,128)S(1)}, f32[3,16384]{1,0:T(4,128)}, u32[]{:S(2)}) copy-start(f32[3,16384]{1,0:T(4,128)} %normal.3) | copy-start | bytes 589828
  0.6 8.7 %copy-start.4 = (s32[16384]{0:T(1024)S(1)}, s32[16384]{0:T(1024)}, u32[]{:S(2)}) copy-start(s32[16384]{0:T(1024)} %param.19) | copy-start | bytes 196612
  0.7 8.7 %copy-start.3 = (s32[16384,1]{0,1:T(1,128)S(1)}, s32[16384,1]{0,1:T(1,128)}, u32[]{:S(2)}) copy-start(s32[16384,1]{0,1:T(1,128)} %param.18) | copy-start | bytes 196612
  3.4 13.2 %all-to-all-start.1 = ((f32[8,48,128]{2,1,0:T(8,128)}), f32[8,48,128]{2,1,0:T(8,128)S(1)}, u32[]{:S(2)}, u32[]{:S(2)}) async-start(f32[8,48,128]{2,1,0:T(8,128)} %shard_map.131), calls=%async_computation.1 | async-start | bytes 393216 | tf_op jit(solution)/shard_map/all_to_all | solution.py:540
  16.6 10.4 %copy-start.7 = (s32[1,16384]{1,0:T(1,128)}, s32[1,16384]{1,0:T(1,128)S(1)}, u32[]{:S(2)}) copy-start(s32[1,16384]{1,0:T(1,128)S(1)} %get-tuple-element.18.place) | copy-start | bytes 196612
  16.6 23.9 %all-to-all-start = ((f32[128,8,128]{2,1,0:T(8,128)}), f32[128,8,128]{2,1,0:T(8,128)S(1)}, u32[]{:S(2)}, u32[]{:S(2)}) async-start(f32[128,8,128]{2,1,0:T(8,128)} %get-tuple-element.17), calls=%async_computation | async-start | bytes 1048576 | tf_op jit(solution)/shard_map/all_to_all | solution.py:558
  48.2 18.1 %all-to-all-start.2 = ((f32[128,8,128]{2,1,0:T(8,128)}), f32[128,8,128]{2,1,0:T(8,128)S(1)}, u32[]{:S(2)}, u32[]{:S(2)}) async-start(f32[128,8,128]{2,1,0:T(8,128)} %shard_map.133), calls=%async_computation.2 | async-start | bytes 1048576 | tf_op jit(solution)/shard_map/all_to_all | solution.py:571
  66.3 10.0 %copy-start.1 = (f32[4,16384]{1,0:T(4,128)S(1)}, f32[4,16384]{1,0:T(4,128)}, u32[]{:S(2)}) copy-start(f32[4,16384]{1,0:T(4,128)} %multiplier.3) | copy-start | bytes 786436
  66.3 10.0 %copy-start.2 = (s32[4,16384]{1,0:T(4,128)S(1)}, s32[4,16384]{1,0:T(4,128)}, u32[]{:S(2)}) copy-start(s32[4,16384]{1,0:T(4,128)} %active.3) | copy-start | bytes 786436
  66.3 10.0 %copy-start.6 = (f32[4,16384]{1,0:T(4,128)S(1)}, f32[4,16384]{1,0:T(4,128)}, u32[]{:S(2)}) copy-start(f32[4,16384]{1,0:T(4,128)} %get-tuple-element.25.part) | copy-start | bytes 786436
  66.3 10.0 %copy-start.8 = (s32[1,16384]{1,0:T(1,128)S(1)}, s32[1,16384]{1,0:T(1,128)}, u32[]{:S(2)}) copy-start(s32[1,16384]{1,0:T(1,128)} %copy-done.7) | copy-start | bytes 196612
  71.1 18.7 %all-to-all-start.3 = ((f32[128,8,128]{2,1,0:T(8,128)}), f32[128,8,128]{2,1,0:T(8,128)S(1)}, u32[]{:S(2)}, u32[]{:S(2)}) async-start(f32[128,8,128]{2,1,0:T(8,128)} %get-tuple-element.30), calls=%async_computation.3 | async-start | bytes 1048576 | tf_op jit(solution)/shard_map/all_to_all | solution.py:605
  79.8 26.0 %copy-start.5 = (s32[1,4096]{1,0:T(1,128)S(1)}, s32[1,4096]{1,0:T(1,128)}, u32[]{:S(2)}) copy-start(s32[1,4096]{1,0:T(1,128)} %pick.3) | copy-start | bytes 49156

commit v8 on v7

--- a/solution.py
+++ b/solution.py
@@ -22,7 +22,7 @@
 F32 = jnp.float32
 LANE = 256
 
-UNROLL = 32
+UNROLL = 64
 PARTS = 2
 NN = (((1,), (0,)), ((), ()))
 NT = (((1,), (1,)), ((), ()))
@@ -211,18 +211,13 @@
         joined = jnp.where(lane >= shift, ordered[block], ordered[block + 1])
         return pltpu.roll(joined, remainder(128 - shift, 128), 1)
 
-    def window(i, _):
-        for u in range(UNROLL):
-            o = i * UNROLL + u
-            later = offsets[1, o + 1]
-            back = cut(later - 256)
-            if masked:
-                back = jnp.where(number >= 256 + offsets[1, o] - later, back, 0.0)
-            start = offsets[0, o]
-            out[o] = jnp.where(number < offsets[0, o + 1] - start, cut(start), back)
-        return 0
-
-    lax.fori_loop(0, out.shape[0] // UNROLL, window, 0)
+    for o in range(out.shape[0]):
+        later = offsets[1, o + 1]
+        back = cut(later - 256)
+        if masked:
+            back = jnp.where(number >= 256 + offsets[1, o] - later, back, 0.0)
+        start = offsets[0, o]
+        out[o] = jnp.where(number < offsets[0, o + 1] - start, cut(start), back)
 
 
 def merge_windows(windows, offsets, merged, lows):

time: 108 us -> 107 us (level)
  no operation moved by 1% of the time
where the time goes in v8:
time: 107 us
  Pallas kernels  49.1 us (46%)
  starting transfers between devices  26.1 us (24%)
  waiting for transfers between devices  21.4 us (20%)
  blocking collectives  9.35 us (9%)
    pallas_call x9, Pallas kernels, call(): pl.pallas_call(kernel, out_shape=[jax.ShapeDtypeStruct(*o) for o in outs]...  49.1 us
    all_to_all x1, starting transfers between devices, on_device(): recv = exchange(request, everyone)  10.3 us
    all_to_all x1, waiting for transfers between devices, on_device(): factor = exchange(terms, everyone)  9.96 us
    all_to_all x1, blocking collectives, on_device(): moved = exchange(forces, 'dom')  9.35 us
    all_to_all x1, waiting for transfers between devices, on_device(): recv = exchange(request, everyone)  6.84 us
    all_to_all x1, starting transfers between devices, on_device(): surf = exchange(picked, 'dom')  5.97 us
    all_to_all x1, starting transfers between devices, on_device(): factor = exchange(terms, everyone)  5.23 us
    all_to_all x1, waiting for transfers between devices, on_device(): returned = exchange(along, everyone)  4.61 us
  transfers between devices with their start and end apart: 4, of which 3 were waited for; matrix products, arithmetic and copies ran while one was open for 0% of the time, Pallas kernels for 24%

profile of v8, /device:TPU:1, one launch (start us, length us, event | category | flops | bytes accessed | tf_op | source)
XLA Modules:
  0.0 106.8 jit_solution(2292152881068683275)
XLA Ops:
  0.6 0.0 copy-start
  0.6 0.0 copy-start.4
  0.7 0.0 copy-start.3
  0.7 2.7 %shard_map.131 = f32[8,48,128]{2,1,0:T(8,128)} custom-call(f32[12,4096]{1,0:T(8,128)} %vol.1, s32[1,4096]{1,0:T(1,128)} %pick.3), custom_call_target="tpu_custom_call" | custom-call | flops 1000000000 | bytes 409600 | tf_op jit(solution)/shard_map/pallas_call | solution.py:493
  3.4 6.0 %all-to-all-start.1 = ((f32[8,48,128]{2,1,0:T(8,128)}), f32[8,48,128]{2,1,0:T(8,128)S(1)}, u32[]{:S(2)}, u32[]{:S(2)}) async-start(f32[8,48,128]{2,1,0:T(8,128)} %shard_map.131), calls=%async_computation.1 | async-start | bytes 393216 | tf_op jit(solution)/shard_map/all_to_all | solution.py:535
  9.3 0.0 copy-done
  9.4 0.0 copy-done.4
  9.4 0.0 copy-done.3
  9.4 6.7 %shard_map.130 = (f32[128,8,128]{2,1,0:T(8,128)}, s32[1,16384]{1,0:T(1,128)S(1)}, s32[8,256]{1,0:T(8,128)S(1)}) custom-call(s32[1,16384]{1,0:T(1,128)S(1)} %bitcast.2, s32[1,16384]{1,0:T(1,128)S(1)} %bitcast.3, f32[3,16384]{1,0:T(4,128)S(1)} %copy-done), custom_call_target="tpu_custom_call" | custom-call | flops 10000000000 | bytes 925696 | tf_op jit(solution)/shard_map/pallas_call | solution.py:493
  16.0 0.0 copy-start.7
  16.0 0.0 all-to-all-done.1.surf
  16.0 10.3 %all-to-all-start = ((f32[128,8,128]{2,1,0:T(8,128)}), f32[128,8,128]{2,1,0:T(8,128)S(1)}, u32[]{:S(2)}, u32[]{:S(2)}) async-start(f32[128,8,128]{2,1,0:T(8,128)} %get-tuple-element.17), calls=%async_computation | async-start | bytes 1048576 | tf_op jit(solution)/shard_map/all_to_all | solution.py:553
  26.4 0.0 copy-done.7
  26.4 6.7 %shard_map.132.proj = f32[2,256,256]{2,1,0:T(8,128)} custom-call(s32[1,16384]{1,0:T(1,128)} %copy-done.7, f32[8,16384]{1,0:T(8,128)} %proj.1), custom_call_target="tpu_custom_call" | custom-call | flops 10000000000 | bytes 1114112 | tf_op jit(solution)/shard_map/pallas_call | solution.py:493
  33.1 6.8 %all-to-all-done.recv = f32[128,8,128]{2,1,0:T(8,128)S(1)} async-done(((f32[128,8,128]{2,1,0:T(8,128)}), f32[128,8,128]{2,1,0:T(8,128)S(1)}, u32[]{:S(2)}, u32[]{:S(2)}) %all-to-all-start) | async-done | bytes 524320 | tf_op jit(solution)/shard_map/all_to_all | solution.py:553
  39.9 7.8 %shard_map.133 = f32[128,8,128]{2,1,0:T(8,128)} custom-call(f32[8,48,128]{2,1,0:T(8,128)S(1)} %all-to-all-done.1.surf, f32[128,8,128]{2,1,0:T(8,128)S(1)} %all-to-all-done.recv), custom_call_target="tpu_custom_call" | custom-call | flops 10000000000 | bytes 1245184 | tf_op jit(solution)/shard_map/pallas_call | solution.py:493
  47.7 4.6 %all-to-all-start.2 = ((f32[128,8,128]{2,1,0:T(8,128)}), f32[128,8,128]{2,1,0:T(8,128)S(1)}, u32[]{:S(2)}, u32[]{:S(2)}) async-start(f32[128,8,128]{2,1,0:T(8,128)} %shard_map.133), calls=%async_computation.2 | async-start | bytes 1048576 | tf_op jit(solution)/shard_map/all_to_all | solution.py:566
  52.3 8.9 %shard_map.134 = (f32[4,16384]{1,0:T(4,128)}, f32[5,256,256]{2,1,0:T(8,128)}) custom-call(s32[1,16384]{1,0:T(1,128)} %copy-done.7, f32[12,16384]{1,0:T(8,128)} %disp.1, f32[3,16384]{1,0:T(4,128)} %normal.3, f32[4,16384]{1,0:T(4,128)} %gap.1, f32[4,16384]{1,0:T(4,128)} %weight.1, f32[4,16384]{1,0:T(4,128)} %multiplier.3, s32[4,16384]{1,0:T(4,128)} %active.3, ...), custom_call_target="tpu_custom_call" | custom-call | flops 10000000000 | bytes 4194304 | tf_op jit(solution)/shard_map/pallas_call | solution.py:493
  61.2 4.6 %all-to-all-done.2.recv = f32[128,8,128]{2,1,0:T(8,128)S(1)} async-done(((f32[128,8,128]{2,1,0:T(8,128)}), f32[128,8,128]{2,1,0:T(8,128)S(1)}, u32[]{:S(2)}, u32[]{:S(2)}) %all-to-all-start.2) | async-done | bytes 524320 | tf_op jit(solution)/shard_map/all_to_all | solution.py:566
  65.8 0.0 copy-start.1
  65.8 0.0 copy-start.2
  65.8 0.0 copy-start.6
  65.8 0.0 copy-start.8
  65.8 4.5 %shard_map.135 = (f32[128,8,128]{2,1,0:T(8,128)}, f32[256,256]{1,0:T(8,128)S(1)}) custom-call(f32[128,8,128]{2,1,0:T(8,128)S(1)} %all-to-all-done.2.recv, s32[8,256]{1,0:T(8,128)S(1)} %get-tuple-element.20.offsets_hbm, f32[5,256,256]{2,1,0:T(8,128)} %get-tuple-element.23.factors_hbm), custom_call_target="tpu_custom_call" | custom-call | flops 1000000000 | bytes 2629632 | tf_op jit(solution)/shard_map/pallas_call | solution.py:493
  70.3 5.2 %all-to-all-start.3 = ((f32[128,8,128]{2,1,0:T(8,128)}), f32[128,8,128]{2,1,0:T(8,128)S(1)}, u32[]{:S(2)}, u32[]{:S(2)}) async-start(f32[128,8,128]{2,1,0:T(8,128)} %get-tuple-element.30), calls=%async_computation.3 | async-start | bytes 1048576 | tf_op jit(solution)/shard_map/all_to_all | solution.py:600
  75.5 0.0 copy-done.1
  75.5 0.0 copy-done.2
  75.5 0.0 copy-done.6
  75.5 0.0 copy-done.8
  75.6 3.5 %shard_map.136 = (f32[4,16384]{1,0:T(4,128)}, f32[4,16384]{1,0:T(4,128)}) custom-call(f32[256,256]{1,0:T(8,128)S(1)} %get-tuple-element.24.mortar, s32[1,16384]{1,0:T(1,128)S(1)} %copy-done.8, f32[4,16384]{1,0:T(4,128)S(1)} %copy-done.6, f32[4,16384]{1,0:T(4,128)S(1)} %copy-done.1, s32[4,16384]{1,0:T(4,128)S(1)} %copy-done.2), custom_call_target="tpu_custom_call" | custom-call | flops 10000000000 | bytes 1638400 | tf_op jit(solution)/shard_map/pallas_call | solution.py:493
  79.1 0.0 copy-start.5
  79.1 10.0 %all-to-all-done.3.factor = f32[128,8,128]{2,1,0:T(8,128)S(1)} async-done(((f32[128,8,128]{2,1,0:T(8,128)}), f32[128,8,128]{2,1,0:T(8,128)S(1)}, u32[]{:S(2)}, u32[]{:S(2)}) %all-to-all-start.3) | async-done | bytes 524320 | tf_op jit(solution)/shard_map/all_to_all | solution.py:600
  89.0 6.7 %shard_map.137 = f32[8,48,128]{2,1,0:T(8,128)S(1)} custom-call(f32[128,8,128]{2,1,0:T(8,128)S(1)} %all-to-all-done.recv, f32[128,8,128]{2,1,0:T(8,128)S(1)} %all-to-all-done.3.factor), custom_call_target="tpu_custom_call" | custom-call | flops 10000000000 | bytes 1245184 | tf_op jit(solution)/shard_map/pallas_call | solution.py:493
  95.7 9.3 %all_to_all.25.moved = f32[8,48,128]{2,1,0:T(8,128)S(1)} all-to-all(f32[8,48,128]{2,1,0:T(8,128)S(1)} %shard_map.137), channel_id=1, replica_groups=mesh['region'=16,'dom'=8] {'dom'}, dimensions={0} | all-to-all | bytes 393216 | tf_op jit(solution)/shard_map/all_to_all | solution.py:624
  105.1 0.0 copy-done.5
  105.1 1.8 %shard_map.138 = f32[12,4096]{1,0:T(8,128)} custom-call(f32[8,48,128]{2,1,0:T(8,128)S(1)} %all_to_all.25.moved, s32[1,4096]{1,0:T(1,128)S(1)} %copy-done.5), custom_call_target="tpu_custom_call" | custom-call | flops 1000000000 | bytes 409600 | tf_op jit(solution)/shard_map/pallas_call | solution.py:493
Async XLA Ops:
  0.6 8.7 %copy-start = (f32[3,16384]{1,0:T(4,128)S(1)}, f32[3,16384]{1,0:T(4,128)}, u32[]{:S(2)}) copy-start(f32[3,16384]{1,0:T(4,128)} %normal.3) | copy-start | bytes 589828
  0.6 8.7 %copy-start.4 = (s32[16384]{0:T(1024)S(1)}, s32[16384]{0:T(1024)}, u32[]{:S(2)}) copy-start(s32[16384]{0:T(1024)} %param.19) | copy-start | bytes 196612
  0.7 8.7 %copy-start.3 = (s32[16384,1]{0,1:T(1,128)S(1)}, s32[16384,1]{0,1:T(1,128)}, u32[]{:S(2)}) copy-start(s32[16384,1]{0,1:T(1,128)} %param.18) | copy-start | bytes 196612
  3.4 12.7 %all-to-all-start.1 = ((f32[8,48,128]{2,1,0:T(8,128)}), f32[8,48,128]{2,1,0:T(8,128)S(1)}, u32[]{:S(2)}, u32[]{:S(2)}) async-start(f32[8,48,128]{2,1,0:T(8,128)} %shard_map.131), calls=%async_computation.1 | async-start | bytes 393216 | tf_op jit(solution)/shard_map/all_to_all | solution.py:535
  16.0 10.4 %copy-start.7 = (s32[1,16384]{1,0:T(1,128)}, s32[1,16384]{1,0:T(1,128)S(1)}, u32[]{:S(2)}) copy-start(s32[1,16384]{1,0:T(1,128)S(1)} %get-tuple-element.18.place) | copy-start | bytes 196612
  16.0 23.9 %all-to-all-start = ((f32[128,8,128]{2,1,0:T(8,128)}), f32[128,8,128]{2,1,0:T(8,128)S(1)}, u32[]{:S(2)}, u32[]{:S(2)}) async-start(f32[128,8,128]{2,1,0:T(8,128)} %get-tuple-element.17), calls=%async_computation | async-start | bytes 1048576 | tf_op jit(solution)/shard_map/all_to_all | solution.py:553
  47.7 18.1 %all-to-all-start.2 = ((f32[128,8,128]{2,1,0:T(8,128)}), f32[128,8,128]{2,1,0:T(8,128)S(1)}, u32[]{:S(2)}, u32[]{:S(2)}) async-start(f32[128,8,128]{2,1,0:T(8,128)} %shard_map.133), calls=%async_computation.2 | async-start | bytes 1048576 | tf_op jit(solution)/shard_map/all_to_all | solution.py:566
  65.8 9.7 %copy-start.1 = (f32[4,16384]{1,0:T(4,128)S(1)}, f32[4,16384]{1,0:T(4,128)}, u32[]{:S(2)}) copy-start(f32[4,16384]{1,0:T(4,128)} %multiplier.3) | copy-start | bytes 786436
  65.8 9.7 %copy-start.2 = (s32[4,16384]{1,0:T(4,128)S(1)}, s32[4,16384]{1,0:T(4,128)}, u32[]{:S(2)}) copy-start(s32[4,16384]{1,0:T(4,128)} %active.3) | copy-start | bytes 786436
  65.8 9.8 %copy-start.6 = (f32[4,16384]{1,0:T(4,128)S(1)}, f32[4,16384]{1,0:T(4,128)}, u32[]{:S(2)}) copy-start(f32[4,16384]{1,0:T(4,128)} %get-tuple-element.25.part) | copy-start | bytes 786436
  65.8 9.8 %copy-start.8 = (s32[1,16384]{1,0:T(1,128)S(1)}, s32[1,16384]{1,0:T(1,128)}, u32[]{:S(2)}) copy-start(s32[1,16384]{1,0:T(1,128)} %copy-done.7) | copy-start | bytes 196612
  70.3 18.7 %all-to-all-start.3 = ((f32[128,8,128]{2,1,0:T(8,128)}), f32[128,8,128]{2,1,0:T(8,128)S(1)}, u32[]{:S(2)}, u32[]{:S(2)}) async-start(f32[128,8,128]{2,1,0:T(8,128)} %get-tuple-element.30), calls=%async_computation.3 | async-start | bytes 1048576 | tf_op jit(solution)/shard_map/all_to_all | solution.py:600
  79.1 26.0 %copy-start.5 = (s32[1,4096]{1,0:T(1,128)S(1)}, s32[1,4096]{1,0:T(1,128)}, u32[]{:S(2)}) copy-start(s32[1,4096]{1,0:T(1,128)} %pick.3) | copy-start | bytes 49156

commit v9 on v8

--- a/solution.py
+++ b/solution.py
@@ -279,7 +279,7 @@
         found = names[0:16] * columns[0:16]
         for g in range(1, groups):
             found = found + names[16 * g : 16 * g + 16] * columns[16 * g : 16 * g + 16]
-        return jnp.sum(found.astype(F32), axis=0, keepdims=True)
+        return found
 
     def tally(i, sums):
         for u in range(step // 256):
@@ -312,8 +312,10 @@
             for u in range(step // 256):
                 lanes = pl.ds(pl.multiple_of(i * step + u * 256, 256), 256)
                 names = named[:, lanes]
-                found = before[:, lanes] + lookup(names, bases[p][0]) + lookup(names, bases[p][1])
-                place[:, lanes] = (found + 1.0 * p * per).astype(jnp.int32)
+                found = lookup(names, bases[p][0]).astype(F32)
+                found = found + (before[:, lanes] + lookup(names, bases[p][1])).astype(F32)
+                found = jnp.sum(found, axis=0, keepdims=True) + 1.0 * p * per
+                place[:, lanes] = found.astype(jnp.int32)
             return 0
 
         lax.fori_loop(p * per // step, (p + 1) * per // step, ranks, 0)
@@ -540,7 +542,7 @@
         [
             pltpu.VMEM((8 * blocks, LANE), F32),
             pltpu.VMEM((owners, count), BF),
-            pltpu.VMEM(whole, F32),
+            pltpu.VMEM((16, count), BF),
             pltpu.VMEM((2 * blocks + 4, 8, 128), F32),
             pltpu.SMEM((8, 2 * owners), jnp.int32),
             pltpu.SemaphoreType.DMA,

time: 107 us -> 107 us (level)
  no operation moved by 1% of the time
where the time goes in v9:
time: 107 us
  Pallas kernels  48.9 us (46%)
  starting transfers between devices  26.1 us (24%)
  waiting for transfers between devices  21.4 us (20%)
  blocking collectives  9.35 us (9%)
    pallas_call x9, Pallas kernels, call(): pl.pallas_call(kernel, out_shape=[jax.ShapeDtypeStruct(*o) for o in outs]...  48.9 us
    all_to_all x1, starting transfers between devices, on_device(): recv = exchange(request, everyone)  10.3 us
    all_to_all x1, waiting for transfers between devices, on_device(): factor = exchange(terms, everyone)  9.96 us
    all_to_all x1, blocking collectives, on_device(): moved = exchange(forces, 'dom')  9.35 us
    all_to_all x1, waiting for transfers between devices, on_device(): recv = exchange(request, everyone)  6.84 us
    all_to_all x1, starting transfers between devices, on_device(): surf = exchange(picked, 'dom')  5.97 us
    all_to_all x1, starting transfers between devices, on_device(): factor = exchange(terms, everyone)  5.23 us
    all_to_all x1, waiting for transfers between devices, on_device(): returned = exchange(along, everyone)  4.61 us
  transfers between devices with their start and end apart: 4, of which 3 were waited for; matrix products, arithmetic and copies ran while one was open for 0% of the time, Pallas kernels for 24%

profile of v9, /device:TPU:1, one launch (start us, length us, event | category | flops | bytes accessed | tf_op | source)
XLA Modules:
  0.0 106.6 jit_solution(4882039189862842077)
XLA Ops:
  0.6 0.0 copy-start
  0.6 0.0 copy-start.4
  0.7 0.0 copy-start.3
  0.7 2.7 %shard_map.131 = f32[8,48,128]{2,1,0:T(8,128)} custom-call(f32[12,4096]{1,0:T(8,128)} %vol.1, s32[1,4096]{1,0:T(1,128)} %pick.3), custom_call_target="tpu_custom_call" | custom-call | flops 1000000000 | bytes 409600 | tf_op jit(solution)/shard_map/pallas_call | solution.py:495
  3.4 6.0 %all-to-all-start.1 = ((f32[8,48,128]{2,1,0:T(8,128)}), f32[8,48,128]{2,1,0:T(8,128)S(1)}, u32[]{:S(2)}, u32[]{:S(2)}) async-start(f32[8,48,128]{2,1,0:T(8,128)} %shard_map.131), calls=%async_computation.1 | async-start | bytes 393216 | tf_op jit(solution)/shard_map/all_to_all | solution.py:537
  9.3 0.0 copy-done
  9.4 0.0 copy-done.4
  9.4 0.0 copy-done.3
  9.4 6.4 %shard_map.130 = (f32[128,8,128]{2,1,0:T(8,128)}, s32[1,16384]{1,0:T(1,128)S(1)}, s32[8,256]{1,0:T(8,128)S(1)}) custom-call(s32[1,16384]{1,0:T(1,128)S(1)} %bitcast.2, s32[1,16384]{1,0:T(1,128)S(1)} %bitcast.3, f32[3,16384]{1,0:T(4,128)S(1)} %copy-done), custom_call_target="tpu_custom_call" | custom-call | flops 10000000000 | bytes 925696 | tf_op jit(solution)/shard_map/pallas_call | solution.py:495
  15.8 0.0 copy-start.7
  15.8 0.0 all-to-all-done.1.surf
  15.8 10.3 %all-to-all-start = ((f32[128,8,128]{2,1,0:T(8,128)}), f32[128,8,128]{2,1,0:T(8,128)S(1)}, u32[]{:S(2)}, u32[]{:S(2)}) async-start(f32[128,8,128]{2,1,0:T(8,128)} %get-tuple-element.17), calls=%async_computation | async-start | bytes 1048576 | tf_op jit(solution)/shard_map/all_to_all | solution.py:555
  26.2 0.0 copy-done.7
  26.2 6.7 %shard_map.132.proj = f32[2,256,256]{2,1,0:T(8,128)} custom-call(s32[1,16384]{1,0:T(1,128)} %copy-done.7, f32[8,16384]{1,0:T(8,128)} %proj.1), custom_call_target="tpu_custom_call" | custom-call | flops 10000000000 | bytes 1114112 | tf_op jit(solution)/shard_map/pallas_call | solution.py:495
  32.8 6.8 %all-to-all-done.recv = f32[128,8,128]{2,1,0:T(8,128)S(1)} async-done(((f32[128,8,128]{2,1,0:T(8,128)}), f32[128,8,128]{2,1,0:T(8,128)S(1)}, u32[]{:S(2)}, u32[]{:S(2)}) %all-to-all-start) | async-done | bytes 524320 | tf_op jit(solution)/shard_map/all_to_all | solution.py:555
  39.7 7.8 %shard_map.133 = f32[128,8,128]{2,1,0:T(8,128)} custom-call(f32[8,48,128]{2,1,0:T(8,128)S(1)} %all-to-all-done.1.surf, f32[128,8,128]{2,1,0:T(8,128)S(1)} %all-to-all-done.recv), custom_call_target="tpu_custom_call" | custom-call | flops 10000000000 | bytes 1245184 | tf_op jit(solution)/shard_map/pallas_call | solution.py:495
  47.4 4.6 %all-to-all-start.2 = ((f32[128,8,128]{2,1,0:T(8,128)}), f32[128,8,128]{2,1,0:T(8,128)S(1)}, u32[]{:S(2)}, u32[]{:S(2)}) async-start(f32[128,8,128]{2,1,0:T(8,128)} %shard_map.133), calls=%async_computation.2 | async-start | bytes 1048576 | tf_op jit(solution)/shard_map/all_to_all | solution.py:568
  52.0 8.9 %shard_map.134 = (f32[4,16384]{1,0:T(4,128)}, f32[5,256,256]{2,1,0:T(8,128)}) custom-call(s32[1,16384]{1,0:T(1,128)} %copy-done.7, f32[12,16384]{1,0:T(8,128)} %disp.1, f32[3,16384]{1,0:T(4,128)} %normal.3, f32[4,16384]{1,0:T(4,128)} %gap.1, f32[4,16384]{1,0:T(4,128)} %weight.1, f32[4,16384]{1,0:T(4,128)} %multiplier.3, s32[4,16384]{1,0:T(4,128)} %active.3, ...), custom_call_target="tpu_custom_call" | custom-call | flops 10000000000 | bytes 4194304 | tf_op jit(solution)/shard_map/pallas_call | solution.py:495
  60.9 4.6 %all-to-all-done.2.recv = f32[128,8,128]{2,1,0:T(8,128)S(1)} async-done(((f32[128,8,128]{2,1,0:T(8,128)}), f32[128,8,128]{2,1,0:T(8,128)S(1)}, u32[]{:S(2)}, u32[]{:S(2)}) %all-to-all-start.2) | async-done | bytes 524320 | tf_op jit(solution)/shard_map/all_to_all | solution.py:568
  65.5 0.0 copy-start.1
  65.5 0.0 copy-start.2
  65.5 0.0 copy-start.6
  65.5 0.0 copy-start.8
  65.6 4.5 %shard_map.135 = (f32[128,8,128]{2,1,0:T(8,128)}, f32[256,256]{1,0:T(8,128)S(1)}) custom-call(f32[128,8,128]{2,1,0:T(8,128)S(1)} %all-to-all-done.2.recv, s32[8,256]{1,0:T(8,128)S(1)} %get-tuple-element.20.offsets_hbm, f32[5,256,256]{2,1,0:T(8,128)} %get-tuple-element.23.factors_hbm), custom_call_target="tpu_custom_call" | custom-call | flops 1000000000 | bytes 2629632 | tf_op jit(solution)/shard_map/pallas_call | solution.py:495
  70.0 5.2 %all-to-all-start.3 = ((f32[128,8,128]{2,1,0:T(8,128)}), f32[128,8,128]{2,1,0:T(8,128)S(1)}, u32[]{:S(2)}, u32[]{:S(2)}) async-start(f32[128,8,128]{2,1,0:T(8,128)} %get-tuple-element.30), calls=%async_computation.3 | async-start | bytes 1048576 | tf_op jit(solution)/shard_map/all_to_all | solution.py:602
  75.3 0.0 copy-done.1
  75.3 0.0 copy-done.2
  75.3 0.0 copy-done.6
  75.3 0.0 copy-done.8
  75.3 3.5 %shard_map.136 = (f32[4,16384]{1,0:T(4,128)}, f32[4,16384]{1,0:T(4,128)}) custom-call(f32[256,256]{1,0:T(8,128)S(1)} %get-tuple-element.24.mortar, s32[1,16384]{1,0:T(1,128)S(1)} %copy-done.8, f32[4,16384]{1,0:T(4,128)S(1)} %copy-done.6, f32[4,16384]{1,0:T(4,128)S(1)} %copy-done.1, s32[4,16384]{1,0:T(4,128)S(1)} %copy-done.2), custom_call_target="tpu_custom_call" | custom-call | flops 10000000000 | bytes 1638400 | tf_op jit(solution)/shard_map/pallas_call | solution.py:495
  78.8 0.0 copy-start.5
  78.8 10.0 %all-to-all-done.3.factor = f32[128,8,128]{2,1,0:T(8,128)S(1)} async-done(((f32[128,8,128]{2,1,0:T(8,128)}), f32[128,8,128]{2,1,0:T(8,128)S(1)}, u32[]{:S(2)}, u32[]{:S(2)}) %all-to-all-start.3) | async-done | bytes 524320 | tf_op jit(solution)/shard_map/all_to_all | solution.py:602
  88.8 6.7 %shard_map.137 = f32[8,48,128]{2,1,0:T(8,128)S(1)} custom-call(f32[128,8,128]{2,1,0:T(8,128)S(1)} %all-to-all-done.recv, f32[128,8,128]{2,1,0:T(8,128)S(1)} %all-to-all-done.3.factor), custom_call_target="tpu_custom_call" | custom-call | flops 10000000000 | bytes 1245184 | tf_op jit(solution)/shard_map/pallas_call | solution.py:495
  95.5 9.4 %all_to_all.25.moved = f32[8,48,128]{2,1,0:T(8,128)S(1)} all-to-all(f32[8,48,128]{2,1,0:T(8,128)S(1)} %shard_map.137), channel_id=1, replica_groups=mesh['region'=16,'dom'=8] {'dom'}, dimensions={0} | all-to-all | bytes 393216 | tf_op jit(solution)/shard_map/all_to_all | solution.py:626
  104.8 0.0 copy-done.5
  104.8 1.8 %shard_map.138 = f32[12,4096]{1,0:T(8,128)} custom-call(f32[8,48,128]{2,1,0:T(8,128)S(1)} %all_to_all.25.moved, s32[1,4096]{1,0:T(1,128)S(1)} %copy-done.5), custom_call_target="tpu_custom_call" | custom-call | flops 1000000000 | bytes 409600 | tf_op jit(solution)/shard_map/pallas_call | solution.py:495
Async XLA Ops:
  0.6 8.7 %copy-start = (f32[3,16384]{1,0:T(4,128)S(1)}, f32[3,16384]{1,0:T(4,128)}, u32[]{:S(2)}) copy-start(f32[3,16384]{1,0:T(4,128)} %normal.3) | copy-start | bytes 589828
  0.6 8.7 %copy-start.4 = (s32[16384]{0:T(1024)S(1)}, s32[16384]{0:T(1024)}, u32[]{:S(2)}) copy-start(s32[16384]{0:T(1024)} %param.19) | copy-start | bytes 196612
  0.7 8.7 %copy-start.3 = (s32[16384,1]{0,1:T(1,128)S(1)}, s32[16384,1]{0,1:T(1,128)}, u32[]{:S(2)}) copy-start(s32[16384,1]{0,1:T(1,128)} %param.18) | copy-start | bytes 196612
  3.4 12.4 %all-to-all-start.1 = ((f32[8,48,128]{2,1,0:T(8,128)}), f32[8,48,128]{2,1,0:T(8,128)S(1)}, u32[]{:S(2)}, u32[]{:S(2)}) async-start(f32[8,48,128]{2,1,0:T(8,128)} %shard_map.131), calls=%async_computation.1 | async-start | bytes 393216 | tf_op jit(solution)/shard_map/all_to_all | solution.py:537
  15.8 10.4 %copy-start.7 = (s32[1,16384]{1,0:T(1,128)}, s32[1,16384]{1,0:T(1,128)S(1)}, u32[]{:S(2)}) copy-start(s32[1,16384]{1,0:T(1,128)S(1)} %get-tuple-element.18.place) | copy-start | bytes 196612
  15.8 23.8 %all-to-all-start = ((f32[128,8,128]{2,1,0:T(8,128)}), f32[128,8,128]{2,1,0:T(8,128)S(1)}, u32[]{:S(2)}, u32[]{:S(2)}) async-start(f32[128,8,128]{2,1,0:T(8,128)} %get-tuple-element.17), calls=%async_computation | async-start | bytes 1048576 | tf_op jit(solution)/shard_map/all_to_all | solution.py:555
  47.4 18.1 %all-to-all-start.2 = ((f32[128,8,128]{2,1,0:T(8,128)}), f32[128,8,128]{2,1,0:T(8,128)S(1)}, u32[]{:S(2)}, u32[]{:S(2)}) async-start(f32[128,8,128]{2,1,0:T(8,128)} %shard_map.133), calls=%async_computation.2 | async-start | bytes 1048576 | tf_op jit(solution)/shard_map/all_to_all | solution.py:568
  65.5 9.7 %copy-start.1 = (f32[4,16384]{1,0:T(4,128)S(1)}, f32[4,16384]{1,0:T(4,128)}, u32[]{:S(2)}) copy-start(f32[4,16384]{1,0:T(4,128)} %multiplier.3) | copy-start | bytes 786436
  65.5 9.7 %copy-start.2 = (s32[4,16384]{1,0:T(4,128)S(1)}, s32[4,16384]{1,0:T(4,128)}, u32[]{:S(2)}) copy-start(s32[4,16384]{1,0:T(4,128)} %active.3) | copy-start | bytes 786436
  65.5 9.8 %copy-start.6 = (f32[4,16384]{1,0:T(4,128)S(1)}, f32[4,16384]{1,0:T(4,128)}, u32[]{:S(2)}) copy-start(f32[4,16384]{1,0:T(4,128)} %get-tuple-element.25.part) | copy-start | bytes 786436
  65.5 9.8 %copy-start.8 = (s32[1,16384]{1,0:T(1,128)S(1)}, s32[1,16384]{1,0:T(1,128)}, u32[]{:S(2)}) copy-start(s32[1,16384]{1,0:T(1,128)} %copy-done.7) | copy-start | bytes 196612
  70.0 18.7 %all-to-all-start.3 = ((f32[128,8,128]{2,1,0:T(8,128)}), f32[128,8,128]{2,1,0:T(8,128)S(1)}, u32[]{:S(2)}, u32[]{:S(2)}) async-start(f32[128,8,128]{2,1,0:T(8,128)} %get-tuple-element.30), calls=%async_computation.3 | async-start | bytes 1048576 | tf_op jit(solution)/shard_map/all_to_all | solution.py:602
  78.8 26.0 %copy-start.5 = (s32[1,4096]{1,0:T(1,128)S(1)}, s32[1,4096]{1,0:T(1,128)}, u32[]{:S(2)}) copy-start(s32[1,4096]{1,0:T(1,128)} %pick.3) | copy-start | bytes 49156

commit v10 on v9

--- a/solution.py
+++ b/solution.py
@@ -22,7 +22,7 @@
 F32 = jnp.float32
 LANE = 256
 
-UNROLL = 64
+UNROLL = 128
 PARTS = 2
 NN = (((1,), (0,)), ((), ()))
 NT = (((1,), (1,)), ((), ()))

time: 107 us -> 106 us (level)
  no operation moved by 1% of the time
where the time goes in v10:
time: 106 us
  Pallas kernels  48.3 us (46%)
  starting transfers between devices  26.1 us (25%)
  waiting for transfers between devices  21.4 us (20%)
  blocking collectives  9.35 us (9%)
    pallas_call x9, Pallas kernels, call(): pl.pallas_call(kernel, out_shape=[jax.ShapeDtypeStruct(*o) for o in outs]...  48.3 us
    all_to_all x1, starting transfers between devices, on_device(): recv = exchange(request, everyone)  10.3 us
    all_to_all x1, waiting for transfers between devices, on_device(): factor = exchange(terms, everyone)  9.96 us
    all_to_all x1, blocking collectives, on_device(): moved = exchange(forces, 'dom')  9.35 us
    all_to_all x1, waiting for transfers between devices, on_device(): recv = exchange(request, everyone)  6.84 us
    all_to_all x1, starting transfers between devices, on_device(): surf = exchange(picked, 'dom')  5.97 us
    all_to_all x1, starting transfers between devices, on_device(): factor = exchange(terms, everyone)  5.23 us
    all_to_all x1, waiting for transfers between devices, on_device(): returned = exchange(along, everyone)  4.61 us
  transfers between devices with their start and end apart: 4, of which 3 were waited for; matrix products, arithmetic and copies ran while one was open for 0% of the time, Pallas kernels for 24%

profile of v10, /device:TPU:1, one launch (start us, length us, event | category | flops | bytes accessed | tf_op | source)
XLA Modules:
  0.0 106.0 jit_solution(2337152730925198461)
XLA Ops:
  0.6 0.0 copy-start
  0.6 0.0 copy-start.4
  0.7 0.0 copy-start.3
  0.7 2.7 %shard_map.131 = f32[8,48,128]{2,1,0:T(8,128)} custom-call(f32[12,4096]{1,0:T(8,128)} %vol.1, s32[1,4096]{1,0:T(1,128)} %pick.3), custom_call_target="tpu_custom_call" | custom-call | flops 1000000000 | bytes 409600 | tf_op jit(solution)/shard_map/pallas_call | solution.py:495
  3.4 6.0 %all-to-all-start.1 = ((f32[8,48,128]{2,1,0:T(8,128)}), f32[8,48,128]{2,1,0:T(8,128)S(1)}, u32[]{:S(2)}, u32[]{:S(2)}) async-start(f32[8,48,128]{2,1,0:T(8,128)} %shard_map.131), calls=%async_computation.1 | async-start | bytes 393216 | tf_op jit(solution)/shard_map/all_to_all | solution.py:537
  9.3 0.0 copy-done
  9.4 0.0 copy-done.4
  9.4 0.0 copy-done.3
  9.4 6.4 %shard_map.130 = (f32[128,8,128]{2,1,0:T(8,128)}, s32[1,16384]{1,0:T(1,128)S(1)}, s32[8,256]{1,0:T(8,128)S(1)}) custom-call(s32[1,16384]{1,0:T(1,128)S(1)} %bitcast.2, s32[1,16384]{1,0:T(1,128)S(1)} %bitcast.3, f32[3,16384]{1,0:T(4,128)S(1)} %copy-done), custom_call_target="tpu_custom_call" | custom-call | flops 10000000000 | bytes 925696 | tf_op jit(solution)/shard_map/pallas_call | solution.py:495
  15.8 0.0 copy-start.7
  15.8 0.0 all-to-all-done.1.surf
  15.8 10.3 %all-to-all-start = ((f32[128,8,128]{2,1,0:T(8,128)}), f32[128,8,128]{2,1,0:T(8,128)S(1)}, u32[]{:S(2)}, u32[]{:S(2)}) async-start(f32[128,8,128]{2,1,0:T(8,128)} %get-tuple-element.17), calls=%async_computation | async-start | bytes 1048576 | tf_op jit(solution)/shard_map/all_to_all | solution.py:555
  26.2 0.0 copy-done.7
  26.2 6.7 %shard_map.132.proj = f32[2,256,256]{2,1,0:T(8,128)} custom-call(s32[1,16384]{1,0:T(1,128)} %copy-done.7, f32[8,16384]{1,0:T(8,128)} %proj.1), custom_call_target="tpu_custom_call" | custom-call | flops 10000000000 | bytes 1114112 | tf_op jit(solution)/shard_map/pallas_call | solution.py:495
  32.8 6.8 %all-to-all-done.recv = f32[128,8,128]{2,1,0:T(8,128)S(1)} async-done(((f32[128,8,128]{2,1,0:T(8,128)}), f32[128,8,128]{2,1,0:T(8,128)S(1)}, u32[]{:S(2)}, u32[]{:S(2)}) %all-to-all-start) | async-done | bytes 524320 | tf_op jit(solution)/shard_map/all_to_all | solution.py:555
  39.7 7.8 %shard_map.133 = f32[128,8,128]{2,1,0:T(8,128)} custom-call(f32[8,48,128]{2,1,0:T(8,128)S(1)} %all-to-all-done.1.surf, f32[128,8,128]{2,1,0:T(8,128)S(1)} %all-to-all-done.recv), custom_call_target="tpu_custom_call" | custom-call | flops 10000000000 | bytes 1245184 | tf_op jit(solution)/shard_map/pallas_call | solution.py:495
  47.4 4.6 %all-to-all-start.2 = ((f32[128,8,128]{2,1,0:T(8,128)}), f32[128,8,128]{2,1,0:T(8,128)S(1)}, u32[]{:S(2)}, u32[]{:S(2)}) async-start(f32[128,8,128]{2,1,0:T(8,128)} %shard_map.133), calls=%async_computation.2 | async-start | bytes 1048576 | tf_op jit(solution)/shard_map/all_to_all | solution.py:568
  52.0 8.9 %shard_map.134 = (f32[4,16384]{1,0:T(4,128)}, f32[5,256,256]{2,1,0:T(8,128)}) custom-call(s32[1,16384]{1,0:T(1,128)} %copy-done.7, f32[12,16384]{1,0:T(8,128)} %disp.1, f32[3,16384]{1,0:T(4,128)} %normal.3, f32[4,16384]{1,0:T(4,128)} %gap.1, f32[4,16384]{1,0:T(4,128)} %weight.1, f32[4,16384]{1,0:T(4,128)} %multiplier.3, s32[4,16384]{1,0:T(4,128)} %active.3, ...), custom_call_target="tpu_custom_call" | custom-call | flops 10000000000 | bytes 4194304 | tf_op jit(solution)/shard_map/pallas_call | solution.py:495
  60.9 4.6 %all-to-all-done.2.recv = f32[128,8,128]{2,1,0:T(8,128)S(1)} async-done(((f32[128,8,128]{2,1,0:T(8,128)}), f32[128,8,128]{2,1,0:T(8,128)S(1)}, u32[]{:S(2)}, u32[]{:S(2)}) %all-to-all-start.2) | async-done | bytes 524320 | tf_op jit(solution)/shard_map/all_to_all | solution.py:568
  65.5 0.0 copy-start.1
  65.5 0.0 copy-start.2
  65.5 0.0 copy-start.6
  65.5 0.0 copy-start.8
  65.6 3.9 %shard_map.135 = (f32[128,8,128]{2,1,0:T(8,128)}, f32[256,256]{1,0:T(8,128)S(1)}) custom-call(f32[128,8,128]{2,1,0:T(8,128)S(1)} %all-to-all-done.2.recv, s32[8,256]{1,0:T(8,128)S(1)} %get-tuple-element.20.offsets_hbm, f32[5,256,256]{2,1,0:T(8,128)} %get-tuple-element.23.factors_hbm), custom_call_target="tpu_custom_call" | custom-call | flops 1000000000 | bytes 2629632 | tf_op jit(solution)/shard_map/pallas_call | solution.py:495
  69.5 5.2 %all-to-all-start.3 = ((f32[128,8,128]{2,1,0:T(8,128)}), f32[128,8,128]{2,1,0:T(8,128)S(1)}, u32[]{:S(2)}, u32[]{:S(2)}) async-start(f32[128,8,128]{2,1,0:T(8,128)} %get-tuple-element.30), calls=%async_computation.3 | async-start | bytes 1048576 | tf_op jit(solution)/shard_map/all_to_all | solution.py:602
  74.7 0.0 copy-done.1
  74.7 0.0 copy-done.2
  74.7 0.0 copy-done.6
  74.7 0.0 copy-done.8
  74.7 3.5 %shard_map.136 = (f32[4,16384]{1,0:T(4,128)}, f32[4,16384]{1,0:T(4,128)}) custom-call(f32[256,256]{1,0:T(8,128)S(1)} %get-tuple-element.24.mortar, s32[1,16384]{1,0:T(1,128)S(1)} %copy-done.8, f32[4,16384]{1,0:T(4,128)S(1)} %copy-done.6, f32[4,16384]{1,0:T(4,128)S(1)} %copy-done.1, s32[4,16384]{1,0:T(4,128)S(1)} %copy-done.2), custom_call_target="tpu_custom_call" | custom-call | flops 10000000000 | bytes 1638400 | tf_op jit(solution)/shard_map/pallas_call | solution.py:495
  78.2 0.0 copy-start.5
  78.2 10.0 %all-to-all-done.3.factor = f32[128,8,128]{2,1,0:T(8,128)S(1)} async-done(((f32[128,8,128]{2,1,0:T(8,128)}), f32[128,8,128]{2,1,0:T(8,128)S(1)}, u32[]{:S(2)}, u32[]{:S(2)}) %all-to-all-start.3) | async-done | bytes 524320 | tf_op jit(solution)/shard_map/all_to_all | solution.py:602
  88.2 6.7 %shard_map.137 = f32[8,48,128]{2,1,0:T(8,128)S(1)} custom-call(f32[128,8,128]{2,1,0:T(8,128)S(1)} %all-to-all-done.recv, f32[128,8,128]{2,1,0:T(8,128)S(1)} %all-to-all-done.3.factor), custom_call_target="tpu_custom_call" | custom-call | flops 10000000000 | bytes 1245184 | tf_op jit(solution)/shard_map/pallas_call | solution.py:495
  94.9 9.4 %all_to_all.25.moved = f32[8,48,128]{2,1,0:T(8,128)S(1)} all-to-all(f32[8,48,128]{2,1,0:T(8,128)S(1)} %shard_map.137), channel_id=1, replica_groups=mesh['region'=16,'dom'=8] {'dom'}, dimensions={0} | all-to-all | bytes 393216 | tf_op jit(solution)/shard_map/all_to_all | solution.py:626
  104.2 0.0 copy-done.5
  104.2 1.8 %shard_map.138 = f32[12,4096]{1,0:T(8,128)} custom-call(f32[8,48,128]{2,1,0:T(8,128)S(1)} %all_to_all.25.moved, s32[1,4096]{1,0:T(1,128)S(1)} %copy-done.5), custom_call_target="tpu_custom_call" | custom-call | flops 1000000000 | bytes 409600 | tf_op jit(solution)/shard_map/pallas_call | solution.py:495
Async XLA Ops:
  0.6 8.7 %copy-start = (f32[3,16384]{1,0:T(4,128)S(1)}, f32[3,16384]{1,0:T(4,128)}, u32[]{:S(2)}) copy-start(f32[3,16384]{1,0:T(4,128)} %normal.3) | copy-start | bytes 589828
  0.6 8.7 %copy-start.4 = (s32[16384]{0:T(1024)S(1)}, s32[16384]{0:T(1024)}, u32[]{:S(2)}) copy-start(s32[16384]{0:T(1024)} %param.19) | copy-start | bytes 196612
  0.7 8.7 %copy-start.3 = (s32[16384,1]{0,1:T(1,128)S(1)}, s32[16384,1]{0,1:T(1,128)}, u32[]{:S(2)}) copy-start(s32[16384,1]{0,1:T(1,128)} %param.18) | copy-start | bytes 196612
  3.4 12.4 %all-to-all-start.1 = ((f32[8,48,128]{2,1,0:T(8,128)}), f32[8,48,128]{2,1,0:T(8,128)S(1)}, u32[]{:S(2)}, u32[]{:S(2)}) async-start(f32[8,48,128]{2,1,0:T(8,128)} %shard_map.131), calls=%async_computation.1 | async-start | bytes 393216 | tf_op jit(solution)/shard_map/all_to_all | solution.py:537
  15.8 10.4 %copy-start.7 = (s32[1,16384]{1,0:T(1,128)}, s32[1,16384]{1,0:T(1,128)S(1)}, u32[]{:S(2)}) copy-start(s32[1,16384]{1,0:T(1,128)S(1)} %get-tuple-element.18.place) | copy-start | bytes 196612
  15.8 23.8 %all-to-all-start = ((f32[128,8,128]{2,1,0:T(8,128)}), f32[128,8,128]{2,1,0:T(8,128)S(1)}, u32[]{:S(2)}, u32[]{:S(2)}) async-start(f32[128,8,128]{2,1,0:T(8,128)} %get-tuple-element.17), calls=%async_computation | async-start | bytes 1048576 | tf_op jit(solution)/shard_map/all_to_all | solution.py:555
  47.4 18.1 %all-to-all-start.2 = ((f32[128,8,128]{2,1,0:T(8,128)}), f32[128,8,128]{2,1,0:T(8,128)S(1)}, u32[]{:S(2)}, u32[]{:S(2)}) async-start(f32[128,8,128]{2,1,0:T(8,128)} %shard_map.133), calls=%async_computation.2 | async-start | bytes 1048576 | tf_op jit(solution)/shard_map/all_to_all | solution.py:568
  65.5 9.2 %copy-start.1 = (f32[4,16384]{1,0:T(4,128)S(1)}, f32[4,16384]{1,0:T(4,128)}, u32[]{:S(2)}) copy-start(f32[4,16384]{1,0:T(4,128)} %multiplier.3) | copy-start | bytes 786436
  65.5 9.2 %copy-start.2 = (s32[4,16384]{1,0:T(4,128)S(1)}, s32[4,16384]{1,0:T(4,128)}, u32[]{:S(2)}) copy-start(s32[4,16384]{1,0:T(4,128)} %active.3) | copy-start | bytes 786436
  65.5 9.2 %copy-start.6 = (f32[4,16384]{1,0:T(4,128)S(1)}, f32[4,16384]{1,0:T(4,128)}, u32[]{:S(2)}) copy-start(f32[4,16384]{1,0:T(4,128)} %get-tuple-element.25.part) | copy-start | bytes 786436
  65.5 9.2 %copy-start.8 = (s32[1,16384]{1,0:T(1,128)S(1)}, s32[1,16384]{1,0:T(1,128)}, u32[]{:S(2)}) copy-start(s32[1,16384]{1,0:T(1,128)} %copy-done.7) | copy-start | bytes 196612
  69.5 18.7 %all-to-all-start.3 = ((f32[128,8,128]{2,1,0:T(8,128)}), f32[128,8,128]{2,1,0:T(8,128)S(1)}, u32[]{:S(2)}, u32[]{:S(2)}) async-start(f32[128,8,128]{2,1,0:T(8,128)} %get-tuple-element.30), calls=%async_computation.3 | async-start | bytes 1048576 | tf_op jit(solution)/shard_map/all_to_all | solution.py:602
  78.2 26.0 %copy-start.5 = (s32[1,4096]{1,0:T(1,128)S(1)}, s32[1,4096]{1,0:T(1,128)}, u32[]{:S(2)}) copy-start(s32[1,4096]{1,0:T(1,128)} %pick.3) | copy-start | bytes 49156
